TPU v7x, 256 devices: a whole 4x4x8 slice. The times are simulated.
256 devices in a mesh: los: 8 (over z_hi, x), sky: 32 (over z_lo, y, core).
Axes of the slice: x: 4, y: 4, z: 8 (z_hi: 2, z_lo: 4; z = z_hi * 4 + z_lo), core: 2. Of those that a mesh axis runs over, the one named last changes fastest.
Arguments:
- density: bfloat16 [64, 2048, 2048], P('los', 'sky'), may hold values from 0.1 to 10
- refine: int32 [8, 256, 256], P('los', 'sky'), may hold values from 0 to 1, as said below
- weight_low: float32 [64], P('los'), may hold values from 0.1 to 0.5
- weight_high: float32 [64], P('los'), may hold values from 0.6 to 3
Outputs:
- deflection_x: float32 [2048, 2048], P('sky', 'los')
- deflection_y: float32 [2048, 2048], P('sky', 'los')
Inputs may be any that keep to these rules, and one draw needn't show every extreme that they name: `refine`: the blocks of one slab and one sky column (one index of los and of sky) hold at most 512 refined blocks, and in every draw some slab and column holds exactly 512.
All inputs are finite; a program needn't handle non-finite values.
Results may differ from a plain program's by a relative error of at most 0.0003.
Values may be sent and summed in bfloat16 or wider, within the bound.
No kernel may reach another device: no remote copies, remote signals or barrier semaphores. Data moves between devices by JAX's collectives and lax.ppermute only.
A program may use at most 64 MiB of HBM per device.

v0:
```python
import functools

import jax
import jax.numpy as jnp
import ml_dtypes
import numpy as np
from jax import lax
from jax.experimental import pallas as pl
from jax.experimental.pallas import tpu as pltpu
from jax.sharding import Mesh, PartitionSpec as P

f32 = jnp.float32
bf16 = jnp.bfloat16
N = 2048
ROWS = 64
SKY = 32
LAYERS = 8
LOS = ("zhi", "x")
MB = 1024 * 1024


def halves(table):
    high = table.astype(np.float32).astype(ml_dtypes.bfloat16)
    low = (table - high.astype(np.float64)).astype(np.float32).astype(ml_dtypes.bfloat16)
    return high, low


def tile_modes(tile):
    n = np.arange(128)
    if tile:
        return tile + 16 * n
    return np.where(n < 64, 16 * n, 8 + 16 * (n - 64))


def tile_order(real, imag):
    pair = np.stack([real.reshape(SKY, 4, -1), imag.reshape(SKY, 4, -1)], axis=1)
    return pair.reshape(256, -1)


def forward_table():
    b = np.arange(128)
    tiles = []
    for tile in range(8):
        angle = (tile_modes(tile)[:, None] * b[None, :] % N) * (2 * np.pi / N)
        cosine, sine = np.cos(angle), np.sin(angle)
        if tile:
            real = np.concatenate([cosine, sine], 1)
            imag = np.concatenate([-sine, cosine], 1)
        else:
            zero = np.zeros((64, 128))
            real = np.block([[cosine[:64], zero], [zero, cosine[64:]]])
            imag = np.block([[-sine[:64], zero], [zero, -sine[64:]]])
            imag[0, :128] = (-1.0) ** b
        tiles.append(tile_order(real, imag).T)
    return np.stack(tiles)


def inverse_table():
    j = np.arange(256)
    tiles = []
    for tile in range(8):
        angle = (tile_modes(tile)[:, None] * j[None, :] % N) * (2 * np.pi / N)
        real, imag = 2 * np.cos(angle), -2 * np.sin(angle)
        if not tile:
            real[0] = 1.0
            imag[0] = (-1.0) ** j
        tiles.append(tile_order(real, imag))
    return np.stack(tiles).reshape(4, 512, 256)


def row_table():
    r = np.arange(64)
    angle = (r[:, None] * r[None, :] % 64) * (2 * np.pi / 64)
    both = np.eye(2)
    return np.concatenate([np.kron(both, np.cos(angle)), np.kron(both, np.sin(angle))], 1)


def twists():
    angle = (np.arange(32)[:, None] * (np.arange(128) % 64)[None, :]) * (2 * np.pi / N)
    sign = np.where(np.arange(8) < 4, 1.0, -1.0)
    cosine = np.broadcast_to(np.cos(angle)[:, None, :], (32, 8, 128))
    sine = np.sin(angle)[:, None, :] * sign[None, :, None]
    return cosine.astype(np.float32), sine.astype(np.float32)


def minmod(a, b):
    return jnp.maximum(jnp.minimum(a, b), 0.0) + jnp.minimum(jnp.maximum(a, b), 0.0)


def split(value):
    high = value.astype(bf16)
    return high, (value - high.astype(f32)).astype(bf16)


def dot3(value, high_table, low_table):
    high, low = split(value)
    dot = functools.partial(jnp.dot, preferred_element_type=f32)
    return dot(high, high_table) + (dot(low, high_table) + dot(high, low_table))


def limit(mib):
    return pltpu.CompilerParams(vmem_limit_bytes=mib * MB)


VM = pl.BlockSpec(memory_space=pltpu.VMEM)
SM = pl.BlockSpec(memory_space=pltpu.SMEM)


def rows_kernel(first_ref, last_ref, low_ref, high_ref):
    for z in range(LAYERS):
        low_ref[z : z + 1, :] = first_ref[z].astype(f32)[0:1]
        high_ref[z : z + 1, :] = last_ref[z].astype(f32)[15:16]


def edge_rows(density):
    shape = jax.ShapeDtypeStruct((LAYERS, N), f32)
    return pl.pallas_call(
        rows_kernel,
        grid=(1,),
        out_shape=(shape, shape),
        in_specs=[
            pl.BlockSpec((LAYERS, 16, N), lambda i: (0, 0, 0)),
            pl.BlockSpec((LAYERS, 16, N), lambda i: (0, 3, 0)),
        ],
        out_specs=(
            pl.BlockSpec((LAYERS, N), lambda i: (0, 0)),
            pl.BlockSpec((LAYERS, N), lambda i: (0, 0)),
        ),
        compiler_params=limit(24),
        name="edge_rows",
    )(density, density)


CHUNK = 512


def inner_kernel(
    low_ref, high_ref, d_ref, refine_ref, calm_ref, lifted_ref, tx_ref, ty_ref, mask_ref, near_ref
):
    block = lax.broadcasted_iota(jnp.int32, (256, N), 0)
    lane = lax.broadcasted_iota(jnp.int32, (256, N), 1)
    grow = jnp.where(lane // 8 == block, 1.0, 0.0).astype(bf16)
    coarse = refine_ref[0].astype(f32).astype(bf16)
    mask_ref[...] = jnp.dot(coarse, grow, preferred_element_type=f32)
    for z in range(LAYERS):
        first = d_ref[z, 0:16, :].astype(f32)
        last = d_ref[z, 48:64, :].astype(f32)
        near_ref[0, z : z + 1, :] = first[0:1]
        near_ref[1, z : z + 1, :] = first[1:2]
        near_ref[2, z : z + 1, :] = last[14:15]
        near_ref[3, z : z + 1, :] = last[15:16]

    wide = CHUNK + 256
    row = lax.broadcasted_iota(jnp.int32, (ROWS, CHUNK), 0)
    inside = jnp.logical_and(row > 0, row < ROWS - 1)

    def chunk(i, carry):
        start = pl.multiple_of(i * CHUNK, CHUNK)
        left = pl.multiple_of((start + N - 128) % N, 128)
        right = pl.multiple_of((start + CHUNK) % N, 128)
        base = jnp.zeros((ROWS, CHUNK), f32)
        tz, tx, ty = base, base, base
        centre, step = None, None
        for z in range(LAYERS):
            average = 0.5 * (low_ref[z] + high_ref[z])
            former = centre
            around = jnp.concatenate(
                [
                    d_ref[z, :, pl.ds(left, 128)],
                    d_ref[z, :, pl.ds(start, CHUNK)],
                    d_ref[z, :, pl.ds(right, 128)],
                ],
                axis=1,
            ).astype(f32)
            centre = around[:, 128 : 128 + CHUNK]
            base = base + average * centre
            dy = pltpu.roll(around, wide - 1, 1) - around
            gy = minmod(dy, pltpu.roll(dy, 1, 1))[:, 128 : 128 + CHUNK]
            ty = ty + average * gy
            dx = pltpu.roll(centre, ROWS - 1, 0) - centre
            tx = tx + average * minmod(dx, pltpu.roll(dx, 1, 0))
            if z > 0:
                latter = centre - former
                if step is not None:
                    slope = 0.125 * (high_ref[z - 1] - low_ref[z - 1])
                    tz = tz + slope * minmod(latter, step)
                step = latter
        marked = mask_ref[:, pl.ds(start, CHUNK)]
        marked = jnp.broadcast_to(marked[:, None, :], (8, 8, CHUNK)).reshape(ROWS, CHUNK)
        at = pl.ds(start, CHUNK)
        calm_ref[:, at] = base - marked * base
        lifted_ref[:, at] = marked * (base + tz)
        tx_ref[:, at] = jnp.where(inside, marked * tx, 0.0)
        ty_ref[:, at] = marked * ty
        return carry

    lax.fori_loop(0, N // CHUNK, chunk, 0)


def inner_sums(low, high, density, refine):
    field = jax.ShapeDtypeStruct((ROWS, N), f32)
    return pl.pallas_call(
        inner_kernel,
        out_shape=(
            field,
            field,
            field,
            field,
            jax.ShapeDtypeStruct((8, N), f32),
            jax.ShapeDtypeStruct((4, LAYERS, N), f32),
        ),
        in_specs=[SM, SM, VM, VM],
        out_specs=(VM,) * 6,
        compiler_params=limit(40),
        cost_estimate=pl.CostEstimate(flops=40_000_000, bytes_accessed=24 * MB, transcendentals=0),
        name="inner_sums",
    )(low, high, density, refine)


def outer_kernel(
    low_ref,
    high_ref,
    pos_ref,
    average_ref,
    bottom_ref,
    top_ref,
    below_ref,
    above_ref,
    before_ref,
    after_ref,
    calm_ref,
    lifted_ref,
    tx_ref,
    ty_ref,
    mask_ref,
    near_ref,
    high_table,
    low_table,
    out_ref,
):
    los = pos_ref[0] * 4 + pos_ref[1]
    v0, v1 = bottom_ref[0].astype(f32), bottom_ref[1].astype(f32)
    v6, v7 = top_ref[0].astype(f32), top_ref[1].astype(f32)
    below = jnp.where(los == 0, v0, below_ref[0].astype(f32))
    above = jnp.where(los == 7, v7, above_ref[0].astype(f32))
    slope0 = 0.125 * (high_ref[0] - low_ref[0])
    slope7 = 0.125 * (high_ref[7] - low_ref[7])
    tz = slope0 * minmod(v1 - v0, v0 - below) + slope7 * minmod(above - v7, v7 - v6)
    mask = mask_ref[...]
    marked = jnp.broadcast_to(mask[:, None, :], (8, 8, N)).reshape(ROWS, N)
    lifted = lifted_ref[...] + marked * tz
    average = average_ref[:, 0:1]
    r0, r1, r62, r63 = near_ref[0], near_ref[1], near_ref[2], near_ref[3]
    e0 = jnp.sum(average * minmod(r1 - r0, r0 - before_ref[...]), axis=0, keepdims=True)
    e63 = jnp.sum(average * minmod(after_ref[...] - r63, r63 - r62), axis=0, keepdims=True)
    row = lax.broadcasted_iota(jnp.int32, (ROWS, N), 0)
    tx = jnp.where(row == 0, mask[0:1] * e0, jnp.where(row == ROWS - 1, mask[7:8] * e63, tx_ref[...]))
    eighth, tilt = 0.125 * lifted, ty_ref[...] * (1.0 / 32.0)
    smooth = 0.75 * lifted + pltpu.roll(eighth + tilt, 1, 1) + pltpu.roll(eighth - tilt, N - 1, 1)
    sloped = 0.75 * tx + 0.125 * (pltpu.roll(tx, 1, 1) + pltpu.roll(tx, N - 1, 1))
    eighth, tilt = 0.125 * smooth, sloped * (1.0 / 32.0)
    none = jnp.zeros((8, N), f32)

    def longer(field):
        return jnp.concatenate([field, none], axis=0)

    kappa = (
        longer(calm_ref[...] + 0.75 * smooth)
        + pltpu.roll(longer(eighth + tilt), 1, 0)
        + pltpu.roll(longer(eighth - tilt), ROWS + 7, 0)
    )
    part = [kappa[:, 128 * a : 128 * a + 128] for a in range(16)]
    even = [part[a] + part[16 - a] for a in range(1, 8)]
    odd = [part[a] - part[16 - a] for a in range(1, 8)]

    def weigh(pairs):
        total = None
        for factor, value in pairs:
            if abs(factor) < 1e-9:
                continue
            term = value if abs(factor - 1) < 1e-9 else factor * value
            total = term if total is None else total + term
        return total

    def cosines(k):
        first = part[0] + part[8] if k % 2 == 0 else part[0] - part[8]
        return first + weigh((float(np.cos(np.pi * k * a / 8)), even[a - 1]) for a in range(1, 8))

    def sines(k):
        return weigh((float(-np.sin(np.pi * k * a / 8)), odd[a - 1]) for a in range(1, 8))

    for tile in range(8):
        second = sines(tile) if tile else cosines(8)
        value = jnp.concatenate([cosines(tile), second], axis=1)
        lanes = 256 * (tile % 2)
        out_ref[tile // 2, :, lanes : lanes + 256] = dot3(value, high_table[tile], low_table[tile])


def outer_sums(low, high, pos, average, density, below, above, before, after, inner, tables):
    whole = lambda *shape: pl.BlockSpec(shape, lambda i: (0,) * len(shape))
    return pl.pallas_call(
        outer_kernel,
        grid=(1,),
        out_shape=jax.ShapeDtypeStruct((4, 72, 512), f32),
        in_specs=[
            SM,
            SM,
            SM,
            whole(LAYERS, 128),
            pl.BlockSpec((2, ROWS, N), lambda i: (0, 0, 0)),
            pl.BlockSpec((2, ROWS, N), lambda i: (3, 0, 0)),
            whole(1, ROWS, N),
            whole(1, ROWS, N),
            whole(LAYERS, N),
            whole(LAYERS, N),
            whole(ROWS, N),
            whole(ROWS, N),
            whole(ROWS, N),
            whole(ROWS, N),
            whole(8, N),
            whole(4, LAYERS, N),
            whole(8, 256, 256),
            whole(8, 256, 256),
        ],
        out_specs=whole(4, 72, 512),
        compiler_params=limit(56),
        name="outer_sums",
    )(low, high, pos, average, density, density, below, above, before, after, *inner, *tables)


def turn_kernel(in_ref, out_ref):
    total = (in_ref[0] + in_ref[1]) + (in_ref[2] + in_ref[3])
    total = jnp.concatenate([total, jnp.zeros((56, 512), f32)], axis=0)
    out_ref[...] = total.T.reshape(64, 8, 128)


def turn(pieces):
    return pl.pallas_call(
        turn_kernel,
        out_shape=jax.ShapeDtypeStruct((64, 8, 128), f32),
        in_specs=[VM],
        out_specs=VM,
        compiler_params=limit(24),
        name="turn",
    )(pieces)


def dft_32(values):
    even = [values[s] + values[32 - s] for s in range(1, 16)]
    odd = [values[s] - values[32 - s] for s in range(1, 16)]
    ends = [values[0] + values[16], values[0] - values[16]]
    cosine, sine = [None] * 17, [None] * 17
    for k in range(9):
        plain = ends[k % 2]
        turned = None
        for s in range(1, 16):
            term = float(np.cos(np.pi * k * s / 16)) * even[s - 1]
            if s % 2 == 0:
                plain = plain + term
            else:
                turned = term if turned is None else turned + term
        cosine[k] = plain + turned
        cosine[16 - k] = plain - turned
    for k in range(1, 9):
        plain, turned = None, None
        for s in range(1, 16):
            term = float(np.sin(np.pi * k * s / 16)) * odd[s - 1]
            if s % 2 == 0:
                plain = term if plain is None else plain + term
            else:
                turned = term if turned is None else turned + term
        sine[k] = turned + plain
        sine[16 - k] = turned - plain
    return cosine, sine


def solve_kernel(pos_ref, in_ref, cos_ref, sin_ref, high_table, low_table, out_ref):
    zhi, column, sky = pos_ref[0], pos_ref[1], pos_ref[2]
    tile = 2 * column + zhi
    lane = lax.broadcasted_iota(jnp.int32, (8, 128), 1)
    sub = lax.broadcasted_iota(jnp.int32, (8, 128), 0)
    lower = lane < 64
    sign = jnp.where(sub < 4, 1.0, -1.0)
    first = jnp.logical_and(tile == 0, sky == 0)
    packed = jnp.logical_and(sub % 4 == 0, first)

    def swap(v):
        return pltpu.roll(v, 4, v.ndim - 2)

    def bent(v):
        return swap(v) * sign

    total = [in_ref[s] + in_ref[SKY + s] for s in range(SKY)]
    values = []
    for s in range(SKY):
        up = pltpu.roll(total[(s - 1) % SKY], 64, 1)
        down = pltpu.roll(total[(s + 1) % SKY], 120, 1)
        v = total[s] + jnp.where(lane == 0, up, jnp.where(lane == 63, down, 0.0))
        v = jnp.where(lower, v, pltpu.roll(v, 64, 1))
        apart = jnp.where(sub == 4, 0.0, jnp.where(lower, v, swap(v)))
        values.append(jnp.where(packed, apart, v))
    cosine, sine = dft_32(values)
    spectrum = [None] * 32
    spectrum[0], spectrum[16] = cosine[0], cosine[16]
    for k in range(1, 16):
        turned = bent(sine[k])
        spectrum[k], spectrum[32 - k] = cosine[k] + turned, cosine[k] - turned
    twisted = [spectrum[k] * cos_ref[k] + swap(spectrum[k]) * sin_ref[k] for k in range(32)]
    rows = jnp.concatenate(twisted, axis=0)
    pair = dot3(rows, high_table[...], low_table[...])
    pair_c = pair[:, :128].reshape(32, 8, 128)
    pair_s = pair[:, 128:].reshape(32, 8, 128)

    k1 = lax.broadcasted_iota(jnp.int32, (32, 8, 128), 0)
    k2 = lax.broadcasted_iota(jnp.int32, (32, 8, 128), 2) % 64
    nx = k1 + 32 * k2
    nx = jnp.where(nx < N // 2, nx, nx - N)
    n = 4 * sky + sub % 4
    ny = jnp.where(tile > 0, tile + 16 * n, jnp.where(n < 64, 16 * n, 8 + 16 * (n - 64)))
    ny = jnp.where(ny < N // 2, ny, ny - N)
    ny = jnp.where(jnp.logical_and(packed, jnp.logical_not(lower)), -(N // 2), ny)
    along_x = jnp.logical_or(packed, lower)[None]
    squared = nx * nx + (ny * ny)[None]
    wave = jnp.where(along_x, jnp.where(nx == -(N // 2), 0, nx), ny[None])
    unit = 2.0 * np.pi / N
    scale = float(-2.0 / unit / 64.0 / N / N)
    factor = scale * wave.astype(f32) / jnp.maximum(squared, 1).astype(f32)
    kappa_hat = pair_c + swap(pair_s) * sign[None]
    field = factor * (swap(kappa_hat) * (-sign)[None])
    pair = dot3(field.reshape(256, 128), high_table[...], low_table[...])
    values = []
    for k in range(32):
        v = pair[8 * k : 8 * k + 8, :128] - bent(pair[8 * k : 8 * k + 8, 128:])
        values.append(v * cos_ref[k] - swap(v) * sin_ref[k])
    cosine, sine = dft_32(values)
    for s in range(17):
        turned = bent(sine[s]) if 0 < s < 16 else None
        for at in (s,) if turned is None else (s, 32 - s):
            v = cosine[s]
            if turned is not None:
                v = v - turned if at == s else v + turned
            other = swap(pltpu.roll(v, 64, 1))
            joined = jnp.where(lower, jnp.where(sub == 4, other, v), 0.0)
            v = jnp.where(packed, joined, v)
            out_ref[at] = v
            out_ref[SKY + at] = v


def solve(pos, pieces, tables):
    return pl.pallas_call(
        solve_kernel,
        out_shape=jax.ShapeDtypeStruct((64, 8, 128), f32),
        in_specs=[SM] + [VM] * 5,
        out_specs=VM,
        compiler_params=limit(24),
        name="solve",
    )(pos, pieces, *tables)


def back_kernel(pos_ref, phase_ref, in_ref, high_table, low_table, out_ref):
    value = in_ref[...]
    sub = lax.broadcasted_iota(jnp.int32, (64, 8, 128), 1)
    bent = pltpu.roll(value, 4, 1) * jnp.where(sub < 4, -1.0, 1.0)
    plain = value.reshape(512, 128).T
    bent = bent.reshape(512, 128).T
    for target in range(4):
        parts = []
        for half in range(2):
            lanes = slice(256 * half, 256 * half + 256)
            at = 4 * target + 2 * half
            parts.append(phase_ref[at] * plain[:, lanes] + phase_ref[at + 1] * bent[:, lanes])
        out_ref[target] = dot3(jnp.concatenate(parts, axis=1), high_table[0], low_table[0])


def back(pos, phase, pieces, tables):
    table = pl.BlockSpec((1, 512, 256), lambda i, pos, phase: (pos[1], 0, 0))
    return pl.pallas_call(
        back_kernel,
        grid_spec=pltpu.PrefetchScalarGridSpec(
            num_scalar_prefetch=2,
            grid=(1,),
            in_specs=[pl.BlockSpec((64, 8, 128), lambda i, pos, phase: (0, 0, 0)), table, table],
            out_specs=pl.BlockSpec((4, 128, 256), lambda i, pos, phase: (0, 0, 0)),
        ),
        out_shape=jax.ShapeDtypeStruct((4, 128, 256), f32),
        compiler_params=limit(24),
        name="back",
    )(pos, phase, pieces, *tables)


def final_kernel(in_ref, x_ref, y_ref):
    total = (in_ref[0] + in_ref[1]) + (in_ref[2] + in_ref[3])
    x_ref[...] = total[:ROWS]
    y_ref[...] = total[ROWS:]


def final(pieces):
    shape = jax.ShapeDtypeStruct((ROWS, 256), f32)
    return pl.pallas_call(
        final_kernel,
        out_shape=(shape, shape),
        in_specs=[VM],
        out_specs=(VM, VM),
        compiler_params=limit(24),
        name="final",
    )(pieces)


def body(density, refine, weight_low, weight_high):
    zhi, column, sky = lax.axis_index("zhi"), lax.axis_index("x"), lax.axis_index("sky")
    pos = jnp.stack([zhi, column, sky]).astype(jnp.int32)
    above = lax.ppermute(density[:1], LOS, [(i + 1, i) for i in range(7)])
    below = lax.ppermute(density[-1:], LOS, [(i, i + 1) for i in range(7)])
    row_first, row_last = edge_rows(density)
    before = lax.ppermute(row_last, "sky", [(i, (i + 1) % SKY) for i in range(SKY)])
    after = lax.ppermute(row_first, "sky", [((i + 1) % SKY, i) for i in range(SKY)])
    inner = inner_sums(weight_low, weight_high, density, refine)
    average = jnp.broadcast_to((0.5 * (weight_low + weight_high))[:, None], (LAYERS, 128))
    summed = outer_sums(
        weight_low,
        weight_high,
        pos,
        average,
        density,
        below,
        above,
        before,
        after,
        inner,
        halves(forward_table()),
    )
    summed = lax.all_to_all(summed, "x", 0, 0, tiled=True)
    pieces = lax.all_to_all(turn(summed), ("zhi", "sky"), 0, 0, tiled=True)
    cosine, sine = twists()
    high, low = halves(row_table())
    pieces = solve(pos, pieces, (cosine, sine, high, low))
    pieces = lax.all_to_all(pieces, ("zhi", "sky"), 0, 0, tiled=True)
    eighths = (2 * column + jnp.arange(2))[None, :] * (4 * zhi + jnp.arange(4))[:, None] % 8
    angle = eighths.astype(f32) * (2 * np.pi / 8)
    phase = jnp.stack([jnp.cos(angle), jnp.sin(angle)], axis=-1).reshape(16)
    fields = back(pos, phase, pieces, halves(inverse_table()))
    fields = lax.all_to_all(fields, "x", 0, 0, tiled=True)
    return final(fields)


def solution(mesh):
    devices = mesh.devices.reshape(2, 4, SKY)
    inner = Mesh(devices, ("zhi", "x", "sky"))
    placed = (P(LOS, "sky", None), P(LOS, "sky", None), P(LOS), P(LOS))
    return jax.shard_map(
        body,
        mesh=inner,
        in_specs=placed,
        out_specs=(P("sky", LOS), P("sky", LOS)),
        check_vma=False,
    )
```

profile of v0, /device:TPU:1, one launch (start us, length us, event | category | flops | bytes accessed | tf_op | source)
XLA Modules:
  0.0 109.7 jit_solution(4358544222403537907)
XLA Ops:
  0.6 1.6 %copy-done = bf16[8,64,2048]{2,1,0:T(8,128)(2,1)S(1)} copy-done((bf16[8,64,2048]{2,1,0:T(8,128)(2,1)S(1)}, bf16[8,64,2048]{2,1,0:T(8,128)(2,1)}, u32[]{:S(2)}) %copy-start) | copy-done | bytes 2097176
  2.2 0.1 edge_rows.1
  2.3 2.8 %collective-permute-start.2 = (f32[8,2048]{1,0:T(8,128)S(1)}, f32[8,2048]{1,0:T(8,128)S(1)}, u32[]{:S(2)}, u32[]{:S(2)}) collective-permute-start(f32[8,2048]{1,0:T(8,128)S(1)} %get-tuple-element.10), channel_id=1, source_target_pairs={{0,1},{1,2},{2,3},{3,4},{4,5},{5,6},{6,7},{7,8},{8,9},{9,10},{10,1... | collective-permute-start | bytes 196616 | tf_op jit(solution)/shard_map/ppermute | solution.py:515
  5.1 0.6 collective-permute-start.3
  5.8 1.3 %collective-permute-start.1 = (bf16[1,64,2048]{2,1,0:T(8,128)(2,1)S(1)}, bf16[1,64,2048]{2,1,0:T(8,128)(2,1)S(1)}, u32[]{:S(2)}, u32[]{:S(2)}) collective-permute-start(bf16[1,64,2048]{2,1,0:T(8,128)(2,1)S(1)} %get-tuple-element.18), channel_id=1, source_target_pairs={{32,0},{64,32},{96,64},{128,96},{160,128},{192,160},{224,192},{33,... | collective-permute-start | bytes 786440 | tf_op jit(solution)/shard_map/ppermute | solution.py:512
  7.1 4.0 %collective-permute-start = (bf16[1,64,2048]{2,1,0:T(8,128)(2,1)S(1)}, bf16[1,64,2048]{2,1,0:T(8,128)(2,1)S(1)}, u32[]{:S(2)}, u32[]{:S(2)}) collective-permute-start(bf16[1,64,2048]{2,1,0:T(8,128)(2,1)S(1)} %get-tuple-element.19), channel_id=1, source_target_pairs={{0,32},{32,64},{64,96},{96,128},{128,160},{160,192},{192,224},{1,3... | collective-permute-start | bytes 786440 | tf_op jit(solution)/shard_map/ppermute | solution.py:513
  11.2 7.4 %inner_sums.1 = (f32[64,2048]{1,0:T(8,128)S(1)}, f32[64,2048]{1,0:T(8,128)S(1)}, f32[64,2048]{1,0:T(8,128)S(1)}, f32[64,2048]{1,0:T(8,128)S(1)}, f32[8,2048]{1,0:T(8,128)S(1)}, /*index=5*/f32[4,8,2048]{2,1,0:T(8,128)S(1)}) custom-call(f32[8]{0:T(128)S(1)} %copy-done.16, f32[8]{0:T(128)S(1)} %copy-done.17, bf16[8,64,2048]{2,1,0:T(8,128)(2,1)S(1)} %copy-done.1, ...), custom_call_target="tpu_custom_call" | custom-call | flops 40000000 | bytes 25165824 | tf_op jit(solution)/shard_map/inner_sums/pallas_call | solution.py:202
  18.6 0.8 copy-done.4
  19.4 0.8 copy-done.5
  20.2 0.8 copy-done.6
  20.9 0.8 copy-done.7
  21.7 0.7 copy-done.8
  22.4 0.6 copy-done.11
  23.1 0.7 pad_add_fusion.pos_ref
  23.8 0.7 broadcast_in_dim.2.average_ref
  24.6 5.5 %outer_sums.1 = f32[4,72,512]{2,1,0:T(8,128)} custom-call(f32[8]{0:T(128)} %low_ref.3, f32[8]{0:T(128)} %high_ref.3, s32[3]{0:T(128)} %pad_add_fusion.pos_ref, f32[8,128]{1,0:T(8,128)} %broadcast_in_dim.2.average_ref, bf16[8,64,2048]{2,1,0:T(8,128)(2,1)} %top_ref.1, bf16[8,64,2048]{2,1,0:T(8,128)(2,1)} %top_ref.1, bf16[1,64,2048]{2,1,0:T(8,128)(2,1)} %copy-done.19, ...), custom_call_target="tpu_custom_call" | custom-call | tf_op jit(solution)/shard_map/outer_sums/pallas_call | solution.py:301
  30.0 0.0 copy-start.12
  30.1 0.0 copy-start.13
  30.1 0.0 copy-start.2
  30.1 16.5 %all_to_all.20.in_ref = f32[4,72,512]{2,1,0:T(8,128)S(1)} all-to-all(f32[4,72,512]{2,1,0:T(8,128)} %outer_sums.1), channel_id=1, replica_groups=mesh['zhi'=2,'x'=4,'sky'=32] {'x'}, dimensions={0} | all-to-all | bytes 1179648 | tf_op jit(solution)/shard_map/all_to_all | solution.py:532
  46.6 0.8 turn.1
  47.5 15.3 %all-to-all-start.1 = ((f32[64,8,128]{2,1,0:T(8,128)}), f32[64,8,128]{2,1,0:T(8,128)S(1)}, u32[]{:S(2)}, u32[]{:S(2)}) async-start(f32[64,8,128]{2,1,0:T(8,128)} %turn.1), calls=%async_computation.1 | async-start | bytes 524288 | tf_op jit(solution)/shard_map/all_to_all | solution.py:533
  62.8 13.2 %all-to-all-done.1.in_ref = f32[64,8,128]{2,1,0:T(8,128)S(1)} async-done(((f32[64,8,128]{2,1,0:T(8,128)}), f32[64,8,128]{2,1,0:T(8,128)S(1)}, u32[]{:S(2)}, u32[]{:S(2)}) %all-to-all-start.1) | async-done | bytes 262176 | tf_op jit(solution)/shard_map/all_to_all | solution.py:533
  75.9 2.2 %solve.1 = f32[64,8,128]{2,1,0:T(8,128)} custom-call(s32[3]{0:T(128)S(1)} %copy-done.15, f32[64,8,128]{2,1,0:T(8,128)S(1)} %all-to-all-done.1.in_ref, f32[32,8,128]{2,1,0:T(8,128)S(1)} %copy-done.10, f32[32,8,128]{2,1,0:T(8,128)S(1)} %copy-done.9, bf16[128,256]{1,0:T(8,128)(2,1)S(1)} %copy-done.13, bf16[128,256]{1,0:T(8,128)(2,1)S(1)} %copy-done.12), custom_call_target="tpu_custom_call" | custom-call | tf_op jit(solution)/shard_map/solve/pallas_call | solution.py:450
  78.2 4.7 %all-to-all-start.2 = ((f32[64,8,128]{2,1,0:T(8,128)}), f32[64,8,128]{2,1,0:T(8,128)S(1)}, u32[]{:S(2)}, u32[]{:S(2)}) async-start(f32[64,8,128]{2,1,0:T(8,128)} %solve.1), calls=%async_computation.2 | async-start | bytes 524288 | tf_op jit(solution)/shard_map/all_to_all | solution.py:537
  82.9 0.1 fusion.4
  83.0 0.1 copy.14
  83.1 0.1 reshape.144.phase_ref
  83.2 12.8 %all-to-all-done.2.in_ref = f32[64,8,128]{2,1,0:T(8,128)S(1)} async-done(((f32[64,8,128]{2,1,0:T(8,128)}), f32[64,8,128]{2,1,0:T(8,128)S(1)}, u32[]{:S(2)}, u32[]{:S(2)}) %all-to-all-start.2) | async-done | bytes 262176 | tf_op jit(solution)/shard_map/all_to_all | solution.py:537
  96.0 1.3 %back.1 = f32[4,128,256]{2,1,0:T(8,128)S(1)} custom-call(s32[3]{0:T(128)S(1)} %copy-done.15, f32[16]{0:T(128)S(1)} %reshape.144.phase_ref, f32[64,8,128]{2,1,0:T(8,128)S(1)} %all-to-all-done.2.in_ref, bf16[4,512,256]{2,1,0:T(8,128)(2,1)S(1)} %copy-done.3, bf16[4,512,256]{2,1,0:T(8,128)(2,1)S(1)} %copy-done.2), custom_call_target="tpu_custom_call" | custom-call | tf_op jit(solution)/shard_map/back/pallas_call | solution.py:477
  97.3 11.7 %all_to_all.21.in_ref = f32[4,128,256]{2,1,0:T(8,128)S(1)} all-to-all(f32[4,128,256]{2,1,0:T(8,128)S(1)} %back.1), channel_id=1, replica_groups=mesh['zhi'=2,'x'=4,'sky'=32] {'x'}, dimensions={0} | all-to-all | bytes 1048576 | tf_op jit(solution)/shard_map/all_to_all | solution.py:542
  109.0 0.7 final.1
  (43 shorter events, 0.1 us)
Async XLA Ops:
  0.6 1.6 %copy-start = (bf16[8,64,2048]{2,1,0:T(8,128)(2,1)S(1)}, bf16[8,64,2048]{2,1,0:T(8,128)(2,1)}, u32[]{:S(2)}) copy-start(bf16[8,64,2048]{2,1,0:T(8,128)(2,1)} %top_ref.1) | copy-start | bytes 6291460
  2.2 8.9 %copy-start.1 = (bf16[8,64,2048]{2,1,0:T(8,128)(2,1)S(1)}, bf16[8,64,2048]{2,1,0:T(8,128)(2,1)}, u32[]{:S(2)}) copy-start(bf16[8,64,2048]{2,1,0:T(8,128)(2,1)} %top_ref.1) | copy-start | bytes 6291460
  2.2 8.9 %copy-start.14 = (s32[1,8,256]{2,1,0:T(8,128)S(1)}, s32[1,8,256]{2,1,0:T(8,128)}, u32[]{:S(2)}) copy-start(s32[1,8,256]{2,1,0:T(8,128)} %refine_ref.1) | copy-start | bytes 24580
  2.2 8.9 %copy-start.16 = (f32[8]{0:T(128)S(1)}, f32[8]{0:T(128)}, u32[]{:S(2)}) copy-start(f32[8]{0:T(128)} %low_ref.3) | copy-start | bytes 100
  2.2 8.9 %copy-start.17 = (f32[8]{0:T(128)S(1)}, f32[8]{0:T(128)}, u32[]{:S(2)}) copy-start(f32[8]{0:T(128)} %high_ref.3) | copy-start | bytes 100
  2.3 21.4 %collective-permute-start.2 = (f32[8,2048]{1,0:T(8,128)S(1)}, f32[8,2048]{1,0:T(8,128)S(1)}, u32[]{:S(2)}, u32[]{:S(2)}) collective-permute-start(f32[8,2048]{1,0:T(8,128)S(1)} %get-tuple-element.10), channel_id=1, source_target_pairs={{0,1},{1,2},{2,3},{3,4},{4,5},{5,6},{6,7},{7,8},{8,9},{9,10},{10,1... | collective-permute-start | bytes 196616 | tf_op jit(solution)/shard_map/ppermute | solution.py:515
  5.1 18.6 %collective-permute-start.3 = (f32[8,2048]{1,0:T(8,128)S(1)}, f32[8,2048]{1,0:T(8,128)S(1)}, u32[]{:S(2)}, u32[]{:S(2)}) collective-permute-start(f32[8,2048]{1,0:T(8,128)S(1)} %get-tuple-element.11), channel_id=1, source_target_pairs={{1,0},{2,1},{3,2},{4,3},{5,4},{6,5},{7,6},{8,7},{9,8},{10,9},{11,1... | collective-permute-start | bytes 196616 | tf_op jit(solution)/shard_map/ppermute | solution.py:516
  5.8 18.0 %collective-permute-start.1 = (bf16[1,64,2048]{2,1,0:T(8,128)(2,1)S(1)}, bf16[1,64,2048]{2,1,0:T(8,128)(2,1)S(1)}, u32[]{:S(2)}, u32[]{:S(2)}) collective-permute-start(bf16[1,64,2048]{2,1,0:T(8,128)(2,1)S(1)} %get-tuple-element.18), channel_id=1, source_target_pairs={{32,0},{64,32},{96,64},{128,96},{160,128},{192,160},{224,192},{33,... | collective-permute-start | bytes 786440 | tf_op jit(solution)/shard_map/ppermute | solution.py:512
  7.1 16.7 %collective-permute-start = (bf16[1,64,2048]{2,1,0:T(8,128)(2,1)S(1)}, bf16[1,64,2048]{2,1,0:T(8,128)(2,1)S(1)}, u32[]{:S(2)}, u32[]{:S(2)}) collective-permute-start(bf16[1,64,2048]{2,1,0:T(8,128)(2,1)S(1)} %get-tuple-element.19), channel_id=1, source_target_pairs={{0,32},{32,64},{64,96},{96,128},{128,160},{160,192},{192,224},{1,3... | collective-permute-start | bytes 786440 | tf_op jit(solution)/shard_map/ppermute | solution.py:513
  18.6 0.8 copy-start.4
  19.4 0.8 copy-start.5
  20.2 0.8 copy-start.6
  20.9 0.8 copy-start.7
  21.7 0.7 copy-start.8
  22.4 0.6 copy-start.11
  23.7 0.8 copy-start.20
  23.7 0.8 copy-start.21
  23.8 0.8 copy-start.18
  23.8 0.8 copy-start.19
  30.0 45.9 %copy-start.9 = (f32[32,8,128]{2,1,0:T(8,128)S(1)}, f32[32,8,128]{2,1,0:T(8,128)}, u32[]{:S(2)}) copy-start(f32[32,8,128]{2,1,0:T(8,128)} %constant.57.clone.sin_ref) | copy-start | bytes 393220
  30.0 45.9 %copy-start.10 = (f32[32,8,128]{2,1,0:T(8,128)S(1)}, f32[32,8,128]{2,1,0:T(8,128)}, u32[]{:S(2)}) copy-start(f32[32,8,128]{2,1,0:T(8,128)} %constant.56.clone.cos_ref) | copy-start | bytes 393220
  30.0 45.9 %copy-start.12 = (bf16[128,256]{1,0:T(8,128)(2,1)S(1)}, bf16[128,256]{1,0:T(8,128)(2,1)}, u32[]{:S(2)}) copy-start(bf16[128,256]{1,0:T(8,128)(2,1)} %constant.59.clone.low_table) | copy-start | bytes 196612
  30.1 45.9 %copy-start.13 = (bf16[128,256]{1,0:T(8,128)(2,1)S(1)}, bf16[128,256]{1,0:T(8,128)(2,1)}, u32[]{:S(2)}) copy-start(bf16[128,256]{1,0:T(8,128)(2,1)} %constant.58.clone.high_table) | copy-start | bytes 196612
  30.1 45.9 %copy-start.15 = (s32[3]{0:T(128)S(1)}, s32[3]{0:T(128)}, u32[]{:S(2)}) copy-start(s32[3]{0:T(128)} %pad_add_fusion.pos_ref) | copy-start | bytes 40
  30.1 66.0 %copy-start.2 = (bf16[4,512,256]{2,1,0:T(8,128)(2,1)S(1)}, bf16[4,512,256]{2,1,0:T(8,128)(2,1)}, u32[]{:S(2)}) copy-start(bf16[4,512,256]{2,1,0:T(8,128)(2,1)} %constant.61.clone.low_table) | copy-start | bytes 3145732
  30.1 66.0 %copy-start.3 = (bf16[4,512,256]{2,1,0:T(8,128)(2,1)S(1)}, bf16[4,512,256]{2,1,0:T(8,128)(2,1)}, u32[]{:S(2)}) copy-start(bf16[4,512,256]{2,1,0:T(8,128)(2,1)} %constant.60.clone.high_table) | copy-start | bytes 3145732
  47.5 28.5 %all-to-all-start.1 = ((f32[64,8,128]{2,1,0:T(8,128)}), f32[64,8,128]{2,1,0:T(8,128)S(1)}, u32[]{:S(2)}, u32[]{:S(2)}) async-start(f32[64,8,128]{2,1,0:T(8,128)} %turn.1), calls=%async_computation.1 | async-start | bytes 524288 | tf_op jit(solution)/shard_map/all_to_all | solution.py:533
  78.2 17.9 %all-to-all-start.2 = ((f32[64,8,128]{2,1,0:T(8,128)}), f32[64,8,128]{2,1,0:T(8,128)S(1)}, u32[]{:S(2)}, u32[]{:S(2)}) async-start(f32[64,8,128]{2,1,0:T(8,128)} %solve.1), calls=%async_computation.2 | async-start | bytes 524288 | tf_op jit(solution)/shard_map/all_to_all | solution.py:537
where the time goes:
time: 110 us
  starting transfers between devices  28.7 us (26%)
  blocking collectives  28.2 us (26%)
  waiting for transfers between devices  26 us (24%)
  Pallas kernels  17.9 us (16%)
  local copies, waits for them, and re-layouts  7.12 us (6%)
    all_to_all x1, blocking collectives, body(): summed = lax.all_to_all(summed, 'x', 0, 0, tiled=True)  16.5 us
    all_to_all x1, starting transfers between devices, body(): pieces = lax.all_to_all(turn(summed), ('zhi', 'sky'), 0, 0, tiled=True)  15.3 us
    all_to_all x1, waiting for transfers between devices, body(): pieces = lax.all_to_all(turn(summed), ('zhi', 'sky'), 0, 0, tiled=True)  13.2 us
    all_to_all x1, waiting for transfers between devices, body(): pieces = lax.all_to_all(pieces, ('zhi', 'sky'), 0, 0, tiled=True)  12.8 us
    all_to_all x1, blocking collectives, body(): fields = lax.all_to_all(fields, 'x', 0, 0, tiled=True)  11.7 us
    pallas_call x1, Pallas kernels, inner_sums(): pl.pallas_call(inner_kernel, out_shape=(field, field, field, field, jax.S...  7.4 us
    unnamed x44, local copies, waits for them, and re-layouts  6.15 us
    pallas_call x1, Pallas kernels, outer_sums(): pl.pallas_call(outer_kernel, grid=(1,), out_shape=jax.ShapeDtypeStruct((4...  5.47 us
  transfers between devices with their start and end apart: 6, of which 2 were waited for; matrix products, arithmetic and copies ran while one was open for 1% of the time, Pallas kernels for 7%

commit v1 on v0

--- a/solution.py
+++ b/solution.py
@@ -106,29 +106,22 @@
 SM = pl.BlockSpec(memory_space=pltpu.SMEM)
 
 
-def rows_kernel(first_ref, last_ref, low_ref, high_ref):
+def rows_kernel(d_ref, low_ref, high_ref):
     for z in range(LAYERS):
-        low_ref[z : z + 1, :] = first_ref[z].astype(f32)[0:1]
-        high_ref[z : z + 1, :] = last_ref[z].astype(f32)[15:16]
+        low_ref[z : z + 1, :] = d_ref[z, 0:16, :].astype(f32)[0:1]
+        high_ref[z : z + 1, :] = d_ref[z, 48:64, :].astype(f32)[15:16]
 
 
 def edge_rows(density):
     shape = jax.ShapeDtypeStruct((LAYERS, N), f32)
     return pl.pallas_call(
         rows_kernel,
-        grid=(1,),
         out_shape=(shape, shape),
-        in_specs=[
-            pl.BlockSpec((LAYERS, 16, N), lambda i: (0, 0, 0)),
-            pl.BlockSpec((LAYERS, 16, N), lambda i: (0, 3, 0)),
-        ],
-        out_specs=(
-            pl.BlockSpec((LAYERS, N), lambda i: (0, 0)),
-            pl.BlockSpec((LAYERS, N), lambda i: (0, 0)),
-        ),
-        compiler_params=limit(24),
+        in_specs=[VM],
+        out_specs=(VM, VM),
+        compiler_params=limit(8),
         name="edge_rows",
-    )(density, density)
+    )(density)
 
 
 CHUNK = 512
@@ -220,10 +213,7 @@
 def outer_kernel(
     low_ref,
     high_ref,
-    pos_ref,
-    average_ref,
-    bottom_ref,
-    top_ref,
+    d_ref,
     below_ref,
     above_ref,
     before_ref,
@@ -238,9 +228,9 @@
     low_table,
     out_ref,
 ):
-    los = pos_ref[0] * 4 + pos_ref[1]
-    v0, v1 = bottom_ref[0].astype(f32), bottom_ref[1].astype(f32)
-    v6, v7 = top_ref[0].astype(f32), top_ref[1].astype(f32)
+    los = lax.axis_index("zhi") * 4 + lax.axis_index("x")
+    v0, v1 = d_ref[0].astype(f32), d_ref[1].astype(f32)
+    v6, v7 = d_ref[6].astype(f32), d_ref[7].astype(f32)
     below = jnp.where(los == 0, v0, below_ref[0].astype(f32))
     above = jnp.where(los == 7, v7, above_ref[0].astype(f32))
     slope0 = 0.125 * (high_ref[0] - low_ref[0])
@@ -249,7 +239,10 @@
     mask = mask_ref[...]
     marked = jnp.broadcast_to(mask[:, None, :], (8, 8, N)).reshape(ROWS, N)
     lifted = lifted_ref[...] + marked * tz
-    average = average_ref[:, 0:1]
+    layer = lax.broadcasted_iota(jnp.int32, (LAYERS, 1), 0)
+    average = jnp.zeros((LAYERS, 1), f32)
+    for z in range(LAYERS):
+        average = jnp.where(layer == z, 0.5 * (low_ref[z] + high_ref[z]), average)
     r0, r1, r62, r63 = near_ref[0], near_ref[1], near_ref[2], near_ref[3]
     e0 = jnp.sum(average * minmod(r1 - r0, r0 - before_ref[...]), axis=0, keepdims=True)
     e63 = jnp.sum(average * minmod(after_ref[...] - r63, r63 - r62), axis=0, keepdims=True)
@@ -296,36 +289,15 @@
         out_ref[tile // 2, :, lanes : lanes + 256] = dot3(value, high_table[tile], low_table[tile])
 
 
-def outer_sums(low, high, pos, average, density, below, above, before, after, inner, tables):
-    whole = lambda *shape: pl.BlockSpec(shape, lambda i: (0,) * len(shape))
+def outer_sums(low, high, density, below, above, before, after, inner, tables):
     return pl.pallas_call(
         outer_kernel,
-        grid=(1,),
         out_shape=jax.ShapeDtypeStruct((4, 72, 512), f32),
-        in_specs=[
-            SM,
-            SM,
-            SM,
-            whole(LAYERS, 128),
-            pl.BlockSpec((2, ROWS, N), lambda i: (0, 0, 0)),
-            pl.BlockSpec((2, ROWS, N), lambda i: (3, 0, 0)),
-            whole(1, ROWS, N),
-            whole(1, ROWS, N),
-            whole(LAYERS, N),
-            whole(LAYERS, N),
-            whole(ROWS, N),
-            whole(ROWS, N),
-            whole(ROWS, N),
-            whole(ROWS, N),
-            whole(8, N),
-            whole(4, LAYERS, N),
-            whole(8, 256, 256),
-            whole(8, 256, 256),
-        ],
-        out_specs=whole(4, 72, 512),
-        compiler_params=limit(56),
+        in_specs=[SM, SM] + [VM] * 13,
+        out_specs=VM,
+        compiler_params=limit(32),
         name="outer_sums",
-    )(low, high, pos, average, density, density, below, above, before, after, *inner, *tables)
+    )(low, high, density, below, above, before, after, *inner, *tables)
 
 
 def turn_kernel(in_ref, out_ref):
@@ -374,9 +346,9 @@
     return cosine, sine
 
 
-def solve_kernel(pos_ref, in_ref, cos_ref, sin_ref, high_table, low_table, out_ref):
-    zhi, column, sky = pos_ref[0], pos_ref[1], pos_ref[2]
-    tile = 2 * column + zhi
+def solve_kernel(in_ref, cos_ref, sin_ref, high_table, low_table, out_ref):
+    sky = lax.axis_index("sky")
+    tile = 2 * lax.axis_index("x") + lax.axis_index("zhi")
     lane = lax.broadcasted_iota(jnp.int32, (8, 128), 1)
     sub = lax.broadcasted_iota(jnp.int32, (8, 128), 0)
     lower = lane < 64
@@ -446,18 +418,19 @@
             out_ref[SKY + at] = v
 
 
-def solve(pos, pieces, tables):
+def solve(pieces, tables):
     return pl.pallas_call(
         solve_kernel,
         out_shape=jax.ShapeDtypeStruct((64, 8, 128), f32),
-        in_specs=[SM] + [VM] * 5,
+        in_specs=[VM] * 5,
         out_specs=VM,
         compiler_params=limit(24),
         name="solve",
-    )(pos, pieces, *tables)
-
-
-def back_kernel(pos_ref, phase_ref, in_ref, high_table, low_table, out_ref):
+    )(pieces, *tables)
+
+
+def back_kernel(eighth_ref, in_ref, high_table, low_table, out_ref):
+    zhi, column = lax.axis_index("zhi"), lax.axis_index("x")
     value = in_ref[...]
     sub = lax.broadcasted_iota(jnp.int32, (64, 8, 128), 1)
     bent = pltpu.roll(value, 4, 1) * jnp.where(sub < 4, -1.0, 1.0)
@@ -467,25 +440,24 @@
         parts = []
         for half in range(2):
             lanes = slice(256 * half, 256 * half + 256)
-            at = 4 * target + 2 * half
-            parts.append(phase_ref[at] * plain[:, lanes] + phase_ref[at + 1] * bent[:, lanes])
-        out_ref[target] = dot3(jnp.concatenate(parts, axis=1), high_table[0], low_table[0])
-
-
-def back(pos, phase, pieces, tables):
-    table = pl.BlockSpec((1, 512, 256), lambda i, pos, phase: (pos[1], 0, 0))
+            turns = (2 * column + half) * (4 * zhi + target) % 8
+            cosine, sine = eighth_ref[turns], eighth_ref[8 + turns]
+            parts.append(cosine * plain[:, lanes] + sine * bent[:, lanes])
+        value = jnp.concatenate(parts, axis=1)
+        out_ref[target] = dot3(value, high_table[column], low_table[column])
+
+
+def back(pieces, tables):
+    turns = np.arange(8) * (2 * np.pi / 8)
+    eighth = np.concatenate([np.cos(turns), np.sin(turns)]).astype(np.float32)
     return pl.pallas_call(
         back_kernel,
-        grid_spec=pltpu.PrefetchScalarGridSpec(
-            num_scalar_prefetch=2,
-            grid=(1,),
-            in_specs=[pl.BlockSpec((64, 8, 128), lambda i, pos, phase: (0, 0, 0)), table, table],
-            out_specs=pl.BlockSpec((4, 128, 256), lambda i, pos, phase: (0, 0, 0)),
-        ),
         out_shape=jax.ShapeDtypeStruct((4, 128, 256), f32),
+        in_specs=[SM, VM, VM, VM],
+        out_specs=VM,
         compiler_params=limit(24),
         name="back",
-    )(pos, phase, pieces, *tables)
+    )(eighth, pieces, *tables)
 
 
 def final_kernel(in_ref, x_ref, y_ref):
@@ -507,38 +479,21 @@
 
 
 def body(density, refine, weight_low, weight_high):
-    zhi, column, sky = lax.axis_index("zhi"), lax.axis_index("x"), lax.axis_index("sky")
-    pos = jnp.stack([zhi, column, sky]).astype(jnp.int32)
     above = lax.ppermute(density[:1], LOS, [(i + 1, i) for i in range(7)])
     below = lax.ppermute(density[-1:], LOS, [(i, i + 1) for i in range(7)])
     row_first, row_last = edge_rows(density)
     before = lax.ppermute(row_last, "sky", [(i, (i + 1) % SKY) for i in range(SKY)])
     after = lax.ppermute(row_first, "sky", [((i + 1) % SKY, i) for i in range(SKY)])
     inner = inner_sums(weight_low, weight_high, density, refine)
-    average = jnp.broadcast_to((0.5 * (weight_low + weight_high))[:, None], (LAYERS, 128))
+    tables = halves(forward_table())
     summed = outer_sums(
-        weight_low,
-        weight_high,
-        pos,
-        average,
-        density,
-        below,
-        above,
-        before,
-        after,
-        inner,
-        halves(forward_table()),
+        weight_low, weight_high, density, below, above, before, after, inner, tables
     )
     summed = lax.all_to_all(summed, "x", 0, 0, tiled=True)
     pieces = lax.all_to_all(turn(summed), ("zhi", "sky"), 0, 0, tiled=True)
-    cosine, sine = twists()
-    high, low = halves(row_table())
-    pieces = solve(pos, pieces, (cosine, sine, high, low))
+    pieces = solve(pieces, twists() + halves(row_table()))
     pieces = lax.all_to_all(pieces, ("zhi", "sky"), 0, 0, tiled=True)
-    eighths = (2 * column + jnp.arange(2))[None, :] * (4 * zhi + jnp.arange(4))[:, None] % 8
-    angle = eighths.astype(f32) * (2 * np.pi / 8)
-    phase = jnp.stack([jnp.cos(angle), jnp.sin(angle)], axis=-1).reshape(16)
-    fields = back(pos, phase, pieces, halves(inverse_table()))
+    fields = back(pieces, halves(inverse_table()))
     fields = lax.all_to_all(fields, "x", 0, 0, tiled=True)
     return final(fields)
 

time: 110 us -> 101 us (0.918)
  blocking collectives: 28.2 us -> 74.3 us
  waiting for transfers between devices: 26 us -> 0.01 us
  starting transfers between devices: 28.7 us -> 9.26 us
  Pallas kernels: 17.9 us -> 13 us
  local copies, waits for them, and re-layouts: 7.12 us -> 2.74 us
    all_to_all x0 -> x2, blocking collectives: none -> 46.3 us  [the longest x1 28.6 us: body(): pieces = lax.all_to_all(turn(summed), ('zhi', 'sky'), 0, 0, tiled=True)]
    all_to_all x2 -> x0, waiting for transfers between devices: 26 us -> none  [the longest x1 13.2 us: body(): pieces = lax.all_to_all(turn(summed), ('zhi', 'sky'), 0, 0, tiled=True)]
    all_to_all x2 -> x0, starting transfers between devices: 20 us -> none  [the longest x1 15.3 us: body(): pieces = lax.all_to_all(turn(summed), ('zhi', 'sky'), 0, 0, tiled=True)]
    unnamed x44 -> x28, local copies, waits for them, and re-layouts: 6.15 us -> 1.65 us
    pallas_call x3, Pallas kernels: 6.84 us -> 3.8 us  [the longest x1 2.4 us: outer_sums(): pl.pallas_call(outer_kernel, out_shape=jax.ShapeDtypeStruct((4, 72, 512),...]
    pallas_call x1, Pallas kernels: 2.2 us -> 0.98 us  [solve(): pl.pallas_call(solve_kernel, out_shape=jax.ShapeDtypeStruct((64, 8, 128),...]
  transfers between devices with their start and end apart: 6 -> 4, of which waited for: 2 -> 0; matrix products, arithmetic and copies ran while one was open for 1% -> 0% of each run, Pallas kernels for 7% -> 7%
where the time goes in v1:
time: 101 us; the launch traced here: 100 us
  blocking collectives  74.3 us (74%)
  Pallas kernels  13 us (13%)
  starting transfers between devices  9.26 us (9%)
  local copies, waits for them, and re-layouts  2.74 us (3%)
    all_to_all x1, blocking collectives, body(): pieces = lax.all_to_all(turn(summed), ('zhi', 'sky'), 0, 0, tiled=True)  28.6 us
    all_to_all x1, blocking collectives, body(): pieces = lax.all_to_all(pieces, ('zhi', 'sky'), 0, 0, tiled=True)  17.7 us
    all_to_all x1, blocking collectives, body(): summed = lax.all_to_all(summed, 'x', 0, 0, tiled=True)  16.3 us
    all_to_all x1, blocking collectives, body(): fields = lax.all_to_all(fields, 'x', 0, 0, tiled=True)  11.7 us
    pallas_call x1, Pallas kernels, inner_sums(): pl.pallas_call(inner_kernel, out_shape=(field, field, field, field, jax.S...  7.4 us
    ppermute x1, starting transfers between devices, body(): below = lax.ppermute(density[-1:], LOS, [(i, i + 1) for i in range(7)])  4.59 us
    ppermute x1, starting transfers between devices, body(): lax.ppermute(row_last, 'sky', [(i, (i + 1) % SKY) for i in range(SKY)])  2.74 us
    pallas_call x1, Pallas kernels, outer_sums(): pl.pallas_call(outer_kernel, out_shape=jax.ShapeDtypeStruct((4, 72, 512),...  2.4 us
  transfers between devices with their start and end apart: 4, of which 0 were waited for; matrix products, arithmetic and copies ran while one was open for 0% of the time, Pallas kernels for 7%

profile of v1, /device:TPU:1, one launch (start us, length us, event | category | flops | bytes accessed | tf_op | source)
XLA Modules:
  0.0 100.2 jit_solution(16044193759580446110)
XLA Ops:
  0.6 0.0 copy-start.12
  0.6 0.0 copy-start.11
  0.7 1.1 %fusion = (bf16[1,64,2048]{2,1,0:T(8,128)(2,1)S(1)}, bf16[1,64,2048]{2,1,0:T(8,128)(2,1)S(1)}) fusion(bf16[8,64,2048]{2,1,0:T(8,128)(2,1)} %d_ref.5), kind=kLoop, calls=%fused_computation | loop fusion | bytes 1048576 | tf_op jit(solution)/shard_map/slice | solution.py:482
  1.7 1.3 %collective-permute-start.1 = (bf16[1,64,2048]{2,1,0:T(8,128)(2,1)S(1)}, bf16[1,64,2048]{2,1,0:T(8,128)(2,1)S(1)}, u32[]{:S(2)}, u32[]{:S(2)}) collective-permute-start(bf16[1,64,2048]{2,1,0:T(8,128)(2,1)S(1)} %get-tuple-element.18), channel_id=1, source_target_pairs={{32,0},{64,32},{96,64},{128,96},{160,128},{192,160},{224,192},{33,... | collective-permute-start | bytes 786440 | tf_op jit(solution)/shard_map/ppermute | solution.py:482
  3.0 4.6 %collective-permute-start = (bf16[1,64,2048]{2,1,0:T(8,128)(2,1)S(1)}, bf16[1,64,2048]{2,1,0:T(8,128)(2,1)S(1)}, u32[]{:S(2)}, u32[]{:S(2)}) collective-permute-start(bf16[1,64,2048]{2,1,0:T(8,128)(2,1)S(1)} %get-tuple-element.19), channel_id=1, source_target_pairs={{0,32},{32,64},{64,96},{96,128},{128,160},{160,192},{192,224},{1,3... | collective-permute-start | bytes 786440 | tf_op jit(solution)/shard_map/ppermute | solution.py:483
  7.6 0.0 copy-start
  7.7 1.6 %copy-done = bf16[8,64,2048]{2,1,0:T(8,128)(2,1)S(1)} copy-done((bf16[8,64,2048]{2,1,0:T(8,128)(2,1)S(1)}, bf16[8,64,2048]{2,1,0:T(8,128)(2,1)}, u32[]{:S(2)}) %copy-start) | copy-done | bytes 2097176
  9.2 0.1 edge_rows.1
  9.3 2.7 %collective-permute-start.2 = (f32[8,2048]{1,0:T(8,128)S(1)}, f32[8,2048]{1,0:T(8,128)S(1)}, u32[]{:S(2)}, u32[]{:S(2)}) collective-permute-start(f32[8,2048]{1,0:T(8,128)S(1)} %get-tuple-element.10), channel_id=1, source_target_pairs={{0,1},{1,2},{2,3},{3,4},{4,5},{5,6},{6,7},{7,8},{8,9},{9,10},{10,1... | collective-permute-start | bytes 196616 | tf_op jit(solution)/shard_map/ppermute | solution.py:485
  12.1 0.6 collective-permute-start.3
  12.7 0.0 copy-done.11
  12.7 7.4 %inner_sums.1 = (f32[64,2048]{1,0:T(8,128)S(1)}, f32[64,2048]{1,0:T(8,128)S(1)}, f32[64,2048]{1,0:T(8,128)S(1)}, f32[64,2048]{1,0:T(8,128)S(1)}, f32[8,2048]{1,0:T(8,128)S(1)}, /*index=5*/f32[4,8,2048]{2,1,0:T(8,128)S(1)}) custom-call(f32[8]{0:T(128)S(1)} %copy-done.11, f32[8]{0:T(128)S(1)} %copy-done.12, bf16[8,64,2048]{2,1,0:T(8,128)(2,1)S(1)} %copy-done.1, ...), custom_call_target="tpu_custom_call" | custom-call | flops 40000000 | bytes 25165824 | tf_op jit(solution)/shard_map/inner_sums/pallas_call | solution.py:195
  20.1 0.0 collective-permute-done.2.before_ref
  20.2 0.0 collective-permute-done.3.after_ref
  20.2 0.0 collective-permute-done.1.above_ref
  20.2 0.0 collective-permute-done.below_ref
  20.2 2.4 %outer_sums.1 = f32[4,72,512]{2,1,0:T(8,128)S(1)} custom-call(f32[8]{0:T(128)S(1)} %copy-done.11, f32[8]{0:T(128)S(1)} %copy-done.12, bf16[8,64,2048]{2,1,0:T(8,128)(2,1)S(1)} %copy-done.1, bf16[1,64,2048]{2,1,0:T(8,128)(2,1)S(1)} %collective-permute-done.below_ref, bf16[1,64,2048]{2,1,0:T(8,128)(2,1)S(1)} %collective-permute-done.1.above_ref, ...), custom_call_target="tpu_custom_call" | custom-call | tf_op jit(solution)/shard_map/outer_sums/pallas_call | solution.py:293
  22.6 0.0 copy-start.7
  22.6 0.0 copy-start.8
  22.6 0.0 copy-start.9
  22.7 0.0 copy-start.2
  22.7 0.0 copy-start.3
  22.7 0.0 copy-start.13
  22.7 16.3 %all_to_all.20.in_ref = f32[4,72,512]{2,1,0:T(8,128)S(1)} all-to-all(f32[4,72,512]{2,1,0:T(8,128)S(1)} %outer_sums.1), channel_id=1, replica_groups=mesh['zhi'=2,'x'=4,'sky'=32] {'x'}, dimensions={0} | all-to-all | bytes 1179648 | tf_op jit(solution)/shard_map/all_to_all | solution.py:492
  39.0 0.1 turn.1
  39.2 28.6 %all_to_all.21.in_ref = f32[64,8,128]{2,1,0:T(8,128)S(1)} all-to-all(f32[64,8,128]{2,1,0:T(8,128)S(1)} %turn.1), channel_id=1, replica_groups=mesh['zhi'=2,'x'=4,'sky'=32] {'zhi','sky'}, dimensions={0} | all-to-all | bytes 524288 | tf_op jit(solution)/shard_map/all_to_all | solution.py:493
  67.8 0.0 copy-done.9
  67.8 1.0 solve.1
  68.8 17.7 %all_to_all.22.in_ref = f32[64,8,128]{2,1,0:T(8,128)S(1)} all-to-all(f32[64,8,128]{2,1,0:T(8,128)S(1)} %solve.1), channel_id=1, replica_groups=mesh['zhi'=2,'x'=4,'sky'=32] {'zhi','sky'}, dimensions={0} | all-to-all | bytes 524288 | tf_op jit(solution)/shard_map/all_to_all | solution.py:495
  86.5 1.3 %back.1 = f32[4,128,256]{2,1,0:T(8,128)S(1)} custom-call(f32[16]{0:T(128)S(1)} %copy-done.13, f32[64,8,128]{2,1,0:T(8,128)S(1)} %all_to_all.22.in_ref, bf16[4,512,256]{2,1,0:T(8,128)(2,1)S(1)} %copy-done.3, bf16[4,512,256]{2,1,0:T(8,128)(2,1)S(1)} %copy-done.2), custom_call_target="tpu_custom_call" | custom-call | tf_op jit(solution)/shard_map/back/pallas_call | solution.py:453
  87.8 11.7 %all_to_all.23.in_ref = f32[4,128,256]{2,1,0:T(8,128)S(1)} all-to-all(f32[4,128,256]{2,1,0:T(8,128)S(1)} %back.1), channel_id=1, replica_groups=mesh['zhi'=2,'x'=4,'sky'=32] {'x'}, dimensions={0} | all-to-all | bytes 1048576 | tf_op jit(solution)/shard_map/all_to_all | solution.py:497
  99.5 0.7 final.1
  (16 shorter events, 0.0 us)
Async XLA Ops:
  0.6 12.1 %copy-start.12 = (f32[8]{0:T(128)S(1)}, f32[8]{0:T(128)}, u32[]{:S(2)}) copy-start(f32[8]{0:T(128)} %high_ref.3) | copy-start | bytes 100
  0.6 12.1 %copy-start.11 = (f32[8]{0:T(128)S(1)}, f32[8]{0:T(128)}, u32[]{:S(2)}) copy-start(f32[8]{0:T(128)} %low_ref.3) | copy-start | bytes 100
  0.7 12.1 %copy-start.10 = (s32[1,8,256]{2,1,0:T(8,128)S(1)}, s32[1,8,256]{2,1,0:T(8,128)}, u32[]{:S(2)}) copy-start(s32[1,8,256]{2,1,0:T(8,128)} %refine_ref.1) | copy-start | bytes 24580
  1.7 18.4 %collective-permute-start.1 = (bf16[1,64,2048]{2,1,0:T(8,128)(2,1)S(1)}, bf16[1,64,2048]{2,1,0:T(8,128)(2,1)S(1)}, u32[]{:S(2)}, u32[]{:S(2)}) collective-permute-start(bf16[1,64,2048]{2,1,0:T(8,128)(2,1)S(1)} %get-tuple-element.18), channel_id=1, source_target_pairs={{32,0},{64,32},{96,64},{128,96},{160,128},{192,160},{224,192},{33,... | collective-permute-start | bytes 786440 | tf_op jit(solution)/shard_map/ppermute | solution.py:482
  3.0 17.1 %collective-permute-start = (bf16[1,64,2048]{2,1,0:T(8,128)(2,1)S(1)}, bf16[1,64,2048]{2,1,0:T(8,128)(2,1)S(1)}, u32[]{:S(2)}, u32[]{:S(2)}) collective-permute-start(bf16[1,64,2048]{2,1,0:T(8,128)(2,1)S(1)} %get-tuple-element.19), channel_id=1, source_target_pairs={{0,32},{32,64},{64,96},{96,128},{128,160},{160,192},{192,224},{1,3... | collective-permute-start | bytes 786440 | tf_op jit(solution)/shard_map/ppermute | solution.py:483
  7.6 1.6 %copy-start = (bf16[8,64,2048]{2,1,0:T(8,128)(2,1)S(1)}, bf16[8,64,2048]{2,1,0:T(8,128)(2,1)}, u32[]{:S(2)}) copy-start(bf16[8,64,2048]{2,1,0:T(8,128)(2,1)} %d_ref.5) | copy-start | bytes 6291460
  9.2 3.5 %copy-start.1 = (bf16[8,64,2048]{2,1,0:T(8,128)(2,1)S(1)}, bf16[8,64,2048]{2,1,0:T(8,128)(2,1)}, u32[]{:S(2)}) copy-start(bf16[8,64,2048]{2,1,0:T(8,128)(2,1)} %d_ref.5) | copy-start | bytes 6291460
  9.2 10.9 %copy-start.4 = (bf16[8,256,256]{2,1,0:T(8,128)(2,1)S(1)}, bf16[8,256,256]{2,1,0:T(8,128)(2,1)}, u32[]{:S(2)}) copy-start(bf16[8,256,256]{2,1,0:T(8,128)(2,1)} %constant.19.clone.low_table) | copy-start | bytes 3145732
  9.2 11.0 %copy-start.5 = (bf16[8,256,256]{2,1,0:T(8,128)(2,1)S(1)}, bf16[8,256,256]{2,1,0:T(8,128)(2,1)}, u32[]{:S(2)}) copy-start(bf16[8,256,256]{2,1,0:T(8,128)(2,1)} %constant.18.clone.high_table) | copy-start | bytes 3145732
  9.3 10.8 %collective-permute-start.2 = (f32[8,2048]{1,0:T(8,128)S(1)}, f32[8,2048]{1,0:T(8,128)S(1)}, u32[]{:S(2)}, u32[]{:S(2)}) collective-permute-start(f32[8,2048]{1,0:T(8,128)S(1)} %get-tuple-element.10), channel_id=1, source_target_pairs={{0,1},{1,2},{2,3},{3,4},{4,5},{5,6},{6,7},{7,8},{8,9},{9,10},{10,1... | collective-permute-start | bytes 196616 | tf_op jit(solution)/shard_map/ppermute | solution.py:485
  12.1 8.1 %collective-permute-start.3 = (f32[8,2048]{1,0:T(8,128)S(1)}, f32[8,2048]{1,0:T(8,128)S(1)}, u32[]{:S(2)}, u32[]{:S(2)}) collective-permute-start(f32[8,2048]{1,0:T(8,128)S(1)} %get-tuple-element.11), channel_id=1, source_target_pairs={{1,0},{2,1},{3,2},{4,3},{5,4},{6,5},{7,6},{8,7},{9,8},{10,9},{11,1... | collective-permute-start | bytes 196616 | tf_op jit(solution)/shard_map/ppermute | solution.py:486
  22.6 45.2 %copy-start.6 = (f32[32,8,128]{2,1,0:T(8,128)S(1)}, f32[32,8,128]{2,1,0:T(8,128)}, u32[]{:S(2)}) copy-start(f32[32,8,128]{2,1,0:T(8,128)} %constant.21.clone.sin_ref) | copy-start | bytes 393220
  22.6 45.2 %copy-start.7 = (f32[32,8,128]{2,1,0:T(8,128)S(1)}, f32[32,8,128]{2,1,0:T(8,128)}, u32[]{:S(2)}) copy-start(f32[32,8,128]{2,1,0:T(8,128)} %constant.20.clone.cos_ref) | copy-start | bytes 393220
  22.6 45.2 %copy-start.8 = (bf16[128,256]{1,0:T(8,128)(2,1)S(1)}, bf16[128,256]{1,0:T(8,128)(2,1)}, u32[]{:S(2)}) copy-start(bf16[128,256]{1,0:T(8,128)(2,1)} %constant.23.clone.low_table) | copy-start | bytes 196612
  22.6 45.2 %copy-start.9 = (bf16[128,256]{1,0:T(8,128)(2,1)S(1)}, bf16[128,256]{1,0:T(8,128)(2,1)}, u32[]{:S(2)}) copy-start(bf16[128,256]{1,0:T(8,128)(2,1)} %constant.22.clone.high_table) | copy-start | bytes 196612
  22.7 63.8 %copy-start.2 = (bf16[4,512,256]{2,1,0:T(8,128)(2,1)S(1)}, bf16[4,512,256]{2,1,0:T(8,128)(2,1)}, u32[]{:S(2)}) copy-start(bf16[4,512,256]{2,1,0:T(8,128)(2,1)} %constant.26.clone.low_table) | copy-start | bytes 3145732
  22.7 63.8 %copy-start.3 = (bf16[4,512,256]{2,1,0:T(8,128)(2,1)S(1)}, bf16[4,512,256]{2,1,0:T(8,128)(2,1)}, u32[]{:S(2)}) copy-start(bf16[4,512,256]{2,1,0:T(8,128)(2,1)} %constant.25.clone.high_table) | copy-start | bytes 3145732
  22.7 63.8 %copy-start.13 = (f32[16]{0:T(128)S(1)}, f32[16]{0:T(128)}, u32[]{:S(2)}) copy-start(f32[16]{0:T(128)} %constant.24.clone.eighth_ref) | copy-start | bytes 196

commit v2 on v1

--- a/solution.py
+++ b/solution.py
@@ -106,19 +106,23 @@
 SM = pl.BlockSpec(memory_space=pltpu.SMEM)
 
 
-def rows_kernel(d_ref, low_ref, high_ref):
+def rows_kernel(d_ref, near_ref, far_ref, layer_ref):
+    layer_ref[0] = jnp.where(lax.axis_index("x") % 2 == 1, d_ref[0], d_ref[LAYERS - 1])
+    even = lax.axis_index("sky") % 2 == 0
     for z in range(LAYERS):
-        low_ref[z : z + 1, :] = d_ref[z, 0:16, :].astype(f32)[0:1]
-        high_ref[z : z + 1, :] = d_ref[z, 48:64, :].astype(f32)[15:16]
+        first = d_ref[z, 0:16, :].astype(f32)[0:1]
+        last = d_ref[z, 48:64, :].astype(f32)[15:16]
+        near_ref[z : z + 1, :] = jnp.where(even, last, first)
+        far_ref[z : z + 1, :] = jnp.where(even, first, last)
 
 
 def edge_rows(density):
     shape = jax.ShapeDtypeStruct((LAYERS, N), f32)
     return pl.pallas_call(
         rows_kernel,
-        out_shape=(shape, shape),
+        out_shape=(shape, shape, jax.ShapeDtypeStruct((1, ROWS, N), bf16)),
         in_specs=[VM],
-        out_specs=(VM, VM),
+        out_specs=(VM, VM, VM),
         compiler_params=limit(8),
         name="edge_rows",
     )(density)
@@ -214,10 +218,10 @@
     low_ref,
     high_ref,
     d_ref,
-    below_ref,
-    above_ref,
-    before_ref,
-    after_ref,
+    layer_ref,
+    other_layer_ref,
+    row_ref,
+    other_row_ref,
     calm_ref,
     lifted_ref,
     tx_ref,
@@ -231,8 +235,10 @@
     los = lax.axis_index("zhi") * 4 + lax.axis_index("x")
     v0, v1 = d_ref[0].astype(f32), d_ref[1].astype(f32)
     v6, v7 = d_ref[6].astype(f32), d_ref[7].astype(f32)
-    below = jnp.where(los == 0, v0, below_ref[0].astype(f32))
-    above = jnp.where(los == 7, v7, above_ref[0].astype(f32))
+    odd = los % 2 == 1
+    one, other = layer_ref[0].astype(f32), other_layer_ref[0].astype(f32)
+    below = jnp.where(los == 0, v0, jnp.where(odd, other, one))
+    above = jnp.where(los == 7, v7, jnp.where(odd, one, other))
     slope0 = 0.125 * (high_ref[0] - low_ref[0])
     slope7 = 0.125 * (high_ref[7] - low_ref[7])
     tz = slope0 * minmod(v1 - v0, v0 - below) + slope7 * minmod(above - v7, v7 - v6)
@@ -244,8 +250,11 @@
     for z in range(LAYERS):
         average = jnp.where(layer == z, 0.5 * (low_ref[z] + high_ref[z]), average)
     r0, r1, r62, r63 = near_ref[0], near_ref[1], near_ref[2], near_ref[3]
-    e0 = jnp.sum(average * minmod(r1 - r0, r0 - before_ref[...]), axis=0, keepdims=True)
-    e63 = jnp.sum(average * minmod(after_ref[...] - r63, r63 - r62), axis=0, keepdims=True)
+    even = lax.axis_index("sky") % 2 == 0
+    before = jnp.where(even, other_row_ref[...], row_ref[...])
+    after = jnp.where(even, row_ref[...], other_row_ref[...])
+    e0 = jnp.sum(average * minmod(r1 - r0, r0 - before), axis=0, keepdims=True)
+    e63 = jnp.sum(average * minmod(after - r63, r63 - r62), axis=0, keepdims=True)
     row = lax.broadcasted_iota(jnp.int32, (ROWS, N), 0)
     tx = jnp.where(row == 0, mask[0:1] * e0, jnp.where(row == ROWS - 1, mask[7:8] * e63, tx_ref[...]))
     eighth, tilt = 0.125 * lifted, ty_ref[...] * (1.0 / 32.0)
@@ -289,7 +298,7 @@
         out_ref[tile // 2, :, lanes : lanes + 256] = dot3(value, high_table[tile], low_table[tile])
 
 
-def outer_sums(low, high, density, below, above, before, after, inner, tables):
+def outer_sums(low, high, density, layers, rows, inner, tables):
     return pl.pallas_call(
         outer_kernel,
         out_shape=jax.ShapeDtypeStruct((4, 72, 512), f32),
@@ -297,7 +306,7 @@
         out_specs=VM,
         compiler_params=limit(32),
         name="outer_sums",
-    )(low, high, density, below, above, before, after, *inner, *tables)
+    )(low, high, density, *layers, *rows, *inner, *tables)
 
 
 def turn_kernel(in_ref, out_ref):
@@ -479,15 +488,21 @@
 
 
 def body(density, refine, weight_low, weight_high):
-    above = lax.ppermute(density[:1], LOS, [(i + 1, i) for i in range(7)])
-    below = lax.ppermute(density[-1:], LOS, [(i, i + 1) for i in range(7)])
-    row_first, row_last = edge_rows(density)
-    before = lax.ppermute(row_last, "sky", [(i, (i + 1) % SKY) for i in range(SKY)])
-    after = lax.ppermute(row_first, "sky", [((i + 1) % SKY, i) for i in range(SKY)])
+    odd = lax.axis_index("x") % 2 == 1
+
+    def swap(array, axes, pairs):
+        return lax.ppermute(array, axes, pairs + [(b, a) for a, b in pairs])
+
+    layer = lax.dynamic_slice_in_dim(density, jnp.where(odd, LAYERS - 1, 0), 1, 0)
+    layer = swap(layer, LOS, [(1, 2), (3, 4), (5, 6)])
+    row, other_row, other_layer = edge_rows(density)
+    other_layer = swap(other_layer, LOS, [(0, 1), (2, 3), (4, 5), (6, 7)])
+    row = swap(row, "sky", [(i, i + 1) for i in range(0, SKY, 2)])
+    other_row = swap(other_row, "sky", [(i, (i + 1) % SKY) for i in range(1, SKY, 2)])
     inner = inner_sums(weight_low, weight_high, density, refine)
     tables = halves(forward_table())
     summed = outer_sums(
-        weight_low, weight_high, density, below, above, before, after, inner, tables
+        weight_low, weight_high, density, (layer, other_layer), (row, other_row), inner, tables
     )
     summed = lax.all_to_all(summed, "x", 0, 0, tiled=True)
     pieces = lax.all_to_all(turn(summed), ("zhi", "sky"), 0, 0, tiled=True)

time: 101 us -> 97 us (0.960)
  blocking collectives: 74.3 us -> 72.4 us
  starting transfers between devices: 9.26 us -> 7.67 us
    all_to_all x1, blocking collectives: 28.6 us -> 26.5 us  [body(): pieces = lax.all_to_all(turn(summed), ('zhi', 'sky'), 0, 0, tiled=True)]
    ppermute x4, starting transfers between devices: 9.26 us -> 7.67 us  [swap(): return lax.ppermute(array, axes, pairs + [(b, a) for a, b in pairs])]
    slice x1 -> x0, local copies, waits for them, and re-layouts: 1.08 us -> none  [body(): above = lax.ppermute(density[:1], LOS, [(i + 1, i) for i in range(7)])]
  transfers between devices with their start and end apart: 4 -> 4, of which waited for: 0 -> 0; matrix products, arithmetic and copies ran while one was open for 0% -> 0% of each run, Pallas kernels for 7% -> 8%
where the time goes in v2:
time: 97 us; the launch traced here: 96.7 us
  blocking collectives  72.4 us (75%)
  Pallas kernels  13.1 us (14%)
  starting transfers between devices  7.67 us (8%)
  local copies, waits for them, and re-layouts  2.63 us (3%)
    all_to_all x1, blocking collectives, body(): pieces = lax.all_to_all(turn(summed), ('zhi', 'sky'), 0, 0, tiled=True)  26.5 us
    all_to_all x1, blocking collectives, body(): pieces = lax.all_to_all(pieces, ('zhi', 'sky'), 0, 0, tiled=True)  17.7 us
    all_to_all x1, blocking collectives, body(): summed = lax.all_to_all(summed, 'x', 0, 0, tiled=True)  16.6 us
    all_to_all x1, blocking collectives, body(): fields = lax.all_to_all(fields, 'x', 0, 0, tiled=True)  11.7 us
    ppermute x4, starting transfers between devices, swap(): return lax.ppermute(array, axes, pairs + [(b, a) for a, b in pairs])  7.67 us
    pallas_call x1, Pallas kernels, inner_sums(): pl.pallas_call(inner_kernel, out_shape=(field, field, field, field, jax.S...  7.4 us
    pallas_call x1, Pallas kernels, outer_sums(): pl.pallas_call(outer_kernel, out_shape=jax.ShapeDtypeStruct((4, 72, 512),...  2.44 us
  transfers between devices with their start and end apart: 4, of which 0 were waited for; matrix products, arithmetic and copies ran while one was open for 0% of the time, Pallas kernels for 8%

profile of v2, /device:TPU:1, one launch (start us, length us, event | category | flops | bytes accessed | tf_op | source)
XLA Modules:
  0.0 96.7 jit_solution(8216021401920771693)
XLA Ops:
  0.6 0.0 copy-start.12
  0.6 0.0 copy-start.11
  0.7 0.0 copy-start.10
  0.7 1.0 %constant_dynamic-slice_fusion = bf16[1,64,2048]{2,1,0:T(8,128)(2,1)S(1)} fusion(bf16[8,64,2048]{2,1,0:T(8,128)(2,1)} %d_ref.5, s32[]{:T(128)S(6)} %select_n.13), kind=kLoop, calls=%fused_computation | loop fusion | bytes 524292 | tf_op jit(solution)/shard_map/dynamic_slice | solution.py:496
  1.6 0.7 collective-permute-start
  2.3 0.0 copy-start
  2.3 1.6 %copy-done = bf16[8,64,2048]{2,1,0:T(8,128)(2,1)S(1)} copy-done((bf16[8,64,2048]{2,1,0:T(8,128)(2,1)S(1)}, bf16[8,64,2048]{2,1,0:T(8,128)(2,1)}, u32[]{:S(2)}) %copy-start) | copy-done | bytes 2097176
  3.9 0.2 edge_rows.1
  4.1 4.6 %collective-permute-start.1 = (bf16[1,64,2048]{2,1,0:T(8,128)(2,1)S(1)}, bf16[1,64,2048]{2,1,0:T(8,128)(2,1)S(1)}, u32[]{:S(2)}, u32[]{:S(2)}) collective-permute-start(bf16[1,64,2048]{2,1,0:T(8,128)(2,1)S(1)} %get-tuple-element.11), channel_id=1, source_target_pairs={{0,32},{64,96},{128,160},{192,224},{32,0},{96,64},{160,128},{224,1... | collective-permute-start | bytes 786440 | tf_op jit(solution)/shard_map/ppermute | solution.py:494
  8.7 1.2 %collective-permute-start.2 = (f32[8,2048]{1,0:T(8,128)S(1)}, f32[8,2048]{1,0:T(8,128)S(1)}, u32[]{:S(2)}, u32[]{:S(2)}) collective-permute-start(f32[8,2048]{1,0:T(8,128)S(1)} %get-tuple-element.12), channel_id=1, source_target_pairs={{0,1},{2,3},{4,5},{6,7},{8,9},{10,11},{12,13},{14,15},{16,17},{18,... | collective-permute-start | bytes 196616 | tf_op jit(solution)/shard_map/ppermute | solution.py:494
  9.9 1.2 %collective-permute-start.3 = (f32[8,2048]{1,0:T(8,128)S(1)}, f32[8,2048]{1,0:T(8,128)S(1)}, u32[]{:S(2)}, u32[]{:S(2)}) collective-permute-start(f32[8,2048]{1,0:T(8,128)S(1)} %get-tuple-element.13), channel_id=1, source_target_pairs={{1,2},{3,4},{5,6},{7,8},{9,10},{11,12},{13,14},{15,16},{17,18},{19... | collective-permute-start | bytes 196616 | tf_op jit(solution)/shard_map/ppermute | solution.py:494
  11.1 7.4 %inner_sums.1 = (f32[64,2048]{1,0:T(8,128)S(1)}, f32[64,2048]{1,0:T(8,128)S(1)}, f32[64,2048]{1,0:T(8,128)S(1)}, f32[64,2048]{1,0:T(8,128)S(1)}, f32[8,2048]{1,0:T(8,128)S(1)}, /*index=5*/f32[4,8,2048]{2,1,0:T(8,128)S(1)}) custom-call(f32[8]{0:T(128)S(1)} %copy-done.11, f32[8]{0:T(128)S(1)} %copy-done.12, bf16[8,64,2048]{2,1,0:T(8,128)(2,1)S(1)} %copy-done.1, ...), custom_call_target="tpu_custom_call" | custom-call | flops 40000000 | bytes 25165824 | tf_op jit(solution)/shard_map/inner_sums/pallas_call | solution.py:199
  18.5 0.0 collective-permute-done.2.row_ref
  18.6 0.0 collective-permute-done.3.other_row_ref
  18.6 0.0 collective-permute-done.layer_ref
  18.6 0.0 collective-permute-done.1.other_layer_ref
  18.6 2.4 %outer_sums.1 = f32[4,72,512]{2,1,0:T(8,128)S(1)} custom-call(f32[8]{0:T(128)S(1)} %copy-done.11, f32[8]{0:T(128)S(1)} %copy-done.12, bf16[8,64,2048]{2,1,0:T(8,128)(2,1)S(1)} %copy-done.1, bf16[1,64,2048]{2,1,0:T(8,128)(2,1)S(1)} %collective-permute-done.layer_ref, bf16[1,64,2048]{2,1,0:T(8,128)(2,1)S(1)} %collective-permute-done.1.other_layer_ref, ...), custom_call_target="tpu_custom_call" | custom-call | tf_op jit(solution)/shard_map/outer_sums/pallas_call | solution.py:302
  21.1 0.0 copy-start.7
  21.1 0.0 copy-start.8
  21.1 0.0 copy-start.9
  21.1 0.0 copy-start.2
  21.1 0.0 copy-start.3
  21.1 0.0 copy-start.13
  21.1 16.6 %all_to_all.20.in_ref = f32[4,72,512]{2,1,0:T(8,128)S(1)} all-to-all(f32[4,72,512]{2,1,0:T(8,128)S(1)} %outer_sums.1), channel_id=1, replica_groups=mesh['zhi'=2,'x'=4,'sky'=32] {'x'}, dimensions={0} | all-to-all | bytes 1179648 | tf_op jit(solution)/shard_map/all_to_all | solution.py:507
  37.7 0.1 turn.1
  37.8 26.5 %all_to_all.21.in_ref = f32[64,8,128]{2,1,0:T(8,128)S(1)} all-to-all(f32[64,8,128]{2,1,0:T(8,128)S(1)} %turn.1), channel_id=1, replica_groups=mesh['zhi'=2,'x'=4,'sky'=32] {'zhi','sky'}, dimensions={0} | all-to-all | bytes 524288 | tf_op jit(solution)/shard_map/all_to_all | solution.py:508
  64.3 0.0 copy-done.6
  64.3 1.0 %solve.1 = f32[64,8,128]{2,1,0:T(8,128)S(1)} custom-call(f32[64,8,128]{2,1,0:T(8,128)S(1)} %all_to_all.21.in_ref, f32[32,8,128]{2,1,0:T(8,128)S(1)} %copy-done.7, f32[32,8,128]{2,1,0:T(8,128)S(1)} %copy-done.6, bf16[128,256]{1,0:T(8,128)(2,1)S(1)} %copy-done.9, bf16[128,256]{1,0:T(8,128)(2,1)S(1)} %copy-done.8), custom_call_target="tpu_custom_call" | custom-call | tf_op jit(solution)/shard_map/solve/pallas_call | solution.py:431
  65.3 17.7 %all_to_all.22.in_ref = f32[64,8,128]{2,1,0:T(8,128)S(1)} all-to-all(f32[64,8,128]{2,1,0:T(8,128)S(1)} %solve.1), channel_id=1, replica_groups=mesh['zhi'=2,'x'=4,'sky'=32] {'zhi','sky'}, dimensions={0} | all-to-all | bytes 524288 | tf_op jit(solution)/shard_map/all_to_all | solution.py:510
  83.0 1.3 %back.1 = f32[4,128,256]{2,1,0:T(8,128)S(1)} custom-call(f32[16]{0:T(128)S(1)} %copy-done.13, f32[64,8,128]{2,1,0:T(8,128)S(1)} %all_to_all.22.in_ref, bf16[4,512,256]{2,1,0:T(8,128)(2,1)S(1)} %copy-done.3, bf16[4,512,256]{2,1,0:T(8,128)(2,1)S(1)} %copy-done.2), custom_call_target="tpu_custom_call" | custom-call | tf_op jit(solution)/shard_map/back/pallas_call | solution.py:462
  84.3 11.7 %all_to_all.23.in_ref = f32[4,128,256]{2,1,0:T(8,128)S(1)} all-to-all(f32[4,128,256]{2,1,0:T(8,128)S(1)} %back.1), channel_id=1, replica_groups=mesh['zhi'=2,'x'=4,'sky'=32] {'x'}, dimensions={0} | all-to-all | bytes 1048576 | tf_op jit(solution)/shard_map/all_to_all | solution.py:512
  96.0 0.7 final.1
  (16 shorter events, 0.0 us)
Async XLA Ops:
  0.6 10.5 %copy-start.12 = (f32[8]{0:T(128)S(1)}, f32[8]{0:T(128)}, u32[]{:S(2)}) copy-start(f32[8]{0:T(128)} %high_ref.3) | copy-start | bytes 100
  0.6 10.5 %copy-start.11 = (f32[8]{0:T(128)S(1)}, f32[8]{0:T(128)}, u32[]{:S(2)}) copy-start(f32[8]{0:T(128)} %low_ref.3) | copy-start | bytes 100
  0.7 10.5 %copy-start.10 = (s32[1,8,256]{2,1,0:T(8,128)S(1)}, s32[1,8,256]{2,1,0:T(8,128)}, u32[]{:S(2)}) copy-start(s32[1,8,256]{2,1,0:T(8,128)} %refine_ref.1) | copy-start | bytes 24580
  1.6 16.9 %collective-permute-start = (bf16[1,64,2048]{2,1,0:T(8,128)(2,1)S(1)}, bf16[1,64,2048]{2,1,0:T(8,128)(2,1)S(1)}, u32[]{:S(2)}, u32[]{:S(2)}) collective-permute-start(bf16[1,64,2048]{2,1,0:T(8,128)(2,1)S(1)} %constant_dynamic-slice_fusion), channel_id=1, source_target_pairs={{32,64},{96,128},{160,192},{64,32},{128,96},{192,160},{33,65},{97,... | collective-permute-start | bytes 786440 | tf_op jit(solution)/shard_map/ppermute | solution.py:494
  2.3 1.6 %copy-start = (bf16[8,64,2048]{2,1,0:T(8,128)(2,1)S(1)}, bf16[8,64,2048]{2,1,0:T(8,128)(2,1)}, u32[]{:S(2)}) copy-start(bf16[8,64,2048]{2,1,0:T(8,128)(2,1)} %d_ref.5) | copy-start | bytes 6291460
  3.9 7.2 %copy-start.1 = (bf16[8,64,2048]{2,1,0:T(8,128)(2,1)S(1)}, bf16[8,64,2048]{2,1,0:T(8,128)(2,1)}, u32[]{:S(2)}) copy-start(bf16[8,64,2048]{2,1,0:T(8,128)(2,1)} %d_ref.5) | copy-start | bytes 6291460
  3.9 14.7 %copy-start.4 = (bf16[8,256,256]{2,1,0:T(8,128)(2,1)S(1)}, bf16[8,256,256]{2,1,0:T(8,128)(2,1)}, u32[]{:S(2)}) copy-start(bf16[8,256,256]{2,1,0:T(8,128)(2,1)} %constant.44.clone.low_table) | copy-start | bytes 3145732
  3.9 14.7 %copy-start.5 = (bf16[8,256,256]{2,1,0:T(8,128)(2,1)S(1)}, bf16[8,256,256]{2,1,0:T(8,128)(2,1)}, u32[]{:S(2)}) copy-start(bf16[8,256,256]{2,1,0:T(8,128)(2,1)} %constant.43.clone.high_table) | copy-start | bytes 3145732
  4.1 14.4 %collective-permute-start.1 = (bf16[1,64,2048]{2,1,0:T(8,128)(2,1)S(1)}, bf16[1,64,2048]{2,1,0:T(8,128)(2,1)S(1)}, u32[]{:S(2)}, u32[]{:S(2)}) collective-permute-start(bf16[1,64,2048]{2,1,0:T(8,128)(2,1)S(1)} %get-tuple-element.11), channel_id=1, source_target_pairs={{0,32},{64,96},{128,160},{192,224},{32,0},{96,64},{160,128},{224,1... | collective-permute-start | bytes 786440 | tf_op jit(solution)/shard_map/ppermute | solution.py:494
  8.7 9.8 %collective-permute-start.2 = (f32[8,2048]{1,0:T(8,128)S(1)}, f32[8,2048]{1,0:T(8,128)S(1)}, u32[]{:S(2)}, u32[]{:S(2)}) collective-permute-start(f32[8,2048]{1,0:T(8,128)S(1)} %get-tuple-element.12), channel_id=1, source_target_pairs={{0,1},{2,3},{4,5},{6,7},{8,9},{10,11},{12,13},{14,15},{16,17},{18,... | collective-permute-start | bytes 196616 | tf_op jit(solution)/shard_map/ppermute | solution.py:494
  9.9 8.6 %collective-permute-start.3 = (f32[8,2048]{1,0:T(8,128)S(1)}, f32[8,2048]{1,0:T(8,128)S(1)}, u32[]{:S(2)}, u32[]{:S(2)}) collective-permute-start(f32[8,2048]{1,0:T(8,128)S(1)} %get-tuple-element.13), channel_id=1, source_target_pairs={{1,2},{3,4},{5,6},{7,8},{9,10},{11,12},{13,14},{15,16},{17,18},{19... | collective-permute-start | bytes 196616 | tf_op jit(solution)/shard_map/ppermute | solution.py:494
  21.0 43.3 %copy-start.6 = (f32[32,8,128]{2,1,0:T(8,128)S(1)}, f32[32,8,128]{2,1,0:T(8,128)}, u32[]{:S(2)}) copy-start(f32[32,8,128]{2,1,0:T(8,128)} %constant.46.clone.sin_ref) | copy-start | bytes 393220
  21.1 43.3 %copy-start.7 = (f32[32,8,128]{2,1,0:T(8,128)S(1)}, f32[32,8,128]{2,1,0:T(8,128)}, u32[]{:S(2)}) copy-start(f32[32,8,128]{2,1,0:T(8,128)} %constant.45.clone.cos_ref) | copy-start | bytes 393220
  21.1 43.3 %copy-start.8 = (bf16[128,256]{1,0:T(8,128)(2,1)S(1)}, bf16[128,256]{1,0:T(8,128)(2,1)}, u32[]{:S(2)}) copy-start(bf16[128,256]{1,0:T(8,128)(2,1)} %constant.48.clone.low_table) | copy-start | bytes 196612
  21.1 43.3 %copy-start.9 = (bf16[128,256]{1,0:T(8,128)(2,1)S(1)}, bf16[128,256]{1,0:T(8,128)(2,1)}, u32[]{:S(2)}) copy-start(bf16[128,256]{1,0:T(8,128)(2,1)} %constant.47.clone.high_table) | copy-start | bytes 196612
  21.1 61.9 %copy-start.2 = (bf16[4,512,256]{2,1,0:T(8,128)(2,1)S(1)}, bf16[4,512,256]{2,1,0:T(8,128)(2,1)}, u32[]{:S(2)}) copy-start(bf16[4,512,256]{2,1,0:T(8,128)(2,1)} %constant.51.clone.low_table) | copy-start | bytes 3145732
  21.1 61.9 %copy-start.3 = (bf16[4,512,256]{2,1,0:T(8,128)(2,1)S(1)}, bf16[4,512,256]{2,1,0:T(8,128)(2,1)}, u32[]{:S(2)}) copy-start(bf16[4,512,256]{2,1,0:T(8,128)(2,1)} %constant.50.clone.high_table) | copy-start | bytes 3145732
  21.1 61.9 %copy-start.13 = (f32[16]{0:T(128)S(1)}, f32[16]{0:T(128)}, u32[]{:S(2)}) copy-start(f32[16]{0:T(128)} %constant.49.clone.eighth_ref) | copy-start | bytes 196

commit v3 on v2

--- a/solution.py
+++ b/solution.py
@@ -230,8 +230,9 @@
     near_ref,
     high_table,
     low_table,
-    out_ref,
+    *rest,
 ):
+    outs, (high_part, low_part) = rest[:4], rest[4:]
     los = lax.axis_index("zhi") * 4 + lax.axis_index("x")
     v0, v1 = d_ref[0].astype(f32), d_ref[1].astype(f32)
     v6, v7 = d_ref[6].astype(f32), d_ref[7].astype(f32)
@@ -293,24 +294,31 @@
 
     for tile in range(8):
         second = sines(tile) if tile else cosines(8)
-        value = jnp.concatenate([cosines(tile), second], axis=1)
-        lanes = 256 * (tile % 2)
-        out_ref[tile // 2, :, lanes : lanes + 256] = dot3(value, high_table[tile], low_table[tile])
+        high_part[tile], low_part[tile] = split(jnp.concatenate([cosines(tile), second], axis=1))
+    dot = functools.partial(jnp.dot, preferred_element_type=f32)
+    for ahead in range(4):
+        target = (lax.axis_index("x") + ahead) % 4
+        for half in range(2):
+            tile = 2 * target + half
+            high, low, table = high_part[tile], low_part[tile], high_table[tile]
+            value = dot(high, table) + (dot(low, table) + dot(high, low_table[tile]))
+            outs[ahead][:, 256 * half : 256 * half + 256] = value
 
 
 def outer_sums(low, high, density, layers, rows, inner, tables):
     return pl.pallas_call(
         outer_kernel,
-        out_shape=jax.ShapeDtypeStruct((4, 72, 512), f32),
+        out_shape=(jax.ShapeDtypeStruct((72, 512), f32),) * 4,
         in_specs=[SM, SM] + [VM] * 13,
-        out_specs=VM,
+        out_specs=(VM,) * 4,
+        scratch_shapes=[pltpu.VMEM((8, 72, 256), bf16)] * 2,
         compiler_params=limit(32),
         name="outer_sums",
     )(low, high, density, *layers, *rows, *inner, *tables)
 
 
-def turn_kernel(in_ref, out_ref):
-    total = (in_ref[0] + in_ref[1]) + (in_ref[2] + in_ref[3])
+def turn_kernel(a_ref, b_ref, c_ref, d_ref, out_ref):
+    total = (a_ref[...] + b_ref[...]) + (c_ref[...] + d_ref[...])
     total = jnp.concatenate([total, jnp.zeros((56, 512), f32)], axis=0)
     out_ref[...] = total.T.reshape(64, 8, 128)
 
@@ -319,11 +327,11 @@
     return pl.pallas_call(
         turn_kernel,
         out_shape=jax.ShapeDtypeStruct((64, 8, 128), f32),
-        in_specs=[VM],
+        in_specs=[VM] * 4,
         out_specs=VM,
         compiler_params=limit(24),
         name="turn",
-    )(pieces)
+    )(*pieces)
 
 
 def dft_32(values):
@@ -438,14 +446,15 @@
     )(pieces, *tables)
 
 
-def back_kernel(eighth_ref, in_ref, high_table, low_table, out_ref):
+def back_kernel(eighth_ref, in_ref, high_table, low_table, *outs):
     zhi, column = lax.axis_index("zhi"), lax.axis_index("x")
     value = in_ref[...]
     sub = lax.broadcasted_iota(jnp.int32, (64, 8, 128), 1)
     bent = pltpu.roll(value, 4, 1) * jnp.where(sub < 4, -1.0, 1.0)
     plain = value.reshape(512, 128).T
     bent = bent.reshape(512, 128).T
-    for target in range(4):
+    for ahead in range(4):
+        target = (column + ahead) % 4
         parts = []
         for half in range(2):
             lanes = slice(256 * half, 256 * half + 256)
@@ -453,7 +462,7 @@
             cosine, sine = eighth_ref[turns], eighth_ref[8 + turns]
             parts.append(cosine * plain[:, lanes] + sine * bent[:, lanes])
         value = jnp.concatenate(parts, axis=1)
-        out_ref[target] = dot3(value, high_table[column], low_table[column])
+        outs[ahead][...] = dot3(value, high_table[column], low_table[column])
 
 
 def back(pieces, tables):
@@ -461,16 +470,16 @@
     eighth = np.concatenate([np.cos(turns), np.sin(turns)]).astype(np.float32)
     return pl.pallas_call(
         back_kernel,
-        out_shape=jax.ShapeDtypeStruct((4, 128, 256), f32),
+        out_shape=(jax.ShapeDtypeStruct((128, 256), f32),) * 4,
         in_specs=[SM, VM, VM, VM],
-        out_specs=VM,
+        out_specs=(VM,) * 4,
         compiler_params=limit(24),
         name="back",
     )(eighth, pieces, *tables)
 
 
-def final_kernel(in_ref, x_ref, y_ref):
-    total = (in_ref[0] + in_ref[1]) + (in_ref[2] + in_ref[3])
+def final_kernel(a_ref, b_ref, c_ref, d_ref, x_ref, y_ref):
+    total = (a_ref[...] + b_ref[...]) + (c_ref[...] + d_ref[...])
     x_ref[...] = total[:ROWS]
     y_ref[...] = total[ROWS:]
 
@@ -480,11 +489,17 @@
     return pl.pallas_call(
         final_kernel,
         out_shape=(shape, shape),
-        in_specs=[VM],
+        in_specs=[VM] * 4,
         out_specs=(VM, VM),
         compiler_params=limit(24),
         name="final",
-    )(pieces)
+    )(*pieces)
+
+
+def deliver(pieces):
+    return [pieces[0]] + [
+        lax.ppermute(pieces[a], "x", [(i, (i + a) % 4) for i in range(4)]) for a in (1, 2, 3)
+    ]
 
 
 def body(density, refine, weight_low, weight_high):
@@ -504,13 +519,12 @@
     summed = outer_sums(
         weight_low, weight_high, density, (layer, other_layer), (row, other_row), inner, tables
     )
-    summed = lax.all_to_all(summed, "x", 0, 0, tiled=True)
+    summed = deliver(summed)
     pieces = lax.all_to_all(turn(summed), ("zhi", "sky"), 0, 0, tiled=True)
     pieces = solve(pieces, twists() + halves(row_table()))
     pieces = lax.all_to_all(pieces, ("zhi", "sky"), 0, 0, tiled=True)
     fields = back(pieces, halves(inverse_table()))
-    fields = lax.all_to_all(fields, "x", 0, 0, tiled=True)
-    return final(fields)
+    return final(deliver(fields))
 
 
 def solution(mesh):

time: 97 us -> 92.6 us (0.955)
  blocking collectives: 72.4 us -> 44.5 us
  starting transfers between devices: 7.67 us -> 21.2 us
  waiting for transfers between devices: 0.01 us -> 9.87 us
    all_to_all x2 -> x0, blocking collectives: 28.3 us -> none  [the longest x1 16.6 us: body(): summed = lax.all_to_all(summed, 'x', 0, 0, tiled=True)]
    ppermute x0 -> x6, starting transfers between devices: none -> 13.5 us  [deliver(): lax.ppermute(pieces[a], 'x', [(i, (i + a) % 4) for i in range(4)])]
    ppermute x0 -> x6, waiting for transfers between devices: none -> 9.86 us  [deliver(): lax.ppermute(pieces[a], 'x', [(i, (i + a) % 4) for i in range(4)])]
  transfers between devices with their start and end apart: 4 -> 10, of which waited for: 0 -> 4; matrix products, arithmetic and copies ran while one was open for 0% -> 0% of each run, Pallas kernels for 8% -> 8%
where the time goes in v3:
time: 92.6 us; the launch traced here: 92.4 us
  blocking collectives  44.5 us (48%)
  starting transfers between devices  21.2 us (23%)
  Pallas kernels  13.3 us (14%)
  waiting for transfers between devices  9.87 us (11%)
  local copies, waits for them, and re-layouts  2.63 us (3%)
    all_to_all x1, blocking collectives, body(): pieces = lax.all_to_all(turn(summed), ('zhi', 'sky'), 0, 0, tiled=True)  26.9 us
    all_to_all x1, blocking collectives, body(): pieces = lax.all_to_all(pieces, ('zhi', 'sky'), 0, 0, tiled=True)  17.7 us
    ppermute x6, starting transfers between devices, deliver(): lax.ppermute(pieces[a], 'x', [(i, (i + a) % 4) for i in range(4)])  13.5 us
    ppermute x6, waiting for transfers between devices, deliver(): lax.ppermute(pieces[a], 'x', [(i, (i + a) % 4) for i in range(4)])  9.86 us
    ppermute x4, starting transfers between devices, swap(): return lax.ppermute(array, axes, pairs + [(b, a) for a, b in pairs])  7.67 us
    pallas_call x1, Pallas kernels, inner_sums(): pl.pallas_call(inner_kernel, out_shape=(field, field, field, field, jax.S...  7.4 us
    pallas_call x1, Pallas kernels, outer_sums(): pl.pallas_call(outer_kernel, out_shape=(jax.ShapeDtypeStruct((72, 512), f...  2.66 us
  transfers between devices with their start and end apart: 10, of which 4 were waited for; matrix products, arithmetic and copies ran while one was open for 0% of the time, Pallas kernels for 8%

profile of v3, /device:TPU:1, one launch (start us, length us, event | category | flops | bytes accessed | tf_op | source)
XLA Modules:
  0.0 92.4 jit_solution(5872309361291415778)
XLA Ops:
  0.7 1.0 %constant_dynamic-slice_fusion = bf16[1,64,2048]{2,1,0:T(8,128)(2,1)S(1)} fusion(bf16[8,64,2048]{2,1,0:T(8,128)(2,1)} %d_ref.5, s32[]{:T(128)S(6)} %select_n.13), kind=kLoop, calls=%fused_computation | loop fusion | bytes 524292 | tf_op jit(solution)/shard_map/dynamic_slice | solution.py:511
  1.6 0.7 collective-permute-start
  2.3 0.0 copy-start
  2.3 1.6 %copy-done = bf16[8,64,2048]{2,1,0:T(8,128)(2,1)S(1)} copy-done((bf16[8,64,2048]{2,1,0:T(8,128)(2,1)S(1)}, bf16[8,64,2048]{2,1,0:T(8,128)(2,1)}, u32[]{:S(2)}) %copy-start) | copy-done | bytes 2097176
  3.9 0.2 edge_rows.1
  4.1 4.6 %collective-permute-start.1 = (bf16[1,64,2048]{2,1,0:T(8,128)(2,1)S(1)}, bf16[1,64,2048]{2,1,0:T(8,128)(2,1)S(1)}, u32[]{:S(2)}, u32[]{:S(2)}) collective-permute-start(bf16[1,64,2048]{2,1,0:T(8,128)(2,1)S(1)} %get-tuple-element.19), channel_id=1, source_target_pairs={{0,32},{64,96},{128,160},{192,224},{32,0},{96,64},{160,128},{224,1... | collective-permute-start | bytes 786440 | tf_op jit(solution)/shard_map/ppermute | solution.py:509
  8.7 1.2 %collective-permute-start.2 = (f32[8,2048]{1,0:T(8,128)S(1)}, f32[8,2048]{1,0:T(8,128)S(1)}, u32[]{:S(2)}, u32[]{:S(2)}) collective-permute-start(f32[8,2048]{1,0:T(8,128)S(1)} %get-tuple-element.20), channel_id=1, source_target_pairs={{0,1},{2,3},{4,5},{6,7},{8,9},{10,11},{12,13},{14,15},{16,17},{18,... | collective-permute-start | bytes 196616 | tf_op jit(solution)/shard_map/ppermute | solution.py:509
  9.9 1.2 %collective-permute-start.3 = (f32[8,2048]{1,0:T(8,128)S(1)}, f32[8,2048]{1,0:T(8,128)S(1)}, u32[]{:S(2)}, u32[]{:S(2)}) collective-permute-start(f32[8,2048]{1,0:T(8,128)S(1)} %get-tuple-element.21), channel_id=1, source_target_pairs={{1,2},{3,4},{5,6},{7,8},{9,10},{11,12},{13,14},{15,16},{17,18},{19... | collective-permute-start | bytes 196616 | tf_op jit(solution)/shard_map/ppermute | solution.py:509
  11.1 7.4 %inner_sums.1 = (f32[64,2048]{1,0:T(8,128)S(1)}, f32[64,2048]{1,0:T(8,128)S(1)}, f32[64,2048]{1,0:T(8,128)S(1)}, f32[64,2048]{1,0:T(8,128)S(1)}, f32[8,2048]{1,0:T(8,128)S(1)}, /*index=5*/f32[4,8,2048]{2,1,0:T(8,128)S(1)}) custom-call(f32[8]{0:T(128)S(1)} %copy-done.11, f32[8]{0:T(128)S(1)} %copy-done.12, bf16[8,64,2048]{2,1,0:T(8,128)(2,1)S(1)} %copy-done.1, ...), custom_call_target="tpu_custom_call" | custom-call | flops 40000000 | bytes 25165824 | tf_op jit(solution)/shard_map/inner_sums/pallas_call | solution.py:199
  18.5 0.0 collective-permute-done.2.row_ref
  18.6 0.0 copy-start.6
  18.6 0.0 copy-start.7
  18.6 0.0 copy-start.8
  18.6 0.0 copy-start.9
  18.7 2.7 %outer_sums.1 = (f32[72,512]{1,0:T(8,128)S(1)}, f32[72,512]{1,0:T(8,128)S(1)}, f32[72,512]{1,0:T(8,128)S(1)}, f32[72,512]{1,0:T(8,128)S(1)}) custom-call(f32[8]{0:T(128)S(1)} %copy-done.11, f32[8]{0:T(128)S(1)} %copy-done.12, bf16[8,64,2048]{2,1,0:T(8,128)(2,1)S(1)} %copy-done.1, bf16[1,64,2048]{2,1,0:T(8,128)(2,1)S(1)} %collective-permute-done.layer_ref, ...), custom_call_target="tpu_custom_call" | custom-call | tf_op jit(solution)/shard_map/outer_sums/pallas_call | solution.py:309
  21.3 0.0 copy-start.3
  21.3 0.0 copy-start.13
  21.4 0.1 collective-permute-start.4
  21.4 8.2 %collective-permute-start.5 = (f32[72,512]{1,0:T(8,128)S(1)}, f32[72,512]{1,0:T(8,128)S(1)}, u32[]{:S(2)}, u32[]{:S(2)}) collective-permute-start(f32[72,512]{1,0:T(8,128)S(1)} %get-tuple-element.30), channel_id=1, source_target_pairs={{0,64},{32,96},{64,0},{96,32},{1,65},{33,97},{65,1},{97,33},{2,66}... | collective-permute-start | bytes 442376 | tf_op jit(solution)/shard_map/ppermute | solution.py:501
  29.6 2.0 %collective-permute-start.6 = (f32[72,512]{1,0:T(8,128)S(1)}, f32[72,512]{1,0:T(8,128)S(1)}, u32[]{:S(2)}, u32[]{:S(2)}) collective-permute-start(f32[72,512]{1,0:T(8,128)S(1)} %get-tuple-element.31), channel_id=1, source_target_pairs={{0,96},{32,0},{64,32},{96,64},{1,97},{33,1},{65,33},{97,65},{2,98}... | collective-permute-start | bytes 442376 | tf_op jit(solution)/shard_map/ppermute | solution.py:501
  31.6 2.1 %collective-permute-done.5.c_ref = f32[72,512]{1,0:T(8,128)S(1)} collective-permute-done((f32[72,512]{1,0:T(8,128)S(1)}, f32[72,512]{1,0:T(8,128)S(1)}, u32[]{:S(2)}, u32[]{:S(2)}) %collective-permute-start.5) | collective-permute-done | bytes 147488 | tf_op jit(solution)/shard_map/ppermute | solution.py:501
  33.7 1.5 %collective-permute-done.6.d_ref = f32[72,512]{1,0:T(8,128)S(1)} collective-permute-done((f32[72,512]{1,0:T(8,128)S(1)}, f32[72,512]{1,0:T(8,128)S(1)}, u32[]{:S(2)}, u32[]{:S(2)}) %collective-permute-start.6) | collective-permute-done | bytes 147488 | tf_op jit(solution)/shard_map/ppermute | solution.py:501
  35.2 0.1 turn.1
  35.4 26.9 %all_to_all.10.in_ref = f32[64,8,128]{2,1,0:T(8,128)S(1)} all-to-all(f32[64,8,128]{2,1,0:T(8,128)S(1)} %turn.1), channel_id=1, replica_groups=mesh['zhi'=2,'x'=4,'sky'=32] {'zhi','sky'}, dimensions={0} | all-to-all | bytes 524288 | tf_op jit(solution)/shard_map/all_to_all | solution.py:523
  62.2 1.0 %solve.1 = f32[64,8,128]{2,1,0:T(8,128)S(1)} custom-call(f32[64,8,128]{2,1,0:T(8,128)S(1)} %all_to_all.10.in_ref, f32[32,8,128]{2,1,0:T(8,128)S(1)} %copy-done.7, f32[32,8,128]{2,1,0:T(8,128)S(1)} %copy-done.6, bf16[128,256]{1,0:T(8,128)(2,1)S(1)} %copy-done.9, bf16[128,256]{1,0:T(8,128)(2,1)S(1)} %copy-done.8), custom_call_target="tpu_custom_call" | custom-call | tf_op jit(solution)/shard_map/solve/pallas_call | solution.py:439
  63.2 17.7 %all_to_all.11.in_ref = f32[64,8,128]{2,1,0:T(8,128)S(1)} all-to-all(f32[64,8,128]{2,1,0:T(8,128)S(1)} %solve.1), channel_id=1, replica_groups=mesh['zhi'=2,'x'=4,'sky'=32] {'zhi','sky'}, dimensions={0} | all-to-all | bytes 524288 | tf_op jit(solution)/shard_map/all_to_all | solution.py:525
  80.9 1.3 %back.1 = (f32[128,256]{1,0:T(8,128)S(1)}, f32[128,256]{1,0:T(8,128)S(1)}, f32[128,256]{1,0:T(8,128)S(1)}, f32[128,256]{1,0:T(8,128)S(1)}) custom-call(f32[16]{0:T(128)S(1)} %copy-done.13, f32[64,8,128]{2,1,0:T(8,128)S(1)} %all_to_all.11.in_ref, bf16[4,512,256]{2,1,0:T(8,128)(2,1)S(1)} %copy-done.3, bf16[4,512,256]{2,1,0:T(8,128)(2,1)S(1)} %copy-done.2), custom_call_target="tpu_custom_call" | custom-call | tf_op jit(solution)/shard_map/back/pallas_call | solution.py:471
  82.2 0.1 collective-permute-start.7
  82.3 3.2 %collective-permute-start.8 = (f32[128,256]{1,0:T(8,128)S(1)}, f32[128,256]{1,0:T(8,128)S(1)}, u32[]{:S(2)}, u32[]{:S(2)}) collective-permute-start(f32[128,256]{1,0:T(8,128)S(1)} %get-tuple-element.34), channel_id=1, source_target_pairs={{0,64},{32,96},{64,0},{96,32},{1,65},{33,97},{65,1},{97,33},{2,66}... | collective-permute-start | bytes 393224 | tf_op jit(solution)/shard_map/ppermute | solution.py:501
  85.6 2.8 %collective-permute-done.7.b_ref = f32[128,256]{1,0:T(8,128)S(1)} collective-permute-done((f32[128,256]{1,0:T(8,128)S(1)}, f32[128,256]{1,0:T(8,128)S(1)}, u32[]{:S(2)}, u32[]{:S(2)}) %collective-permute-start.7) | collective-permute-done | bytes 131104 | tf_op jit(solution)/shard_map/ppermute | solution.py:501
  88.4 3.4 %collective-permute-done.8.c_ref = f32[128,256]{1,0:T(8,128)S(1)} collective-permute-done((f32[128,256]{1,0:T(8,128)S(1)}, f32[128,256]{1,0:T(8,128)S(1)}, u32[]{:S(2)}, u32[]{:S(2)}) %collective-permute-start.8) | collective-permute-done | bytes 131104 | tf_op jit(solution)/shard_map/ppermute | solution.py:501
  91.7 0.7 final.1
  (26 shorter events, 0.1 us)
Async XLA Ops:
  0.6 10.5 %copy-start.12 = (f32[8]{0:T(128)S(1)}, f32[8]{0:T(128)}, u32[]{:S(2)}) copy-start(f32[8]{0:T(128)} %high_ref.3) | copy-start | bytes 100
  0.6 10.5 %copy-start.11 = (f32[8]{0:T(128)S(1)}, f32[8]{0:T(128)}, u32[]{:S(2)}) copy-start(f32[8]{0:T(128)} %low_ref.3) | copy-start | bytes 100
  0.7 10.5 %copy-start.10 = (s32[1,8,256]{2,1,0:T(8,128)S(1)}, s32[1,8,256]{2,1,0:T(8,128)}, u32[]{:S(2)}) copy-start(s32[1,8,256]{2,1,0:T(8,128)} %refine_ref.1) | copy-start | bytes 24580
  1.6 16.9 %collective-permute-start = (bf16[1,64,2048]{2,1,0:T(8,128)(2,1)S(1)}, bf16[1,64,2048]{2,1,0:T(8,128)(2,1)S(1)}, u32[]{:S(2)}, u32[]{:S(2)}) collective-permute-start(bf16[1,64,2048]{2,1,0:T(8,128)(2,1)S(1)} %constant_dynamic-slice_fusion), channel_id=1, source_target_pairs={{32,64},{96,128},{160,192},{64,32},{128,96},{192,160},{33,65},{97,... | collective-permute-start | bytes 786440 | tf_op jit(solution)/shard_map/ppermute | solution.py:509
  2.3 1.6 %copy-start = (bf16[8,64,2048]{2,1,0:T(8,128)(2,1)S(1)}, bf16[8,64,2048]{2,1,0:T(8,128)(2,1)}, u32[]{:S(2)}) copy-start(bf16[8,64,2048]{2,1,0:T(8,128)(2,1)} %d_ref.5) | copy-start | bytes 6291460
  3.9 7.2 %copy-start.1 = (bf16[8,64,2048]{2,1,0:T(8,128)(2,1)S(1)}, bf16[8,64,2048]{2,1,0:T(8,128)(2,1)}, u32[]{:S(2)}) copy-start(bf16[8,64,2048]{2,1,0:T(8,128)(2,1)} %d_ref.5) | copy-start | bytes 6291460
  3.9 14.7 %copy-start.4 = (bf16[8,256,256]{2,1,0:T(8,128)(2,1)S(1)}, bf16[8,256,256]{2,1,0:T(8,128)(2,1)}, u32[]{:S(2)}) copy-start(bf16[8,256,256]{2,1,0:T(8,128)(2,1)} %constant.44.clone.low_table) | copy-start | bytes 3145732
  3.9 14.7 %copy-start.5 = (bf16[8,256,256]{2,1,0:T(8,128)(2,1)S(1)}, bf16[8,256,256]{2,1,0:T(8,128)(2,1)}, u32[]{:S(2)}) copy-start(bf16[8,256,256]{2,1,0:T(8,128)(2,1)} %constant.43.clone.high_table) | copy-start | bytes 3145732
  4.1 14.4 %collective-permute-start.1 = (bf16[1,64,2048]{2,1,0:T(8,128)(2,1)S(1)}, bf16[1,64,2048]{2,1,0:T(8,128)(2,1)S(1)}, u32[]{:S(2)}, u32[]{:S(2)}) collective-permute-start(bf16[1,64,2048]{2,1,0:T(8,128)(2,1)S(1)} %get-tuple-element.19), channel_id=1, source_target_pairs={{0,32},{64,96},{128,160},{192,224},{32,0},{96,64},{160,128},{224,1... | collective-permute-start | bytes 786440 | tf_op jit(solution)/shard_map/ppermute | solution.py:509
  8.7 9.8 %collective-permute-start.2 = (f32[8,2048]{1,0:T(8,128)S(1)}, f32[8,2048]{1,0:T(8,128)S(1)}, u32[]{:S(2)}, u32[]{:S(2)}) collective-permute-start(f32[8,2048]{1,0:T(8,128)S(1)} %get-tuple-element.20), channel_id=1, source_target_pairs={{0,1},{2,3},{4,5},{6,7},{8,9},{10,11},{12,13},{14,15},{16,17},{18,... | collective-permute-start | bytes 196616 | tf_op jit(solution)/shard_map/ppermute | solution.py:509
  9.9 8.6 %collective-permute-start.3 = (f32[8,2048]{1,0:T(8,128)S(1)}, f32[8,2048]{1,0:T(8,128)S(1)}, u32[]{:S(2)}, u32[]{:S(2)}) collective-permute-start(f32[8,2048]{1,0:T(8,128)S(1)} %get-tuple-element.21), channel_id=1, source_target_pairs={{1,2},{3,4},{5,6},{7,8},{9,10},{11,12},{13,14},{15,16},{17,18},{19... | collective-permute-start | bytes 196616 | tf_op jit(solution)/shard_map/ppermute | solution.py:509
  18.6 43.6 %copy-start.6 = (f32[32,8,128]{2,1,0:T(8,128)S(1)}, f32[32,8,128]{2,1,0:T(8,128)}, u32[]{:S(2)}) copy-start(f32[32,8,128]{2,1,0:T(8,128)} %constant.46.clone.sin_ref) | copy-start | bytes 393220
  18.6 43.6 %copy-start.7 = (f32[32,8,128]{2,1,0:T(8,128)S(1)}, f32[32,8,128]{2,1,0:T(8,128)}, u32[]{:S(2)}) copy-start(f32[32,8,128]{2,1,0:T(8,128)} %constant.45.clone.cos_ref) | copy-start | bytes 393220
  18.6 43.6 %copy-start.8 = (bf16[128,256]{1,0:T(8,128)(2,1)S(1)}, bf16[128,256]{1,0:T(8,128)(2,1)}, u32[]{:S(2)}) copy-start(bf16[128,256]{1,0:T(8,128)(2,1)} %constant.48.clone.low_table) | copy-start | bytes 196612
  18.6 43.6 %copy-start.9 = (bf16[128,256]{1,0:T(8,128)(2,1)S(1)}, bf16[128,256]{1,0:T(8,128)(2,1)}, u32[]{:S(2)}) copy-start(bf16[128,256]{1,0:T(8,128)(2,1)} %constant.47.clone.high_table) | copy-start | bytes 196612
  21.3 59.6 %copy-start.2 = (bf16[4,512,256]{2,1,0:T(8,128)(2,1)S(1)}, bf16[4,512,256]{2,1,0:T(8,128)(2,1)}, u32[]{:S(2)}) copy-start(bf16[4,512,256]{2,1,0:T(8,128)(2,1)} %constant.51.clone.low_table) | copy-start | bytes 3145732
  21.3 59.6 %copy-start.3 = (bf16[4,512,256]{2,1,0:T(8,128)(2,1)S(1)}, bf16[4,512,256]{2,1,0:T(8,128)(2,1)}, u32[]{:S(2)}) copy-start(bf16[4,512,256]{2,1,0:T(8,128)(2,1)} %constant.50.clone.high_table) | copy-start | bytes 3145732
  21.3 59.6 %copy-start.13 = (f32[16]{0:T(128)S(1)}, f32[16]{0:T(128)}, u32[]{:S(2)}) copy-start(f32[16]{0:T(128)} %constant.49.clone.eighth_ref) | copy-start | bytes 196
  21.4 10.2 %collective-permute-start.4 = (f32[72,512]{1,0:T(8,128)S(1)}, f32[72,512]{1,0:T(8,128)S(1)}, u32[]{:S(2)}, u32[]{:S(2)}) collective-permute-start(f32[72,512]{1,0:T(8,128)S(1)} %get-tuple-element.29), channel_id=1, source_target_pairs={{0,32},{32,64},{64,96},{96,0},{1,33},{33,65},{65,97},{97,1},{2,34}... | collective-permute-start | bytes 442376 | tf_op jit(solution)/shard_map/ppermute | solution.py:501
  21.4 12.3 %collective-permute-start.5 = (f32[72,512]{1,0:T(8,128)S(1)}, f32[72,512]{1,0:T(8,128)S(1)}, u32[]{:S(2)}, u32[]{:S(2)}) collective-permute-start(f32[72,512]{1,0:T(8,128)S(1)} %get-tuple-element.30), channel_id=1, source_target_pairs={{0,64},{32,96},{64,0},{96,32},{1,65},{33,97},{65,1},{97,33},{2,66}... | collective-permute-start | bytes 442376 | tf_op jit(solution)/shard_map/ppermute | solution.py:501
  29.6 5.6 %collective-permute-start.6 = (f32[72,512]{1,0:T(8,128)S(1)}, f32[72,512]{1,0:T(8,128)S(1)}, u32[]{:S(2)}, u32[]{:S(2)}) collective-permute-start(f32[72,512]{1,0:T(8,128)S(1)} %get-tuple-element.31), channel_id=1, source_target_pairs={{0,96},{32,0},{64,32},{96,64},{1,97},{33,1},{65,33},{97,65},{2,98}... | collective-permute-start | bytes 442376 | tf_op jit(solution)/shard_map/ppermute | solution.py:501
  82.2 6.1 %collective-permute-start.7 = (f32[128,256]{1,0:T(8,128)S(1)}, f32[128,256]{1,0:T(8,128)S(1)}, u32[]{:S(2)}, u32[]{:S(2)}) collective-permute-start(f32[128,256]{1,0:T(8,128)S(1)} %get-tuple-element.33), channel_id=1, source_target_pairs={{0,32},{32,64},{64,96},{96,0},{1,33},{33,65},{65,97},{97,1},{2,34}... | collective-permute-start | bytes 393224 | tf_op jit(solution)/shard_map/ppermute | solution.py:501
  82.3 9.4 %collective-permute-start.8 = (f32[128,256]{1,0:T(8,128)S(1)}, f32[128,256]{1,0:T(8,128)S(1)}, u32[]{:S(2)}, u32[]{:S(2)}) collective-permute-start(f32[128,256]{1,0:T(8,128)S(1)} %get-tuple-element.34), channel_id=1, source_target_pairs={{0,64},{32,96},{64,0},{96,32},{1,65},{33,97},{65,1},{97,33},{2,66}... | collective-permute-start | bytes 393224 | tf_op jit(solution)/shard_map/ppermute | solution.py:501
  85.5 6.2 %collective-permute-start.9 = (f32[128,256]{1,0:T(8,128)S(1)}, f32[128,256]{1,0:T(8,128)S(1)}, u32[]{:S(2)}, u32[]{:S(2)}) collective-permute-start(f32[128,256]{1,0:T(8,128)S(1)} %get-tuple-element.35), channel_id=1, source_target_pairs={{0,96},{32,0},{64,32},{96,64},{1,97},{33,1},{65,33},{97,65},{2,98}... | collective-permute-start | bytes 393224 | tf_op jit(solution)/shard_map/ppermute | solution.py:501

commit v4 on v3

--- a/solution.py
+++ b/solution.py
@@ -128,11 +128,29 @@
     )(density)
 
 
+def longer(field):
+    return jnp.concatenate([field, jnp.zeros((8, N), f32)], axis=0)
+
+
+def smooth_y(field):
+    return 0.75 * field + 0.125 * (pltpu.roll(field, 1, 1) + pltpu.roll(field, N - 1, 1))
+
+
 CHUNK = 512
 
 
 def inner_kernel(
-    low_ref, high_ref, d_ref, refine_ref, calm_ref, lifted_ref, tx_ref, ty_ref, mask_ref, near_ref
+    low_ref,
+    high_ref,
+    d_ref,
+    refine_ref,
+    kappa_ref,
+    mask_ref,
+    near_ref,
+    calm_ref,
+    lifted_ref,
+    tx_ref,
+    ty_ref,
 ):
     block = lax.broadcasted_iota(jnp.int32, (256, N), 0)
     lane = lax.broadcasted_iota(jnp.int32, (256, N), 1)
@@ -192,22 +210,28 @@
         return carry
 
     lax.fori_loop(0, N // CHUNK, chunk, 0)
+    lifted, tx = lifted_ref[...], tx_ref[...]
+    eighth, tilt = 0.125 * lifted, ty_ref[...] * (1.0 / 32.0)
+    smooth = 0.75 * lifted + pltpu.roll(eighth + tilt, 1, 1) + pltpu.roll(eighth - tilt, N - 1, 1)
+    eighth, tilt = 0.125 * smooth, smooth_y(tx) * (1.0 / 32.0)
+    kappa_ref[...] = (
+        longer(calm_ref[...] + 0.75 * smooth)
+        + pltpu.roll(longer(eighth + tilt), 1, 0)
+        + pltpu.roll(longer(eighth - tilt), ROWS + 7, 0)
+    )
 
 
 def inner_sums(low, high, density, refine):
-    field = jax.ShapeDtypeStruct((ROWS, N), f32)
     return pl.pallas_call(
         inner_kernel,
         out_shape=(
-            field,
-            field,
-            field,
-            field,
+            jax.ShapeDtypeStruct((ROWS + 8, N), f32),
             jax.ShapeDtypeStruct((8, N), f32),
             jax.ShapeDtypeStruct((4, LAYERS, N), f32),
         ),
         in_specs=[SM, SM, VM, VM],
-        out_specs=(VM,) * 6,
+        out_specs=(VM,) * 3,
+        scratch_shapes=[pltpu.VMEM((ROWS, N), f32)] * 4,
         compiler_params=limit(40),
         cost_estimate=pl.CostEstimate(flops=40_000_000, bytes_accessed=24 * MB, transcendentals=0),
         name="inner_sums",
@@ -222,10 +246,7 @@
     other_layer_ref,
     row_ref,
     other_row_ref,
-    calm_ref,
-    lifted_ref,
-    tx_ref,
-    ty_ref,
+    kappa_ref,
     mask_ref,
     near_ref,
     high_table,
@@ -245,7 +266,7 @@
     tz = slope0 * minmod(v1 - v0, v0 - below) + slope7 * minmod(above - v7, v7 - v6)
     mask = mask_ref[...]
     marked = jnp.broadcast_to(mask[:, None, :], (8, 8, N)).reshape(ROWS, N)
-    lifted = lifted_ref[...] + marked * tz
+    smooth = smooth_y(marked * tz)
     layer = lax.broadcasted_iota(jnp.int32, (LAYERS, 1), 0)
     average = jnp.zeros((LAYERS, 1), f32)
     for z in range(LAYERS):
@@ -256,21 +277,18 @@
     after = jnp.where(even, row_ref[...], other_row_ref[...])
     e0 = jnp.sum(average * minmod(r1 - r0, r0 - before), axis=0, keepdims=True)
     e63 = jnp.sum(average * minmod(after - r63, r63 - r62), axis=0, keepdims=True)
-    row = lax.broadcasted_iota(jnp.int32, (ROWS, N), 0)
-    tx = jnp.where(row == 0, mask[0:1] * e0, jnp.where(row == ROWS - 1, mask[7:8] * e63, tx_ref[...]))
-    eighth, tilt = 0.125 * lifted, ty_ref[...] * (1.0 / 32.0)
-    smooth = 0.75 * lifted + pltpu.roll(eighth + tilt, 1, 1) + pltpu.roll(eighth - tilt, N - 1, 1)
-    sloped = 0.75 * tx + 0.125 * (pltpu.roll(tx, 1, 1) + pltpu.roll(tx, N - 1, 1))
-    eighth, tilt = 0.125 * smooth, sloped * (1.0 / 32.0)
-    none = jnp.zeros((8, N), f32)
-
-    def longer(field):
-        return jnp.concatenate([field, none], axis=0)
-
+    row = lax.broadcasted_iota(jnp.int32, (8, N), 0)
+    e0 = smooth_y(jnp.where(row == 0, mask[0:1] * e0, 0.0)) * (1.0 / 32.0)
+    e63 = smooth_y(jnp.where(row == 7, mask[7:8] * e63, 0.0)) * (1.0 / 32.0)
+    first = pltpu.roll(e0, 1, 0)
+    last = pltpu.roll(e63, 7, 0)
+    spill = jnp.where(row == 0, pltpu.roll(e63, 1, 0), -pltpu.roll(e0, 7, 0))
+    sides = jnp.concatenate([first, jnp.zeros((ROWS - 16, N), f32), -last, spill], axis=0)
+    eighth = longer(0.125 * smooth)
     kappa = (
-        longer(calm_ref[...] + 0.75 * smooth)
-        + pltpu.roll(longer(eighth + tilt), 1, 0)
-        + pltpu.roll(longer(eighth - tilt), ROWS + 7, 0)
+        (kappa_ref[...] + sides)
+        + longer(0.75 * smooth)
+        + (pltpu.roll(eighth, 1, 0) + pltpu.roll(eighth, ROWS + 7, 0))
     )
     part = [kappa[:, 128 * a : 128 * a + 128] for a in range(16)]
     even = [part[a] + part[16 - a] for a in range(1, 8)]
@@ -309,7 +327,7 @@
     return pl.pallas_call(
         outer_kernel,
         out_shape=(jax.ShapeDtypeStruct((72, 512), f32),) * 4,
-        in_specs=[SM, SM] + [VM] * 13,
+        in_specs=[SM, SM] + [VM] * 10,
         out_specs=(VM,) * 4,
         scratch_shapes=[pltpu.VMEM((8, 72, 256), bf16)] * 2,
         compiler_params=limit(32),
@@ -503,11 +521,10 @@
 
 
 def body(density, refine, weight_low, weight_high):
-    odd = lax.axis_index("x") % 2 == 1
-
     def swap(array, axes, pairs):
         return lax.ppermute(array, axes, pairs + [(b, a) for a, b in pairs])
 
+    odd = lax.axis_index("x") % 2 == 1
     layer = lax.dynamic_slice_in_dim(density, jnp.where(odd, LAYERS - 1, 0), 1, 0)
     layer = swap(layer, LOS, [(1, 2), (3, 4), (5, 6)])
     row, other_row, other_layer = edge_rows(density)

time: 92.6 us -> 92.4 us (level)
  transfers between devices with their start and end apart: 10 -> 10, of which waited for: 4 -> 4; matrix products, arithmetic and copies ran while one was open for 0% -> 0% of each run, Pallas kernels for 8% -> 9%
where the time goes in v4:
time: 92.4 us; the launch traced here: 92.2 us
  blocking collectives  43.7 us (47%)
  starting transfers between devices  21.2 us (23%)
  Pallas kernels  13.9 us (15%)
  waiting for transfers between devices  9.86 us (11%)
  local copies, waits for them, and re-layouts  2.63 us (3%)
    all_to_all x1, blocking collectives, body(): pieces = lax.all_to_all(turn(summed), ('zhi', 'sky'), 0, 0, tiled=True)  26 us
    all_to_all x1, blocking collectives, body(): pieces = lax.all_to_all(pieces, ('zhi', 'sky'), 0, 0, tiled=True)  17.7 us
    ppermute x6, starting transfers between devices, deliver(): lax.ppermute(pieces[a], 'x', [(i, (i + a) % 4) for i in range(4)])  13.5 us
    ppermute x6, waiting for transfers between devices, deliver(): lax.ppermute(pieces[a], 'x', [(i, (i + a) % 4) for i in range(4)])  9.85 us
    pallas_call x1, Pallas kernels, inner_sums(): pl.pallas_call(inner_kernel, out_shape=(jax.ShapeDtypeStruct((ROWS + 8, N...  8.23 us
    ppermute x4, starting transfers between devices, swap(): return lax.ppermute(array, axes, pairs + [(b, a) for a, b in pairs])  7.67 us
    pallas_call x1, Pallas kernels, outer_sums(): pl.pallas_call(outer_kernel, out_shape=(jax.ShapeDtypeStruct((72, 512), f...  2.4 us
  transfers between devices with their start and end apart: 10, of which 4 were waited for; matrix products, arithmetic and copies ran while one was open for 0% of the time, Pallas kernels for 9%

profile of v4, /device:TPU:1, one launch (start us, length us, event | category | flops | bytes accessed | tf_op | source)
XLA Modules:
  0.0 92.2 jit_solution(17703664330545225969)
XLA Ops:
  0.7 1.0 %constant_dynamic-slice_fusion = bf16[1,64,2048]{2,1,0:T(8,128)(2,1)S(1)} fusion(bf16[8,64,2048]{2,1,0:T(8,128)(2,1)} %d_ref.5, s32[]{:T(128)S(6)} %select_n.13), kind=kLoop, calls=%fused_computation | loop fusion | bytes 524292 | tf_op jit(solution)/shard_map/dynamic_slice | solution.py:528
  1.6 0.7 collective-permute-start
  2.3 0.0 copy-start
  2.3 1.6 %copy-done = bf16[8,64,2048]{2,1,0:T(8,128)(2,1)S(1)} copy-done((bf16[8,64,2048]{2,1,0:T(8,128)(2,1)S(1)}, bf16[8,64,2048]{2,1,0:T(8,128)(2,1)}, u32[]{:S(2)}) %copy-start) | copy-done | bytes 2097176
  3.9 0.2 edge_rows.1
  4.1 4.6 %collective-permute-start.1 = (bf16[1,64,2048]{2,1,0:T(8,128)(2,1)S(1)}, bf16[1,64,2048]{2,1,0:T(8,128)(2,1)S(1)}, u32[]{:S(2)}, u32[]{:S(2)}) collective-permute-start(bf16[1,64,2048]{2,1,0:T(8,128)(2,1)S(1)} %get-tuple-element.16), channel_id=1, source_target_pairs={{0,32},{64,96},{128,160},{192,224},{32,0},{96,64},{160,128},{224,1... | collective-permute-start | bytes 786440 | tf_op jit(solution)/shard_map/ppermute | solution.py:525
  8.7 1.2 %collective-permute-start.2 = (f32[8,2048]{1,0:T(8,128)S(1)}, f32[8,2048]{1,0:T(8,128)S(1)}, u32[]{:S(2)}, u32[]{:S(2)}) collective-permute-start(f32[8,2048]{1,0:T(8,128)S(1)} %get-tuple-element.17), channel_id=1, source_target_pairs={{0,1},{2,3},{4,5},{6,7},{8,9},{10,11},{12,13},{14,15},{16,17},{18,... | collective-permute-start | bytes 196616 | tf_op jit(solution)/shard_map/ppermute | solution.py:525
  9.9 1.2 %collective-permute-start.3 = (f32[8,2048]{1,0:T(8,128)S(1)}, f32[8,2048]{1,0:T(8,128)S(1)}, u32[]{:S(2)}, u32[]{:S(2)}) collective-permute-start(f32[8,2048]{1,0:T(8,128)S(1)} %get-tuple-element.18), channel_id=1, source_target_pairs={{1,2},{3,4},{5,6},{7,8},{9,10},{11,12},{13,14},{15,16},{17,18},{19... | collective-permute-start | bytes 196616 | tf_op jit(solution)/shard_map/ppermute | solution.py:525
  11.1 8.2 %inner_sums.1 = (f32[72,2048]{1,0:T(8,128)S(1)}, f32[8,2048]{1,0:T(8,128)S(1)}, f32[4,8,2048]{2,1,0:T(8,128)S(1)}) custom-call(f32[8]{0:T(128)S(1)} %copy-done.11, f32[8]{0:T(128)S(1)} %copy-done.12, bf16[8,64,2048]{2,1,0:T(8,128)(2,1)S(1)} %copy-done.1, s32[1,8,256]{2,1,0:T(8,128)S(1)} %copy-done.10), custom_call_target="tpu_custom_call" | custom-call | flops 40000000 | bytes 25165824 | tf_op jit(solution)/shard_map/inner_sums/pallas_call | solution.py:225
  19.4 0.0 copy-start.6
  19.5 0.0 copy-start.7
  19.5 0.0 copy-start.8
  19.5 0.0 copy-start.9
  19.5 2.4 %outer_sums.1 = (f32[72,512]{1,0:T(8,128)S(1)}, f32[72,512]{1,0:T(8,128)S(1)}, f32[72,512]{1,0:T(8,128)S(1)}, f32[72,512]{1,0:T(8,128)S(1)}) custom-call(f32[8]{0:T(128)S(1)} %copy-done.11, f32[8]{0:T(128)S(1)} %copy-done.12, bf16[8,64,2048]{2,1,0:T(8,128)(2,1)S(1)} %copy-done.1, bf16[1,64,2048]{2,1,0:T(8,128)(2,1)S(1)} %collective-permute-done.layer_ref, ...), custom_call_target="tpu_custom_call" | custom-call | tf_op jit(solution)/shard_map/outer_sums/pallas_call | solution.py:327
  21.9 0.0 copy-start.2
  21.9 0.0 copy-start.3
  21.9 0.0 copy-start.13
  21.9 0.1 collective-permute-start.4
  22.0 8.1 %collective-permute-start.5 = (f32[72,512]{1,0:T(8,128)S(1)}, f32[72,512]{1,0:T(8,128)S(1)}, u32[]{:S(2)}, u32[]{:S(2)}) collective-permute-start(f32[72,512]{1,0:T(8,128)S(1)} %get-tuple-element.24), channel_id=1, source_target_pairs={{0,64},{32,96},{64,0},{96,32},{1,65},{33,97},{65,1},{97,33},{2,66}... | collective-permute-start | bytes 442376 | tf_op jit(solution)/shard_map/ppermute | solution.py:519
  30.2 2.0 %collective-permute-start.6 = (f32[72,512]{1,0:T(8,128)S(1)}, f32[72,512]{1,0:T(8,128)S(1)}, u32[]{:S(2)}, u32[]{:S(2)}) collective-permute-start(f32[72,512]{1,0:T(8,128)S(1)} %get-tuple-element.25), channel_id=1, source_target_pairs={{0,96},{32,0},{64,32},{96,64},{1,97},{33,1},{65,33},{97,65},{2,98}... | collective-permute-start | bytes 442376 | tf_op jit(solution)/shard_map/ppermute | solution.py:519
  32.1 2.1 %collective-permute-done.5.c_ref = f32[72,512]{1,0:T(8,128)S(1)} collective-permute-done((f32[72,512]{1,0:T(8,128)S(1)}, f32[72,512]{1,0:T(8,128)S(1)}, u32[]{:S(2)}, u32[]{:S(2)}) %collective-permute-start.5) | collective-permute-done | bytes 147488 | tf_op jit(solution)/shard_map/ppermute | solution.py:519
  34.3 1.5 %collective-permute-done.6.d_ref = f32[72,512]{1,0:T(8,128)S(1)} collective-permute-done((f32[72,512]{1,0:T(8,128)S(1)}, f32[72,512]{1,0:T(8,128)S(1)}, u32[]{:S(2)}, u32[]{:S(2)}) %collective-permute-start.6) | collective-permute-done | bytes 147488 | tf_op jit(solution)/shard_map/ppermute | solution.py:519
  35.8 0.1 turn.1
  35.9 26.0 %all_to_all.10.in_ref = f32[64,8,128]{2,1,0:T(8,128)S(1)} all-to-all(f32[64,8,128]{2,1,0:T(8,128)S(1)} %turn.1), channel_id=1, replica_groups=mesh['zhi'=2,'x'=4,'sky'=32] {'zhi','sky'}, dimensions={0} | all-to-all | bytes 524288 | tf_op jit(solution)/shard_map/all_to_all | solution.py:540
  62.0 1.0 %solve.1 = f32[64,8,128]{2,1,0:T(8,128)S(1)} custom-call(f32[64,8,128]{2,1,0:T(8,128)S(1)} %all_to_all.10.in_ref, f32[32,8,128]{2,1,0:T(8,128)S(1)} %copy-done.7, f32[32,8,128]{2,1,0:T(8,128)S(1)} %copy-done.6, bf16[128,256]{1,0:T(8,128)(2,1)S(1)} %copy-done.9, bf16[128,256]{1,0:T(8,128)(2,1)S(1)} %copy-done.8), custom_call_target="tpu_custom_call" | custom-call | tf_op jit(solution)/shard_map/solve/pallas_call | solution.py:457
  63.0 17.7 %all_to_all.11.in_ref = f32[64,8,128]{2,1,0:T(8,128)S(1)} all-to-all(f32[64,8,128]{2,1,0:T(8,128)S(1)} %solve.1), channel_id=1, replica_groups=mesh['zhi'=2,'x'=4,'sky'=32] {'zhi','sky'}, dimensions={0} | all-to-all | bytes 524288 | tf_op jit(solution)/shard_map/all_to_all | solution.py:542
  80.7 1.3 %back.1 = (f32[128,256]{1,0:T(8,128)S(1)}, f32[128,256]{1,0:T(8,128)S(1)}, f32[128,256]{1,0:T(8,128)S(1)}, f32[128,256]{1,0:T(8,128)S(1)}) custom-call(f32[16]{0:T(128)S(1)} %copy-done.13, f32[64,8,128]{2,1,0:T(8,128)S(1)} %all_to_all.11.in_ref, bf16[4,512,256]{2,1,0:T(8,128)(2,1)S(1)} %copy-done.3, bf16[4,512,256]{2,1,0:T(8,128)(2,1)S(1)} %copy-done.2), custom_call_target="tpu_custom_call" | custom-call | tf_op jit(solution)/shard_map/back/pallas_call | solution.py:489
  82.0 0.1 collective-permute-start.7
  82.1 3.2 %collective-permute-start.8 = (f32[128,256]{1,0:T(8,128)S(1)}, f32[128,256]{1,0:T(8,128)S(1)}, u32[]{:S(2)}, u32[]{:S(2)}) collective-permute-start(f32[128,256]{1,0:T(8,128)S(1)} %get-tuple-element.28), channel_id=1, source_target_pairs={{0,64},{32,96},{64,0},{96,32},{1,65},{33,97},{65,1},{97,33},{2,66}... | collective-permute-start | bytes 393224 | tf_op jit(solution)/shard_map/ppermute | solution.py:519
  85.3 2.8 %collective-permute-done.7.b_ref = f32[128,256]{1,0:T(8,128)S(1)} collective-permute-done((f32[128,256]{1,0:T(8,128)S(1)}, f32[128,256]{1,0:T(8,128)S(1)}, u32[]{:S(2)}, u32[]{:S(2)}) %collective-permute-start.7) | collective-permute-done | bytes 131104 | tf_op jit(solution)/shard_map/ppermute | solution.py:519
  88.1 3.4 %collective-permute-done.8.c_ref = f32[128,256]{1,0:T(8,128)S(1)} collective-permute-done((f32[128,256]{1,0:T(8,128)S(1)}, f32[128,256]{1,0:T(8,128)S(1)}, u32[]{:S(2)}, u32[]{:S(2)}) %collective-permute-start.8) | collective-permute-done | bytes 131104 | tf_op jit(solution)/shard_map/ppermute | solution.py:519
  91.5 0.7 final.1
  (26 shorter events, 0.1 us)
Async XLA Ops:
  0.6 10.5 %copy-start.12 = (f32[8]{0:T(128)S(1)}, f32[8]{0:T(128)}, u32[]{:S(2)}) copy-start(f32[8]{0:T(128)} %high_ref.3) | copy-start | bytes 100
  0.6 10.5 %copy-start.11 = (f32[8]{0:T(128)S(1)}, f32[8]{0:T(128)}, u32[]{:S(2)}) copy-start(f32[8]{0:T(128)} %low_ref.3) | copy-start | bytes 100
  0.7 10.5 %copy-start.10 = (s32[1,8,256]{2,1,0:T(8,128)S(1)}, s32[1,8,256]{2,1,0:T(8,128)}, u32[]{:S(2)}) copy-start(s32[1,8,256]{2,1,0:T(8,128)} %refine_ref.1) | copy-start | bytes 24580
  1.6 17.8 %collective-permute-start = (bf16[1,64,2048]{2,1,0:T(8,128)(2,1)S(1)}, bf16[1,64,2048]{2,1,0:T(8,128)(2,1)S(1)}, u32[]{:S(2)}, u32[]{:S(2)}) collective-permute-start(bf16[1,64,2048]{2,1,0:T(8,128)(2,1)S(1)} %constant_dynamic-slice_fusion), channel_id=1, source_target_pairs={{32,64},{96,128},{160,192},{64,32},{128,96},{192,160},{33,65},{97,... | collective-permute-start | bytes 786440 | tf_op jit(solution)/shard_map/ppermute | solution.py:525
  2.3 1.6 %copy-start = (bf16[8,64,2048]{2,1,0:T(8,128)(2,1)S(1)}, bf16[8,64,2048]{2,1,0:T(8,128)(2,1)}, u32[]{:S(2)}) copy-start(bf16[8,64,2048]{2,1,0:T(8,128)(2,1)} %d_ref.5) | copy-start | bytes 6291460
  3.9 7.2 %copy-start.1 = (bf16[8,64,2048]{2,1,0:T(8,128)(2,1)S(1)}, bf16[8,64,2048]{2,1,0:T(8,128)(2,1)}, u32[]{:S(2)}) copy-start(bf16[8,64,2048]{2,1,0:T(8,128)(2,1)} %d_ref.5) | copy-start | bytes 6291460
  3.9 15.5 %copy-start.4 = (bf16[8,256,256]{2,1,0:T(8,128)(2,1)S(1)}, bf16[8,256,256]{2,1,0:T(8,128)(2,1)}, u32[]{:S(2)}) copy-start(bf16[8,256,256]{2,1,0:T(8,128)(2,1)} %constant.44.clone.low_table) | copy-start | bytes 3145732
  3.9 15.5 %copy-start.5 = (bf16[8,256,256]{2,1,0:T(8,128)(2,1)S(1)}, bf16[8,256,256]{2,1,0:T(8,128)(2,1)}, u32[]{:S(2)}) copy-start(bf16[8,256,256]{2,1,0:T(8,128)(2,1)} %constant.43.clone.high_table) | copy-start | bytes 3145732
  4.1 15.3 %collective-permute-start.1 = (bf16[1,64,2048]{2,1,0:T(8,128)(2,1)S(1)}, bf16[1,64,2048]{2,1,0:T(8,128)(2,1)S(1)}, u32[]{:S(2)}, u32[]{:S(2)}) collective-permute-start(bf16[1,64,2048]{2,1,0:T(8,128)(2,1)S(1)} %get-tuple-element.16), channel_id=1, source_target_pairs={{0,32},{64,96},{128,160},{192,224},{32,0},{96,64},{160,128},{224,1... | collective-permute-start | bytes 786440 | tf_op jit(solution)/shard_map/ppermute | solution.py:525
  8.7 10.7 %collective-permute-start.2 = (f32[8,2048]{1,0:T(8,128)S(1)}, f32[8,2048]{1,0:T(8,128)S(1)}, u32[]{:S(2)}, u32[]{:S(2)}) collective-permute-start(f32[8,2048]{1,0:T(8,128)S(1)} %get-tuple-element.17), channel_id=1, source_target_pairs={{0,1},{2,3},{4,5},{6,7},{8,9},{10,11},{12,13},{14,15},{16,17},{18,... | collective-permute-start | bytes 196616 | tf_op jit(solution)/shard_map/ppermute | solution.py:525
  9.9 9.5 %collective-permute-start.3 = (f32[8,2048]{1,0:T(8,128)S(1)}, f32[8,2048]{1,0:T(8,128)S(1)}, u32[]{:S(2)}, u32[]{:S(2)}) collective-permute-start(f32[8,2048]{1,0:T(8,128)S(1)} %get-tuple-element.18), channel_id=1, source_target_pairs={{1,2},{3,4},{5,6},{7,8},{9,10},{11,12},{13,14},{15,16},{17,18},{19... | collective-permute-start | bytes 196616 | tf_op jit(solution)/shard_map/ppermute | solution.py:525
  19.4 42.5 %copy-start.6 = (f32[32,8,128]{2,1,0:T(8,128)S(1)}, f32[32,8,128]{2,1,0:T(8,128)}, u32[]{:S(2)}) copy-start(f32[32,8,128]{2,1,0:T(8,128)} %constant.46.clone.sin_ref) | copy-start | bytes 393220
  19.5 42.5 %copy-start.7 = (f32[32,8,128]{2,1,0:T(8,128)S(1)}, f32[32,8,128]{2,1,0:T(8,128)}, u32[]{:S(2)}) copy-start(f32[32,8,128]{2,1,0:T(8,128)} %constant.45.clone.cos_ref) | copy-start | bytes 393220
  19.5 42.5 %copy-start.8 = (bf16[128,256]{1,0:T(8,128)(2,1)S(1)}, bf16[128,256]{1,0:T(8,128)(2,1)}, u32[]{:S(2)}) copy-start(bf16[128,256]{1,0:T(8,128)(2,1)} %constant.48.clone.low_table) | copy-start | bytes 196612
  19.5 42.5 %copy-start.9 = (bf16[128,256]{1,0:T(8,128)(2,1)S(1)}, bf16[128,256]{1,0:T(8,128)(2,1)}, u32[]{:S(2)}) copy-start(bf16[128,256]{1,0:T(8,128)(2,1)} %constant.47.clone.high_table) | copy-start | bytes 196612
  21.9 58.8 %copy-start.2 = (bf16[4,512,256]{2,1,0:T(8,128)(2,1)S(1)}, bf16[4,512,256]{2,1,0:T(8,128)(2,1)}, u32[]{:S(2)}) copy-start(bf16[4,512,256]{2,1,0:T(8,128)(2,1)} %constant.51.clone.low_table) | copy-start | bytes 3145732
  21.9 58.8 %copy-start.3 = (bf16[4,512,256]{2,1,0:T(8,128)(2,1)S(1)}, bf16[4,512,256]{2,1,0:T(8,128)(2,1)}, u32[]{:S(2)}) copy-start(bf16[4,512,256]{2,1,0:T(8,128)(2,1)} %constant.50.clone.high_table) | copy-start | bytes 3145732
  21.9 58.7 %copy-start.13 = (f32[16]{0:T(128)S(1)}, f32[16]{0:T(128)}, u32[]{:S(2)}) copy-start(f32[16]{0:T(128)} %constant.49.clone.eighth_ref) | copy-start | bytes 196
  21.9 10.2 %collective-permute-start.4 = (f32[72,512]{1,0:T(8,128)S(1)}, f32[72,512]{1,0:T(8,128)S(1)}, u32[]{:S(2)}, u32[]{:S(2)}) collective-permute-start(f32[72,512]{1,0:T(8,128)S(1)} %get-tuple-element.23), channel_id=1, source_target_pairs={{0,32},{32,64},{64,96},{96,0},{1,33},{33,65},{65,97},{97,1},{2,34}... | collective-permute-start | bytes 442376 | tf_op jit(solution)/shard_map/ppermute | solution.py:519
  22.0 12.3 %collective-permute-start.5 = (f32[72,512]{1,0:T(8,128)S(1)}, f32[72,512]{1,0:T(8,128)S(1)}, u32[]{:S(2)}, u32[]{:S(2)}) collective-permute-start(f32[72,512]{1,0:T(8,128)S(1)} %get-tuple-element.24), channel_id=1, source_target_pairs={{0,64},{32,96},{64,0},{96,32},{1,65},{33,97},{65,1},{97,33},{2,66}... | collective-permute-start | bytes 442376 | tf_op jit(solution)/shard_map/ppermute | solution.py:519
  30.2 5.6 %collective-permute-start.6 = (f32[72,512]{1,0:T(8,128)S(1)}, f32[72,512]{1,0:T(8,128)S(1)}, u32[]{:S(2)}, u32[]{:S(2)}) collective-permute-start(f32[72,512]{1,0:T(8,128)S(1)} %get-tuple-element.25), channel_id=1, source_target_pairs={{0,96},{32,0},{64,32},{96,64},{1,97},{33,1},{65,33},{97,65},{2,98}... | collective-permute-start | bytes 442376 | tf_op jit(solution)/shard_map/ppermute | solution.py:519
  82.0 6.1 %collective-permute-start.7 = (f32[128,256]{1,0:T(8,128)S(1)}, f32[128,256]{1,0:T(8,128)S(1)}, u32[]{:S(2)}, u32[]{:S(2)}) collective-permute-start(f32[128,256]{1,0:T(8,128)S(1)} %get-tuple-element.27), channel_id=1, source_target_pairs={{0,32},{32,64},{64,96},{96,0},{1,33},{33,65},{65,97},{97,1},{2,34}... | collective-permute-start | bytes 393224 | tf_op jit(solution)/shard_map/ppermute | solution.py:519
  82.1 9.4 %collective-permute-start.8 = (f32[128,256]{1,0:T(8,128)S(1)}, f32[128,256]{1,0:T(8,128)S(1)}, u32[]{:S(2)}, u32[]{:S(2)}) collective-permute-start(f32[128,256]{1,0:T(8,128)S(1)} %get-tuple-element.28), channel_id=1, source_target_pairs={{0,64},{32,96},{64,0},{96,32},{1,65},{33,97},{65,1},{97,33},{2,66}... | collective-permute-start | bytes 393224 | tf_op jit(solution)/shard_map/ppermute | solution.py:519
  85.3 6.2 %collective-permute-start.9 = (f32[128,256]{1,0:T(8,128)S(1)}, f32[128,256]{1,0:T(8,128)S(1)}, u32[]{:S(2)}, u32[]{:S(2)}) collective-permute-start(f32[128,256]{1,0:T(8,128)S(1)} %get-tuple-element.29), channel_id=1, source_target_pairs={{0,96},{32,0},{64,32},{96,64},{1,97},{33,1},{65,33},{97,65},{2,98}... | collective-permute-start | bytes 393224 | tf_op jit(solution)/shard_map/ppermute | solution.py:519

commit v5 on v4

--- a/solution.py
+++ b/solution.py
@@ -96,6 +96,17 @@
     high, low = split(value)
     dot = functools.partial(jnp.dot, preferred_element_type=f32)
     return dot(high, high_table) + (dot(low, high_table) + dot(high, low_table))
+
+
+def stacked(value):
+    return jnp.concatenate(split(value), axis=0)
+
+
+def dot3_stacked(parts, high_table, low_table):
+    rows = parts.shape[0] // 2
+    dot = functools.partial(jnp.dot, preferred_element_type=f32)
+    both = dot(parts, high_table)
+    return both[:rows] + (both[rows:] + dot(parts[:rows], low_table))
 
 
 def limit(mib):
@@ -251,9 +262,11 @@
     near_ref,
     high_table,
     low_table,
-    *rest,
+    far_ref,
+    next_ref,
+    last_ref,
+    part_ref,
 ):
-    outs, (high_part, low_part) = rest[:4], rest[4:]
     los = lax.axis_index("zhi") * 4 + lax.axis_index("x")
     v0, v1 = d_ref[0].astype(f32), d_ref[1].astype(f32)
     v6, v7 = d_ref[6].astype(f32), d_ref[7].astype(f32)
@@ -312,27 +325,45 @@
 
     for tile in range(8):
         second = sines(tile) if tile else cosines(8)
-        high_part[tile], low_part[tile] = split(jnp.concatenate([cosines(tile), second], axis=1))
-    dot = functools.partial(jnp.dot, preferred_element_type=f32)
-    for ahead in range(4):
-        target = (lax.axis_index("x") + ahead) % 4
-        for half in range(2):
-            tile = 2 * target + half
-            high, low, table = high_part[tile], low_part[tile], high_table[tile]
-            value = dot(high, table) + (dot(low, table) + dot(high, low_table[tile]))
-            outs[ahead][:, 256 * half : 256 * half + 256] = value
+        value = jnp.concatenate([cosines(tile), second], axis=1)
+        value = jnp.concatenate([value, jnp.zeros((8, 256), f32)], axis=0)
+        part_ref[tile] = stacked(value)
+    transform_for(2, part_ref, high_table, low_table, far_ref)
+    transform_for(1, part_ref, high_table, low_table, next_ref)
+    transform_for(3, part_ref, high_table, low_table, last_ref)
+
+
+def transform_for(ahead, part_ref, high_table, low_table, out_ref):
+    target = (lax.axis_index("x") + ahead) % 4
+    for half in range(2):
+        tile = 2 * target + half
+        value = dot3_stacked(part_ref[tile], high_table[tile], low_table[tile])
+        out_ref[:, 256 * half : 256 * half + 256] = value[:72]
+
+
+def rest_kernel(part_ref, high_table, low_table, own_ref):
+    transform_for(0, part_ref, high_table, low_table, own_ref)
 
 
 def outer_sums(low, high, density, layers, rows, inner, tables):
-    return pl.pallas_call(
+    piece = jax.ShapeDtypeStruct((72, 512), f32)
+    two, one, three, parts = pl.pallas_call(
         outer_kernel,
-        out_shape=(jax.ShapeDtypeStruct((72, 512), f32),) * 4,
+        out_shape=(piece, piece, piece, jax.ShapeDtypeStruct((8, 160, 256), bf16)),
         in_specs=[SM, SM] + [VM] * 10,
         out_specs=(VM,) * 4,
-        scratch_shapes=[pltpu.VMEM((8, 72, 256), bf16)] * 2,
         compiler_params=limit(32),
         name="outer_sums",
     )(low, high, density, *layers, *rows, *inner, *tables)
+    own = pl.pallas_call(
+        rest_kernel,
+        out_shape=piece,
+        in_specs=[VM] * 3,
+        out_specs=VM,
+        compiler_params=limit(24),
+        name="other_sums",
+    )(parts, *tables)
+    return own, one, two, three
 
 
 def turn_kernel(a_ref, b_ref, c_ref, d_ref, out_ref):
@@ -464,36 +495,59 @@
     )(pieces, *tables)
 
 
-def back_kernel(eighth_ref, in_ref, high_table, low_table, *outs):
+def back_for(ahead, eighth_ref, plain, bent, high_table, low_table, out_ref):
     zhi, column = lax.axis_index("zhi"), lax.axis_index("x")
+    target = (column + ahead) % 4
+    parts = []
+    for half in range(2):
+        lanes = slice(256 * half, 256 * half + 256)
+        turns = (2 * column + half) * (4 * zhi + target) % 8
+        cosine, sine = eighth_ref[turns], eighth_ref[8 + turns]
+        parts.append(cosine * plain[:, lanes] + sine * bent[:, lanes])
+    value = stacked(jnp.concatenate(parts, axis=1))
+    out_ref[...] = dot3_stacked(value, high_table[column], low_table[column])
+
+
+def back_kernel(
+    eighth_ref, in_ref, high_table, low_table, far_ref, next_ref, last_ref, plain_ref, bent_ref
+):
     value = in_ref[...]
     sub = lax.broadcasted_iota(jnp.int32, (64, 8, 128), 1)
     bent = pltpu.roll(value, 4, 1) * jnp.where(sub < 4, -1.0, 1.0)
-    plain = value.reshape(512, 128).T
-    bent = bent.reshape(512, 128).T
-    for ahead in range(4):
-        target = (column + ahead) % 4
-        parts = []
-        for half in range(2):
-            lanes = slice(256 * half, 256 * half + 256)
-            turns = (2 * column + half) * (4 * zhi + target) % 8
-            cosine, sine = eighth_ref[turns], eighth_ref[8 + turns]
-            parts.append(cosine * plain[:, lanes] + sine * bent[:, lanes])
-        value = jnp.concatenate(parts, axis=1)
-        outs[ahead][...] = dot3(value, high_table[column], low_table[column])
+    plain, bent = value.reshape(512, 128).T, bent.reshape(512, 128).T
+    plain_ref[...] = plain
+    bent_ref[...] = bent
+    back_for(2, eighth_ref, plain, bent, high_table, low_table, far_ref)
+    back_for(1, eighth_ref, plain, bent, high_table, low_table, next_ref)
+    back_for(3, eighth_ref, plain, bent, high_table, low_table, last_ref)
+
+
+def back_rest_kernel(eighth_ref, plain_ref, bent_ref, high_table, low_table, own_ref):
+    back_for(0, eighth_ref, plain_ref[...], bent_ref[...], high_table, low_table, own_ref)
 
 
 def back(pieces, tables):
     turns = np.arange(8) * (2 * np.pi / 8)
     eighth = np.concatenate([np.cos(turns), np.sin(turns)]).astype(np.float32)
-    return pl.pallas_call(
+    piece = jax.ShapeDtypeStruct((128, 256), f32)
+    held = jax.ShapeDtypeStruct((128, 512), f32)
+    two, one, three, plain, bent = pl.pallas_call(
         back_kernel,
-        out_shape=(jax.ShapeDtypeStruct((128, 256), f32),) * 4,
+        out_shape=(piece, piece, piece, held, held),
         in_specs=[SM, VM, VM, VM],
-        out_specs=(VM,) * 4,
+        out_specs=(VM,) * 5,
         compiler_params=limit(24),
         name="back",
     )(eighth, pieces, *tables)
+    own = pl.pallas_call(
+        back_rest_kernel,
+        out_shape=piece,
+        in_specs=[SM] + [VM] * 4,
+        out_specs=VM,
+        compiler_params=limit(24),
+        name="back_rest",
+    )(eighth, plain, bent, *tables)
+    return own, one, two, three
 
 
 def final_kernel(a_ref, b_ref, c_ref, d_ref, x_ref, y_ref):
@@ -516,7 +570,7 @@
 
 def deliver(pieces):
     return [pieces[0]] + [
-        lax.ppermute(pieces[a], "x", [(i, (i + a) % 4) for i in range(4)]) for a in (1, 2, 3)
+        lax.ppermute(pieces[a], "x", [(i, (i + a) % 4) for i in range(4)]) for a in (2, 1, 3)
     ]
 
 

time: 92.4 us -> 91.6 us (level)
  blocking collectives: 43.7 us -> 42.1 us
    all_to_all x1, blocking collectives: 26 us -> 24.4 us  [body(): pieces = lax.all_to_all(turn(summed), ('zhi', 'sky'), 0, 0, tiled=True)]
    pallas_call x2 -> x4, Pallas kernels: 3.71 us -> 4.43 us  [the longest x1 2.16 us: outer_sums(): pl.pallas_call(outer_kernel, out_shape=(piece, piece, piece, jax.ShapeDty...]
  transfers between devices with their start and end apart: 10 -> 10, of which waited for: 4 -> 3; matrix products, arithmetic and copies ran while one was open for 0% -> 0% of each run, Pallas kernels for 9% -> 10%
where the time goes in v5:
time: 91.6 us; the launch traced here: 91.4 us
  blocking collectives  42.1 us (46%)
  starting transfers between devices  21.5 us (23%)
  Pallas kernels  14.6 us (16%)
  waiting for transfers between devices  9.66 us (11%)
  local copies, waits for them, and re-layouts  2.62 us (3%)
    all_to_all x1, blocking collectives, body(): pieces = lax.all_to_all(turn(summed), ('zhi', 'sky'), 0, 0, tiled=True)  24.4 us
    all_to_all x1, blocking collectives, body(): pieces = lax.all_to_all(pieces, ('zhi', 'sky'), 0, 0, tiled=True)  17.7 us
    ppermute x6, starting transfers between devices, deliver(): lax.ppermute(pieces[a], 'x', [(i, (i + a) % 4) for i in range(4)])  13.8 us
    ppermute x6, waiting for transfers between devices, deliver(): lax.ppermute(pieces[a], 'x', [(i, (i + a) % 4) for i in range(4)])  9.65 us
    pallas_call x1, Pallas kernels, inner_sums(): pl.pallas_call(inner_kernel, out_shape=(jax.ShapeDtypeStruct((ROWS + 8, N...  8.23 us
    ppermute x4, starting transfers between devices, swap(): return lax.ppermute(array, axes, pairs + [(b, a) for a, b in pairs])  7.67 us
    pallas_call x1, Pallas kernels, outer_sums(): pl.pallas_call(outer_kernel, out_shape=(piece, piece, piece, jax.ShapeDty...  2.16 us
  transfers between devices with their start and end apart: 10, of which 3 were waited for; matrix products, arithmetic and copies ran while one was open for 0% of the time, Pallas kernels for 10%

profile of v5, /device:TPU:1, one launch (start us, length us, event | category | flops | bytes accessed | tf_op | source)
XLA Modules:
  0.0 91.4 jit_solution(6296315221969134381)
XLA Ops:
  0.7 1.0 %constant_dynamic-slice_fusion = bf16[1,64,2048]{2,1,0:T(8,128)(2,1)S(1)} fusion(bf16[8,64,2048]{2,1,0:T(8,128)(2,1)} %d_ref.5, s32[]{:T(128)S(6)} %select_n.13), kind=kLoop, calls=%fused_computation | loop fusion | bytes 524292 | tf_op jit(solution)/shard_map/dynamic_slice | solution.py:582
  1.6 0.7 collective-permute-start
  2.3 0.0 copy-start
  2.3 1.6 %copy-done = bf16[8,64,2048]{2,1,0:T(8,128)(2,1)S(1)} copy-done((bf16[8,64,2048]{2,1,0:T(8,128)(2,1)S(1)}, bf16[8,64,2048]{2,1,0:T(8,128)(2,1)}, u32[]{:S(2)}) %copy-start) | copy-done | bytes 2097176
  3.9 0.2 edge_rows.1
  4.1 4.6 %collective-permute-start.1 = (bf16[1,64,2048]{2,1,0:T(8,128)(2,1)S(1)}, bf16[1,64,2048]{2,1,0:T(8,128)(2,1)S(1)}, u32[]{:S(2)}, u32[]{:S(2)}) collective-permute-start(bf16[1,64,2048]{2,1,0:T(8,128)(2,1)S(1)} %get-tuple-element.17), channel_id=1, source_target_pairs={{0,32},{64,96},{128,160},{192,224},{32,0},{96,64},{160,128},{224,1... | collective-permute-start | bytes 786440 | tf_op jit(solution)/shard_map/ppermute | solution.py:579
  8.7 1.2 %collective-permute-start.2 = (f32[8,2048]{1,0:T(8,128)S(1)}, f32[8,2048]{1,0:T(8,128)S(1)}, u32[]{:S(2)}, u32[]{:S(2)}) collective-permute-start(f32[8,2048]{1,0:T(8,128)S(1)} %get-tuple-element.18), channel_id=1, source_target_pairs={{0,1},{2,3},{4,5},{6,7},{8,9},{10,11},{12,13},{14,15},{16,17},{18,... | collective-permute-start | bytes 196616 | tf_op jit(solution)/shard_map/ppermute | solution.py:579
  9.9 1.2 %collective-permute-start.3 = (f32[8,2048]{1,0:T(8,128)S(1)}, f32[8,2048]{1,0:T(8,128)S(1)}, u32[]{:S(2)}, u32[]{:S(2)}) collective-permute-start(f32[8,2048]{1,0:T(8,128)S(1)} %get-tuple-element.19), channel_id=1, source_target_pairs={{1,2},{3,4},{5,6},{7,8},{9,10},{11,12},{13,14},{15,16},{17,18},{19... | collective-permute-start | bytes 196616 | tf_op jit(solution)/shard_map/ppermute | solution.py:579
  11.1 8.2 %inner_sums.1 = (f32[72,2048]{1,0:T(8,128)S(1)}, f32[8,2048]{1,0:T(8,128)S(1)}, f32[4,8,2048]{2,1,0:T(8,128)S(1)}) custom-call(f32[8]{0:T(128)S(1)} %copy-done.12, f32[8]{0:T(128)S(1)} %copy-done.13, bf16[8,64,2048]{2,1,0:T(8,128)(2,1)S(1)} %copy-done.1, s32[1,8,256]{2,1,0:T(8,128)S(1)} %copy-done.10), custom_call_target="tpu_custom_call" | custom-call | flops 40000000 | bytes 25165824 | tf_op jit(solution)/shard_map/inner_sums/pallas_call | solution.py:236
  19.4 0.0 collective-permute-done.2.row_ref
  19.4 0.0 collective-permute-done.layer_ref
  19.4 0.0 collective-permute-done.1.other_layer_ref
  19.4 2.2 %outer_sums.1 = (f32[72,512]{1,0:T(8,128)S(1)}, f32[72,512]{1,0:T(8,128)S(1)}, f32[72,512]{1,0:T(8,128)S(1)}, bf16[8,160,256]{2,1,0:T(8,128)(2,1)S(1)}) custom-call(f32[8]{0:T(128)S(1)} %copy-done.12, f32[8]{0:T(128)S(1)} %copy-done.13, bf16[8,64,2048]{2,1,0:T(8,128)(2,1)S(1)} %copy-done.1, bf16[1,64,2048]{2,1,0:T(8,128)(2,1)S(1)} %collective-permute-done.layer_ref, ...), custom_call_target="tpu_custom_call" | custom-call | tf_op jit(solution)/shard_map/outer_sums/pallas_call | solution.py:350
  21.6 8.2 %collective-permute-start.4 = (f32[72,512]{1,0:T(8,128)S(1)}, f32[72,512]{1,0:T(8,128)S(1)}, u32[]{:S(2)}, u32[]{:S(2)}) collective-permute-start(f32[72,512]{1,0:T(8,128)S(1)} %get-tuple-element.24), channel_id=1, source_target_pairs={{0,64},{32,96},{64,0},{96,32},{1,65},{33,97},{65,1},{97,33},{2,66}... | collective-permute-start | bytes 442376 | tf_op jit(solution)/shard_map/ppermute | solution.py:573
  29.8 2.7 %collective-permute-start.6 = (f32[72,512]{1,0:T(8,128)S(1)}, f32[72,512]{1,0:T(8,128)S(1)}, u32[]{:S(2)}, u32[]{:S(2)}) collective-permute-start(f32[72,512]{1,0:T(8,128)S(1)} %get-tuple-element.26), channel_id=1, source_target_pairs={{0,96},{32,0},{64,32},{96,64},{1,97},{33,1},{65,33},{97,65},{2,98}... | collective-permute-start | bytes 442376 | tf_op jit(solution)/shard_map/ppermute | solution.py:573
  32.4 0.2 other_sums.1.a_ref
  32.7 0.0 copy-start.2
  32.7 0.0 copy-start.3
  32.7 0.0 copy-start.11
  32.7 3.8 %collective-permute-done.5.c_ref = f32[72,512]{1,0:T(8,128)S(1)} collective-permute-done((f32[72,512]{1,0:T(8,128)S(1)}, f32[72,512]{1,0:T(8,128)S(1)}, u32[]{:S(2)}, u32[]{:S(2)}) %collective-permute-start.5) | collective-permute-done | bytes 147488 | tf_op jit(solution)/shard_map/ppermute | solution.py:573
  36.5 0.1 turn.1
  36.7 24.4 %all_to_all.10.in_ref = f32[64,8,128]{2,1,0:T(8,128)S(1)} all-to-all(f32[64,8,128]{2,1,0:T(8,128)S(1)} %turn.1), channel_id=1, replica_groups=mesh['zhi'=2,'x'=4,'sky'=32] {'zhi','sky'}, dimensions={0} | all-to-all | bytes 524288 | tf_op jit(solution)/shard_map/all_to_all | solution.py:594
  61.2 1.0 %solve.1 = f32[64,8,128]{2,1,0:T(8,128)S(1)} custom-call(f32[64,8,128]{2,1,0:T(8,128)S(1)} %all_to_all.10.in_ref, f32[32,8,128]{2,1,0:T(8,128)S(1)} %copy-done.7, f32[32,8,128]{2,1,0:T(8,128)S(1)} %copy-done.6, bf16[128,256]{1,0:T(8,128)(2,1)S(1)} %copy-done.9, bf16[128,256]{1,0:T(8,128)(2,1)S(1)} %copy-done.8), custom_call_target="tpu_custom_call" | custom-call | tf_op jit(solution)/shard_map/solve/pallas_call | solution.py:488
  62.1 17.7 %all_to_all.11.in_ref = f32[64,8,128]{2,1,0:T(8,128)S(1)} all-to-all(f32[64,8,128]{2,1,0:T(8,128)S(1)} %solve.1), channel_id=1, replica_groups=mesh['zhi'=2,'x'=4,'sky'=32] {'zhi','sky'}, dimensions={0} | all-to-all | bytes 524288 | tf_op jit(solution)/shard_map/all_to_all | solution.py:596
  79.8 1.2 %back.1 = (f32[128,256]{1,0:T(8,128)S(1)}, f32[128,256]{1,0:T(8,128)S(1)}, f32[128,256]{1,0:T(8,128)S(1)}, f32[128,512]{1,0:T(8,128)S(1)}, f32[128,512]{1,0:T(8,128)S(1)}) custom-call(f32[16]{0:T(128)S(1)} %copy-done.11, f32[64,8,128]{2,1,0:T(8,128)S(1)} %all_to_all.11.in_ref, bf16[4,512,256]{2,1,0:T(8,128)(2,1)S(1)} %copy-done.3, ...), custom_call_target="tpu_custom_call" | custom-call | tf_op jit(solution)/shard_map/back/pallas_call | solution.py:534
  81.0 0.3 collective-permute-start.7
  81.3 0.9 collective-permute-start.8
  82.2 1.8 %collective-permute-start.9 = (f32[128,256]{1,0:T(8,128)S(1)}, f32[128,256]{1,0:T(8,128)S(1)}, u32[]{:S(2)}, u32[]{:S(2)}) collective-permute-start(f32[128,256]{1,0:T(8,128)S(1)} %get-tuple-element.31), channel_id=1, source_target_pairs={{0,96},{32,0},{64,32},{96,64},{1,97},{33,1},{65,33},{97,65},{2,98}... | collective-permute-start | bytes 393224 | tf_op jit(solution)/shard_map/ppermute | solution.py:573
  84.0 0.8 back_rest.1.a_ref
  84.8 2.7 %collective-permute-done.7.b_ref = f32[128,256]{1,0:T(8,128)S(1)} collective-permute-done((f32[128,256]{1,0:T(8,128)S(1)}, f32[128,256]{1,0:T(8,128)S(1)}, u32[]{:S(2)}, u32[]{:S(2)}) %collective-permute-start.7) | collective-permute-done | bytes 131104 | tf_op jit(solution)/shard_map/ppermute | solution.py:573
  87.5 3.2 %collective-permute-done.8.c_ref = f32[128,256]{1,0:T(8,128)S(1)} collective-permute-done((f32[128,256]{1,0:T(8,128)S(1)}, f32[128,256]{1,0:T(8,128)S(1)}, u32[]{:S(2)}, u32[]{:S(2)}) %collective-permute-start.8) | collective-permute-done | bytes 131104 | tf_op jit(solution)/shard_map/ppermute | solution.py:573
  90.7 0.7 final.1
  (28 shorter events, 0.1 us)
Async XLA Ops:
  0.6 10.5 %copy-start.13 = (f32[8]{0:T(128)S(1)}, f32[8]{0:T(128)}, u32[]{:S(2)}) copy-start(f32[8]{0:T(128)} %high_ref.3) | copy-start | bytes 100
  0.6 10.5 %copy-start.12 = (f32[8]{0:T(128)S(1)}, f32[8]{0:T(128)}, u32[]{:S(2)}) copy-start(f32[8]{0:T(128)} %low_ref.3) | copy-start | bytes 100
  0.7 10.5 %copy-start.10 = (s32[1,8,256]{2,1,0:T(8,128)S(1)}, s32[1,8,256]{2,1,0:T(8,128)}, u32[]{:S(2)}) copy-start(s32[1,8,256]{2,1,0:T(8,128)} %refine_ref.1) | copy-start | bytes 24580
  1.6 17.8 %collective-permute-start = (bf16[1,64,2048]{2,1,0:T(8,128)(2,1)S(1)}, bf16[1,64,2048]{2,1,0:T(8,128)(2,1)S(1)}, u32[]{:S(2)}, u32[]{:S(2)}) collective-permute-start(bf16[1,64,2048]{2,1,0:T(8,128)(2,1)S(1)} %constant_dynamic-slice_fusion), channel_id=1, source_target_pairs={{32,64},{96,128},{160,192},{64,32},{128,96},{192,160},{33,65},{97,... | collective-permute-start | bytes 786440 | tf_op jit(solution)/shard_map/ppermute | solution.py:579
  2.3 1.6 %copy-start = (bf16[8,64,2048]{2,1,0:T(8,128)(2,1)S(1)}, bf16[8,64,2048]{2,1,0:T(8,128)(2,1)}, u32[]{:S(2)}) copy-start(bf16[8,64,2048]{2,1,0:T(8,128)(2,1)} %d_ref.5) | copy-start | bytes 6291460
  3.9 7.2 %copy-start.1 = (bf16[8,64,2048]{2,1,0:T(8,128)(2,1)S(1)}, bf16[8,64,2048]{2,1,0:T(8,128)(2,1)}, u32[]{:S(2)}) copy-start(bf16[8,64,2048]{2,1,0:T(8,128)(2,1)} %d_ref.5) | copy-start | bytes 6291460
  3.9 15.5 %copy-start.4 = (bf16[8,256,256]{2,1,0:T(8,128)(2,1)S(1)}, bf16[8,256,256]{2,1,0:T(8,128)(2,1)}, u32[]{:S(2)}) copy-start(bf16[8,256,256]{2,1,0:T(8,128)(2,1)} %constant.44.clone.low_table) | copy-start | bytes 3145732
  3.9 15.5 %copy-start.5 = (bf16[8,256,256]{2,1,0:T(8,128)(2,1)S(1)}, bf16[8,256,256]{2,1,0:T(8,128)(2,1)}, u32[]{:S(2)}) copy-start(bf16[8,256,256]{2,1,0:T(8,128)(2,1)} %constant.43.clone.high_table) | copy-start | bytes 3145732
  4.1 15.3 %collective-permute-start.1 = (bf16[1,64,2048]{2,1,0:T(8,128)(2,1)S(1)}, bf16[1,64,2048]{2,1,0:T(8,128)(2,1)S(1)}, u32[]{:S(2)}, u32[]{:S(2)}) collective-permute-start(bf16[1,64,2048]{2,1,0:T(8,128)(2,1)S(1)} %get-tuple-element.17), channel_id=1, source_target_pairs={{0,32},{64,96},{128,160},{192,224},{32,0},{96,64},{160,128},{224,1... | collective-permute-start | bytes 786440 | tf_op jit(solution)/shard_map/ppermute | solution.py:579
  8.7 10.7 %collective-permute-start.2 = (f32[8,2048]{1,0:T(8,128)S(1)}, f32[8,2048]{1,0:T(8,128)S(1)}, u32[]{:S(2)}, u32[]{:S(2)}) collective-permute-start(f32[8,2048]{1,0:T(8,128)S(1)} %get-tuple-element.18), channel_id=1, source_target_pairs={{0,1},{2,3},{4,5},{6,7},{8,9},{10,11},{12,13},{14,15},{16,17},{18,... | collective-permute-start | bytes 196616 | tf_op jit(solution)/shard_map/ppermute | solution.py:579
  9.9 9.5 %collective-permute-start.3 = (f32[8,2048]{1,0:T(8,128)S(1)}, f32[8,2048]{1,0:T(8,128)S(1)}, u32[]{:S(2)}, u32[]{:S(2)}) collective-permute-start(f32[8,2048]{1,0:T(8,128)S(1)} %get-tuple-element.19), channel_id=1, source_target_pairs={{1,2},{3,4},{5,6},{7,8},{9,10},{11,12},{13,14},{15,16},{17,18},{19... | collective-permute-start | bytes 196616 | tf_op jit(solution)/shard_map/ppermute | solution.py:579
  21.6 11.1 %collective-permute-start.4 = (f32[72,512]{1,0:T(8,128)S(1)}, f32[72,512]{1,0:T(8,128)S(1)}, u32[]{:S(2)}, u32[]{:S(2)}) collective-permute-start(f32[72,512]{1,0:T(8,128)S(1)} %get-tuple-element.24), channel_id=1, source_target_pairs={{0,64},{32,96},{64,0},{96,32},{1,65},{33,97},{65,1},{97,33},{2,66}... | collective-permute-start | bytes 442376 | tf_op jit(solution)/shard_map/ppermute | solution.py:573
  29.8 6.8 %collective-permute-start.5 = (f32[72,512]{1,0:T(8,128)S(1)}, f32[72,512]{1,0:T(8,128)S(1)}, u32[]{:S(2)}, u32[]{:S(2)}) collective-permute-start(f32[72,512]{1,0:T(8,128)S(1)} %get-tuple-element.25), channel_id=1, source_target_pairs={{0,32},{32,64},{64,96},{96,0},{1,33},{33,65},{65,97},{97,1},{2,34}... | collective-permute-start | bytes 442376 | tf_op jit(solution)/shard_map/ppermute | solution.py:573
  29.8 6.8 %collective-permute-start.6 = (f32[72,512]{1,0:T(8,128)S(1)}, f32[72,512]{1,0:T(8,128)S(1)}, u32[]{:S(2)}, u32[]{:S(2)}) collective-permute-start(f32[72,512]{1,0:T(8,128)S(1)} %get-tuple-element.26), channel_id=1, source_target_pairs={{0,96},{32,0},{64,32},{96,64},{1,97},{33,1},{65,33},{97,65},{2,98}... | collective-permute-start | bytes 442376 | tf_op jit(solution)/shard_map/ppermute | solution.py:573
  32.4 28.7 %copy-start.6 = (f32[32,8,128]{2,1,0:T(8,128)S(1)}, f32[32,8,128]{2,1,0:T(8,128)}, u32[]{:S(2)}) copy-start(f32[32,8,128]{2,1,0:T(8,128)} %constant.46.clone.sin_ref) | copy-start | bytes 393220
  32.4 28.7 %copy-start.7 = (f32[32,8,128]{2,1,0:T(8,128)S(1)}, f32[32,8,128]{2,1,0:T(8,128)}, u32[]{:S(2)}) copy-start(f32[32,8,128]{2,1,0:T(8,128)} %constant.45.clone.cos_ref) | copy-start | bytes 393220
  32.4 28.7 %copy-start.8 = (bf16[128,256]{1,0:T(8,128)(2,1)S(1)}, bf16[128,256]{1,0:T(8,128)(2,1)}, u32[]{:S(2)}) copy-start(bf16[128,256]{1,0:T(8,128)(2,1)} %constant.48.clone.low_table) | copy-start | bytes 196612
  32.4 28.7 %copy-start.9 = (bf16[128,256]{1,0:T(8,128)(2,1)S(1)}, bf16[128,256]{1,0:T(8,128)(2,1)}, u32[]{:S(2)}) copy-start(bf16[128,256]{1,0:T(8,128)(2,1)} %constant.47.clone.high_table) | copy-start | bytes 196612
  32.7 47.1 %copy-start.2 = (bf16[4,512,256]{2,1,0:T(8,128)(2,1)S(1)}, bf16[4,512,256]{2,1,0:T(8,128)(2,1)}, u32[]{:S(2)}) copy-start(bf16[4,512,256]{2,1,0:T(8,128)(2,1)} %constant.51.clone.low_table) | copy-start | bytes 3145732
  32.7 47.1 %copy-start.3 = (bf16[4,512,256]{2,1,0:T(8,128)(2,1)S(1)}, bf16[4,512,256]{2,1,0:T(8,128)(2,1)}, u32[]{:S(2)}) copy-start(bf16[4,512,256]{2,1,0:T(8,128)(2,1)} %constant.50.clone.high_table) | copy-start | bytes 3145732
  32.7 47.1 %copy-start.11 = (f32[16]{0:T(128)S(1)}, f32[16]{0:T(128)}, u32[]{:S(2)}) copy-start(f32[16]{0:T(128)} %constant.49.clone.eighth_ref) | copy-start | bytes 196
  81.0 6.5 %collective-permute-start.7 = (f32[128,256]{1,0:T(8,128)S(1)}, f32[128,256]{1,0:T(8,128)S(1)}, u32[]{:S(2)}, u32[]{:S(2)}) collective-permute-start(f32[128,256]{1,0:T(8,128)S(1)} %get-tuple-element.29), channel_id=1, source_target_pairs={{0,64},{32,96},{64,0},{96,32},{1,65},{33,97},{65,1},{97,33},{2,66}... | collective-permute-start | bytes 393224 | tf_op jit(solution)/shard_map/ppermute | solution.py:573
  81.3 9.4 %collective-permute-start.8 = (f32[128,256]{1,0:T(8,128)S(1)}, f32[128,256]{1,0:T(8,128)S(1)}, u32[]{:S(2)}, u32[]{:S(2)}) collective-permute-start(f32[128,256]{1,0:T(8,128)S(1)} %get-tuple-element.30), channel_id=1, source_target_pairs={{0,32},{32,64},{64,96},{96,0},{1,33},{33,65},{65,97},{97,1},{2,34}... | collective-permute-start | bytes 393224 | tf_op jit(solution)/shard_map/ppermute | solution.py:573
  82.2 8.5 %collective-permute-start.9 = (f32[128,256]{1,0:T(8,128)S(1)}, f32[128,256]{1,0:T(8,128)S(1)}, u32[]{:S(2)}, u32[]{:S(2)}) collective-permute-start(f32[128,256]{1,0:T(8,128)S(1)} %get-tuple-element.31), channel_id=1, source_target_pairs={{0,96},{32,0},{64,32},{96,64},{1,97},{33,1},{65,33},{97,65},{2,98}... | collective-permute-start | bytes 393224 | tf_op jit(solution)/shard_map/ppermute | solution.py:573

commit v6 on v5

--- a/solution.py
+++ b/solution.py
@@ -35,6 +35,11 @@
 def tile_order(real, imag):
     pair = np.stack([real.reshape(SKY, 4, -1), imag.reshape(SKY, 4, -1)], axis=1)
     return pair.reshape(256, -1)
+
+
+def tile_groups(real, imag):
+    pair = np.stack([real.reshape(SKY, 4, -1), imag.reshape(SKY, 4, -1)], axis=1)
+    return pair.transpose(2, 1, 0, 3).reshape(256, -1)
 
 
 def forward_table():
@@ -51,7 +56,7 @@
             real = np.block([[cosine[:64], zero], [zero, cosine[64:]]])
             imag = np.block([[-sine[:64], zero], [zero, -sine[64:]]])
             imag[0, :128] = (-1.0) ** b
-        tiles.append(tile_order(real, imag).T)
+        tiles.append(tile_groups(real, imag).T)
     return np.stack(tiles)
 
 
@@ -368,14 +373,29 @@
 
 def turn_kernel(a_ref, b_ref, c_ref, d_ref, out_ref):
     total = (a_ref[...] + b_ref[...]) + (c_ref[...] + d_ref[...])
-    total = jnp.concatenate([total, jnp.zeros((56, 512), f32)], axis=0)
-    out_ref[...] = total.T.reshape(64, 8, 128)
+    turned = jnp.concatenate([total, jnp.zeros((56, 512), f32)], axis=0).T
+    lane = lax.broadcasted_iota(jnp.int32, (SKY, 128), 1)
+    for half in range(2):
+        at = slice(SKY * half, SKY * half + SKY)
+        spill = jnp.zeros((SKY, 128), f32)
+        for c in range(4):
+            first = 256 * half + 64 * c
+            real, imag = turned[first : first + SKY], turned[first + SKY : first + 2 * SKY]
+            out_ref[at, 0, 128 * c : 128 * c + 128] = jnp.where(
+                lane < 64, real, pltpu.roll(imag, 64, 1)
+            )
+            for sub, part in ((c, real), (4 + c, imag)):
+                up = (128 - 16 * sub) % 128
+                down = (up + 63) % 128
+                spill = jnp.where(lane == up, pltpu.roll(part, (up - 64) % 128, 1), spill)
+                spill = jnp.where(lane == down, pltpu.roll(part, (down - 71) % 128, 1), spill)
+        out_ref[at, 0, 512:640] = spill
 
 
 def turn(pieces):
     return pl.pallas_call(
         turn_kernel,
-        out_shape=jax.ShapeDtypeStruct((64, 8, 128), f32),
+        out_shape=jax.ShapeDtypeStruct((64, 1, 640), f32),
         in_specs=[VM] * 4,
         out_specs=VM,
         compiler_params=limit(24),
@@ -428,12 +448,21 @@
     def bent(v):
         return swap(v) * sign
 
-    total = [in_ref[s] + in_ref[SKY + s] for s in range(SKY)]
+    main, spill = [], []
+    for s in range(SKY):
+        rows = [
+            jnp.broadcast_to(in_ref[s, :, lanes] + in_ref[SKY + s, :, lanes], (8, 128))
+            for lanes in (slice(128 * c, 128 * c + 128) for c in range(5))
+        ]
+        v = rows[3]
+        for c in range(3):
+            v = jnp.where(sub % 4 == c, rows[c], v)
+        main.append(jnp.where(sub < 4, v, pltpu.roll(v, 64, 1)))
+        spill.append(pltpu.roll(rows[4], 0, 1, stride=16, stride_axis=0))
     values = []
     for s in range(SKY):
-        up = pltpu.roll(total[(s - 1) % SKY], 64, 1)
-        down = pltpu.roll(total[(s + 1) % SKY], 120, 1)
-        v = total[s] + jnp.where(lane == 0, up, jnp.where(lane == 63, down, 0.0))
+        up, down = spill[(s - 1) % SKY], spill[(s + 1) % SKY]
+        v = main[s] + jnp.where(lane == 0, up, jnp.where(lane == 63, down, 0.0))
         v = jnp.where(lower, v, pltpu.roll(v, 64, 1))
         apart = jnp.where(sub == 4, 0.0, jnp.where(lower, v, swap(v)))
         values.append(jnp.where(packed, apart, v))

time: 91.6 us -> 89.8 us (0.980)
  blocking collectives: 42.1 us -> 40.1 us
    all_to_all x1, blocking collectives: 24.4 us -> 23 us  [body(): pieces = lax.all_to_all(turn(summed), ('zhi', 'sky'), 0, 0, tiled=True)]
  transfers between devices with their start and end apart: 10 -> 10, of which waited for: 3 -> 3; matrix products, arithmetic and copies ran while one was open for 0% -> 0% of each run, Pallas kernels for 10% -> 11%
where the time goes in v6:
time: 89.8 us; the launch traced here: 89.6 us
  blocking collectives  40.1 us (45%)
  starting transfers between devices  21.5 us (24%)
  Pallas kernels  14.9 us (17%)
  waiting for transfers between devices  9.72 us (11%)
  local copies, waits for them, and re-layouts  2.62 us (3%)
    all_to_all x1, blocking collectives, body(): pieces = lax.all_to_all(turn(summed), ('zhi', 'sky'), 0, 0, tiled=True)  23 us
    all_to_all x1, blocking collectives, body(): pieces = lax.all_to_all(pieces, ('zhi', 'sky'), 0, 0, tiled=True)  17.1 us
    ppermute x6, starting transfers between devices, deliver(): lax.ppermute(pieces[a], 'x', [(i, (i + a) % 4) for i in range(4)])  13.8 us
    ppermute x6, waiting for transfers between devices, deliver(): lax.ppermute(pieces[a], 'x', [(i, (i + a) % 4) for i in range(4)])  9.71 us
    pallas_call x1, Pallas kernels, inner_sums(): pl.pallas_call(inner_kernel, out_shape=(jax.ShapeDtypeStruct((ROWS + 8, N...  8.23 us
    ppermute x4, starting transfers between devices, swap(): return lax.ppermute(array, axes, pairs + [(b, a) for a, b in pairs])  7.67 us
    pallas_call x1, Pallas kernels, outer_sums(): pl.pallas_call(outer_kernel, out_shape=(piece, piece, piece, jax.ShapeDty...  2.18 us
  transfers between devices with their start and end apart: 10, of which 3 were waited for; matrix products, arithmetic and copies ran while one was open for 0% of the time, Pallas kernels for 11%

profile of v6, /device:TPU:1, one launch (start us, length us, event | category | flops | bytes accessed | tf_op | source)
XLA Modules:
  0.0 89.6 jit_solution(17453290878573193589)
XLA Ops:
  0.7 1.0 %constant_dynamic-slice_fusion = bf16[1,64,2048]{2,1,0:T(8,128)(2,1)S(1)} fusion(bf16[8,64,2048]{2,1,0:T(8,128)(2,1)} %d_ref.5, s32[]{:T(128)S(6)} %select_n.13), kind=kLoop, calls=%fused_computation | loop fusion | bytes 524292 | tf_op jit(solution)/shard_map/dynamic_slice | solution.py:611
  1.6 0.7 collective-permute-start
  2.3 0.0 copy-start
  2.3 1.6 %copy-done = bf16[8,64,2048]{2,1,0:T(8,128)(2,1)S(1)} copy-done((bf16[8,64,2048]{2,1,0:T(8,128)(2,1)S(1)}, bf16[8,64,2048]{2,1,0:T(8,128)(2,1)}, u32[]{:S(2)}) %copy-start) | copy-done | bytes 2097176
  3.9 0.2 edge_rows.1
  4.1 4.6 %collective-permute-start.1 = (bf16[1,64,2048]{2,1,0:T(8,128)(2,1)S(1)}, bf16[1,64,2048]{2,1,0:T(8,128)(2,1)S(1)}, u32[]{:S(2)}, u32[]{:S(2)}) collective-permute-start(bf16[1,64,2048]{2,1,0:T(8,128)(2,1)S(1)} %get-tuple-element.17), channel_id=1, source_target_pairs={{0,32},{64,96},{128,160},{192,224},{32,0},{96,64},{160,128},{224,1... | collective-permute-start | bytes 786440 | tf_op jit(solution)/shard_map/ppermute | solution.py:608
  8.7 1.2 %collective-permute-start.2 = (f32[8,2048]{1,0:T(8,128)S(1)}, f32[8,2048]{1,0:T(8,128)S(1)}, u32[]{:S(2)}, u32[]{:S(2)}) collective-permute-start(f32[8,2048]{1,0:T(8,128)S(1)} %get-tuple-element.18), channel_id=1, source_target_pairs={{0,1},{2,3},{4,5},{6,7},{8,9},{10,11},{12,13},{14,15},{16,17},{18,... | collective-permute-start | bytes 196616 | tf_op jit(solution)/shard_map/ppermute | solution.py:608
  9.9 1.2 %collective-permute-start.3 = (f32[8,2048]{1,0:T(8,128)S(1)}, f32[8,2048]{1,0:T(8,128)S(1)}, u32[]{:S(2)}, u32[]{:S(2)}) collective-permute-start(f32[8,2048]{1,0:T(8,128)S(1)} %get-tuple-element.19), channel_id=1, source_target_pairs={{1,2},{3,4},{5,6},{7,8},{9,10},{11,12},{13,14},{15,16},{17,18},{19... | collective-permute-start | bytes 196616 | tf_op jit(solution)/shard_map/ppermute | solution.py:608
  11.1 8.2 %inner_sums.1 = (f32[72,2048]{1,0:T(8,128)S(1)}, f32[8,2048]{1,0:T(8,128)S(1)}, f32[4,8,2048]{2,1,0:T(8,128)S(1)}) custom-call(f32[8]{0:T(128)S(1)} %copy-done.12, f32[8]{0:T(128)S(1)} %copy-done.13, bf16[8,64,2048]{2,1,0:T(8,128)(2,1)S(1)} %copy-done.1, s32[1,8,256]{2,1,0:T(8,128)S(1)} %copy-done.10), custom_call_target="tpu_custom_call" | custom-call | flops 40000000 | bytes 25165824 | tf_op jit(solution)/shard_map/inner_sums/pallas_call | solution.py:241
  19.4 0.0 collective-permute-done.layer_ref
  19.4 0.0 collective-permute-done.1.other_layer_ref
  19.4 2.2 %outer_sums.1 = (f32[72,512]{1,0:T(8,128)S(1)}, f32[72,512]{1,0:T(8,128)S(1)}, f32[72,512]{1,0:T(8,128)S(1)}, bf16[8,160,256]{2,1,0:T(8,128)(2,1)S(1)}) custom-call(f32[8]{0:T(128)S(1)} %copy-done.12, f32[8]{0:T(128)S(1)} %copy-done.13, bf16[8,64,2048]{2,1,0:T(8,128)(2,1)S(1)} %copy-done.1, bf16[1,64,2048]{2,1,0:T(8,128)(2,1)S(1)} %collective-permute-done.layer_ref, ...), custom_call_target="tpu_custom_call" | custom-call | tf_op jit(solution)/shard_map/outer_sums/pallas_call | solution.py:355
  21.6 0.0 copy-start.6
  21.6 0.0 copy-start.7
  21.6 0.0 copy-start.8
  21.7 0.0 copy-start.9
  21.7 8.1 %collective-permute-start.4 = (f32[72,512]{1,0:T(8,128)S(1)}, f32[72,512]{1,0:T(8,128)S(1)}, u32[]{:S(2)}, u32[]{:S(2)}) collective-permute-start(f32[72,512]{1,0:T(8,128)S(1)} %get-tuple-element.24), channel_id=1, source_target_pairs={{0,64},{32,96},{64,0},{96,32},{1,65},{33,97},{65,1},{97,33},{2,66}... | collective-permute-start | bytes 442376 | tf_op jit(solution)/shard_map/ppermute | solution.py:602
  29.8 2.7 %collective-permute-start.6 = (f32[72,512]{1,0:T(8,128)S(1)}, f32[72,512]{1,0:T(8,128)S(1)}, u32[]{:S(2)}, u32[]{:S(2)}) collective-permute-start(f32[72,512]{1,0:T(8,128)S(1)} %get-tuple-element.26), channel_id=1, source_target_pairs={{0,96},{32,0},{64,32},{96,64},{1,97},{33,1},{65,33},{97,65},{2,98}... | collective-permute-start | bytes 442376 | tf_op jit(solution)/shard_map/ppermute | solution.py:602
  32.5 0.2 other_sums.1.a_ref
  32.7 3.9 %collective-permute-done.5.c_ref = f32[72,512]{1,0:T(8,128)S(1)} collective-permute-done((f32[72,512]{1,0:T(8,128)S(1)}, f32[72,512]{1,0:T(8,128)S(1)}, u32[]{:S(2)}, u32[]{:S(2)}) %collective-permute-start.5) | collective-permute-done | bytes 147488 | tf_op jit(solution)/shard_map/ppermute | solution.py:602
  36.6 0.3 turn.1
  37.0 23.0 %all_to_all.10.in_ref = f32[64,1,640]{2,1,0:T(1,128)S(1)} all-to-all(f32[64,1,640]{2,1,0:T(1,128)S(1)} %turn.1), channel_id=1, replica_groups=mesh['zhi'=2,'x'=4,'sky'=32] {'zhi','sky'}, dimensions={0} | all-to-all | bytes 327680 | tf_op jit(solution)/shard_map/all_to_all | solution.py:623
  60.0 1.0 %solve.1 = f32[64,8,128]{2,1,0:T(8,128)S(1)} custom-call(f32[64,1,640]{2,1,0:T(1,128)S(1)} %all_to_all.10.in_ref, f32[32,8,128]{2,1,0:T(8,128)S(1)} %copy-done.7, f32[32,8,128]{2,1,0:T(8,128)S(1)} %copy-done.6, bf16[128,256]{1,0:T(8,128)(2,1)S(1)} %copy-done.9, bf16[128,256]{1,0:T(8,128)(2,1)S(1)} %copy-done.8), custom_call_target="tpu_custom_call" | custom-call | tf_op jit(solution)/shard_map/solve/pallas_call | solution.py:517
  60.9 17.1 %all_to_all.11.in_ref = f32[64,8,128]{2,1,0:T(8,128)S(1)} all-to-all(f32[64,8,128]{2,1,0:T(8,128)S(1)} %solve.1), channel_id=1, replica_groups=mesh['zhi'=2,'x'=4,'sky'=32] {'zhi','sky'}, dimensions={0} | all-to-all | bytes 524288 | tf_op jit(solution)/shard_map/all_to_all | solution.py:625
  78.0 1.2 %back.1 = (f32[128,256]{1,0:T(8,128)S(1)}, f32[128,256]{1,0:T(8,128)S(1)}, f32[128,256]{1,0:T(8,128)S(1)}, f32[128,512]{1,0:T(8,128)S(1)}, f32[128,512]{1,0:T(8,128)S(1)}) custom-call(f32[16]{0:T(128)S(1)} %copy-done.11, f32[64,8,128]{2,1,0:T(8,128)S(1)} %all_to_all.11.in_ref, bf16[4,512,256]{2,1,0:T(8,128)(2,1)S(1)} %copy-done.3, ...), custom_call_target="tpu_custom_call" | custom-call | tf_op jit(solution)/shard_map/back/pallas_call | solution.py:563
  79.2 0.3 collective-permute-start.7
  79.5 0.9 %collective-permute-start.8 = (f32[128,256]{1,0:T(8,128)S(1)}, f32[128,256]{1,0:T(8,128)S(1)}, u32[]{:S(2)}, u32[]{:S(2)}) collective-permute-start(f32[128,256]{1,0:T(8,128)S(1)} %get-tuple-element.30), channel_id=1, source_target_pairs={{0,32},{32,64},{64,96},{96,0},{1,33},{33,65},{65,97},{97,1},{2,34}... | collective-permute-start | bytes 393224 | tf_op jit(solution)/shard_map/ppermute | solution.py:602
  80.4 1.8 %collective-permute-start.9 = (f32[128,256]{1,0:T(8,128)S(1)}, f32[128,256]{1,0:T(8,128)S(1)}, u32[]{:S(2)}, u32[]{:S(2)}) collective-permute-start(f32[128,256]{1,0:T(8,128)S(1)} %get-tuple-element.31), channel_id=1, source_target_pairs={{0,96},{32,0},{64,32},{96,64},{1,97},{33,1},{65,33},{97,65},{2,98}... | collective-permute-start | bytes 393224 | tf_op jit(solution)/shard_map/ppermute | solution.py:602
  82.2 0.8 back_rest.1.a_ref
  83.1 2.7 %collective-permute-done.7.b_ref = f32[128,256]{1,0:T(8,128)S(1)} collective-permute-done((f32[128,256]{1,0:T(8,128)S(1)}, f32[128,256]{1,0:T(8,128)S(1)}, u32[]{:S(2)}, u32[]{:S(2)}) %collective-permute-start.7) | collective-permute-done | bytes 131104 | tf_op jit(solution)/shard_map/ppermute | solution.py:602
  85.7 3.2 %collective-permute-done.8.c_ref = f32[128,256]{1,0:T(8,128)S(1)} collective-permute-done((f32[128,256]{1,0:T(8,128)S(1)}, f32[128,256]{1,0:T(8,128)S(1)}, u32[]{:S(2)}, u32[]{:S(2)}) %collective-permute-start.8) | collective-permute-done | bytes 131104 | tf_op jit(solution)/shard_map/ppermute | solution.py:602
  88.9 0.7 final.1
  (28 shorter events, 0.1 us)
Async XLA Ops:
  0.6 10.5 %copy-start.13 = (f32[8]{0:T(128)S(1)}, f32[8]{0:T(128)}, u32[]{:S(2)}) copy-start(f32[8]{0:T(128)} %high_ref.3) | copy-start | bytes 100
  0.6 10.5 %copy-start.12 = (f32[8]{0:T(128)S(1)}, f32[8]{0:T(128)}, u32[]{:S(2)}) copy-start(f32[8]{0:T(128)} %low_ref.3) | copy-start | bytes 100
  0.7 10.5 %copy-start.10 = (s32[1,8,256]{2,1,0:T(8,128)S(1)}, s32[1,8,256]{2,1,0:T(8,128)}, u32[]{:S(2)}) copy-start(s32[1,8,256]{2,1,0:T(8,128)} %refine_ref.1) | copy-start | bytes 24580
  1.6 17.8 %collective-permute-start = (bf16[1,64,2048]{2,1,0:T(8,128)(2,1)S(1)}, bf16[1,64,2048]{2,1,0:T(8,128)(2,1)S(1)}, u32[]{:S(2)}, u32[]{:S(2)}) collective-permute-start(bf16[1,64,2048]{2,1,0:T(8,128)(2,1)S(1)} %constant_dynamic-slice_fusion), channel_id=1, source_target_pairs={{32,64},{96,128},{160,192},{64,32},{128,96},{192,160},{33,65},{97,... | collective-permute-start | bytes 786440 | tf_op jit(solution)/shard_map/ppermute | solution.py:608
  2.3 1.6 %copy-start = (bf16[8,64,2048]{2,1,0:T(8,128)(2,1)S(1)}, bf16[8,64,2048]{2,1,0:T(8,128)(2,1)}, u32[]{:S(2)}) copy-start(bf16[8,64,2048]{2,1,0:T(8,128)(2,1)} %d_ref.5) | copy-start | bytes 6291460
  3.9 7.2 %copy-start.1 = (bf16[8,64,2048]{2,1,0:T(8,128)(2,1)S(1)}, bf16[8,64,2048]{2,1,0:T(8,128)(2,1)}, u32[]{:S(2)}) copy-start(bf16[8,64,2048]{2,1,0:T(8,128)(2,1)} %d_ref.5) | copy-start | bytes 6291460
  3.9 15.5 %copy-start.4 = (bf16[8,256,256]{2,1,0:T(8,128)(2,1)S(1)}, bf16[8,256,256]{2,1,0:T(8,128)(2,1)}, u32[]{:S(2)}) copy-start(bf16[8,256,256]{2,1,0:T(8,128)(2,1)} %constant.44.clone.low_table) | copy-start | bytes 3145732
  3.9 15.5 %copy-start.5 = (bf16[8,256,256]{2,1,0:T(8,128)(2,1)S(1)}, bf16[8,256,256]{2,1,0:T(8,128)(2,1)}, u32[]{:S(2)}) copy-start(bf16[8,256,256]{2,1,0:T(8,128)(2,1)} %constant.43.clone.high_table) | copy-start | bytes 3145732
  4.1 15.3 %collective-permute-start.1 = (bf16[1,64,2048]{2,1,0:T(8,128)(2,1)S(1)}, bf16[1,64,2048]{2,1,0:T(8,128)(2,1)S(1)}, u32[]{:S(2)}, u32[]{:S(2)}) collective-permute-start(bf16[1,64,2048]{2,1,0:T(8,128)(2,1)S(1)} %get-tuple-element.17), channel_id=1, source_target_pairs={{0,32},{64,96},{128,160},{192,224},{32,0},{96,64},{160,128},{224,1... | collective-permute-start | bytes 786440 | tf_op jit(solution)/shard_map/ppermute | solution.py:608
  8.7 10.7 %collective-permute-start.2 = (f32[8,2048]{1,0:T(8,128)S(1)}, f32[8,2048]{1,0:T(8,128)S(1)}, u32[]{:S(2)}, u32[]{:S(2)}) collective-permute-start(f32[8,2048]{1,0:T(8,128)S(1)} %get-tuple-element.18), channel_id=1, source_target_pairs={{0,1},{2,3},{4,5},{6,7},{8,9},{10,11},{12,13},{14,15},{16,17},{18,... | collective-permute-start | bytes 196616 | tf_op jit(solution)/shard_map/ppermute | solution.py:608
  9.9 9.5 %collective-permute-start.3 = (f32[8,2048]{1,0:T(8,128)S(1)}, f32[8,2048]{1,0:T(8,128)S(1)}, u32[]{:S(2)}, u32[]{:S(2)}) collective-permute-start(f32[8,2048]{1,0:T(8,128)S(1)} %get-tuple-element.19), channel_id=1, source_target_pairs={{1,2},{3,4},{5,6},{7,8},{9,10},{11,12},{13,14},{15,16},{17,18},{19... | collective-permute-start | bytes 196616 | tf_op jit(solution)/shard_map/ppermute | solution.py:608
  21.6 38.3 %copy-start.6 = (f32[32,8,128]{2,1,0:T(8,128)S(1)}, f32[32,8,128]{2,1,0:T(8,128)}, u32[]{:S(2)}) copy-start(f32[32,8,128]{2,1,0:T(8,128)} %constant.46.clone.sin_ref) | copy-start | bytes 393220
  21.6 38.3 %copy-start.7 = (f32[32,8,128]{2,1,0:T(8,128)S(1)}, f32[32,8,128]{2,1,0:T(8,128)}, u32[]{:S(2)}) copy-start(f32[32,8,128]{2,1,0:T(8,128)} %constant.45.clone.cos_ref) | copy-start | bytes 393220
  21.6 38.3 %copy-start.8 = (bf16[128,256]{1,0:T(8,128)(2,1)S(1)}, bf16[128,256]{1,0:T(8,128)(2,1)}, u32[]{:S(2)}) copy-start(bf16[128,256]{1,0:T(8,128)(2,1)} %constant.48.clone.low_table) | copy-start | bytes 196612
  21.7 38.3 %copy-start.9 = (bf16[128,256]{1,0:T(8,128)(2,1)S(1)}, bf16[128,256]{1,0:T(8,128)(2,1)}, u32[]{:S(2)}) copy-start(bf16[128,256]{1,0:T(8,128)(2,1)} %constant.47.clone.high_table) | copy-start | bytes 196612
  21.7 11.1 %collective-permute-start.4 = (f32[72,512]{1,0:T(8,128)S(1)}, f32[72,512]{1,0:T(8,128)S(1)}, u32[]{:S(2)}, u32[]{:S(2)}) collective-permute-start(f32[72,512]{1,0:T(8,128)S(1)} %get-tuple-element.24), channel_id=1, source_target_pairs={{0,64},{32,96},{64,0},{96,32},{1,65},{33,97},{65,1},{97,33},{2,66}... | collective-permute-start | bytes 442376 | tf_op jit(solution)/shard_map/ppermute | solution.py:602
  29.8 6.8 %collective-permute-start.5 = (f32[72,512]{1,0:T(8,128)S(1)}, f32[72,512]{1,0:T(8,128)S(1)}, u32[]{:S(2)}, u32[]{:S(2)}) collective-permute-start(f32[72,512]{1,0:T(8,128)S(1)} %get-tuple-element.25), channel_id=1, source_target_pairs={{0,32},{32,64},{64,96},{96,0},{1,33},{33,65},{65,97},{97,1},{2,34}... | collective-permute-start | bytes 442376 | tf_op jit(solution)/shard_map/ppermute | solution.py:602
  29.8 6.8 %collective-permute-start.6 = (f32[72,512]{1,0:T(8,128)S(1)}, f32[72,512]{1,0:T(8,128)S(1)}, u32[]{:S(2)}, u32[]{:S(2)}) collective-permute-start(f32[72,512]{1,0:T(8,128)S(1)} %get-tuple-element.26), channel_id=1, source_target_pairs={{0,96},{32,0},{64,32},{96,64},{1,97},{33,1},{65,33},{97,65},{2,98}... | collective-permute-start | bytes 442376 | tf_op jit(solution)/shard_map/ppermute | solution.py:602
  32.5 45.5 %copy-start.2 = (bf16[4,512,256]{2,1,0:T(8,128)(2,1)S(1)}, bf16[4,512,256]{2,1,0:T(8,128)(2,1)}, u32[]{:S(2)}) copy-start(bf16[4,512,256]{2,1,0:T(8,128)(2,1)} %constant.51.clone.low_table) | copy-start | bytes 3145732
  32.5 45.5 %copy-start.3 = (bf16[4,512,256]{2,1,0:T(8,128)(2,1)S(1)}, bf16[4,512,256]{2,1,0:T(8,128)(2,1)}, u32[]{:S(2)}) copy-start(bf16[4,512,256]{2,1,0:T(8,128)(2,1)} %constant.50.clone.high_table) | copy-start | bytes 3145732
  32.5 45.5 %copy-start.11 = (f32[16]{0:T(128)S(1)}, f32[16]{0:T(128)}, u32[]{:S(2)}) copy-start(f32[16]{0:T(128)} %constant.49.clone.eighth_ref) | copy-start | bytes 196
  79.2 6.5 %collective-permute-start.7 = (f32[128,256]{1,0:T(8,128)S(1)}, f32[128,256]{1,0:T(8,128)S(1)}, u32[]{:S(2)}, u32[]{:S(2)}) collective-permute-start(f32[128,256]{1,0:T(8,128)S(1)} %get-tuple-element.29), channel_id=1, source_target_pairs={{0,64},{32,96},{64,0},{96,32},{1,65},{33,97},{65,1},{97,33},{2,66}... | collective-permute-start | bytes 393224 | tf_op jit(solution)/shard_map/ppermute | solution.py:602
  79.5 9.4 %collective-permute-start.8 = (f32[128,256]{1,0:T(8,128)S(1)}, f32[128,256]{1,0:T(8,128)S(1)}, u32[]{:S(2)}, u32[]{:S(2)}) collective-permute-start(f32[128,256]{1,0:T(8,128)S(1)} %get-tuple-element.30), channel_id=1, source_target_pairs={{0,32},{32,64},{64,96},{96,0},{1,33},{33,65},{65,97},{97,1},{2,34}... | collective-permute-start | bytes 393224 | tf_op jit(solution)/shard_map/ppermute | solution.py:602
  80.4 8.4 %collective-permute-start.9 = (f32[128,256]{1,0:T(8,128)S(1)}, f32[128,256]{1,0:T(8,128)S(1)}, u32[]{:S(2)}, u32[]{:S(2)}) collective-permute-start(f32[128,256]{1,0:T(8,128)S(1)} %get-tuple-element.31), channel_id=1, source_target_pairs={{0,96},{32,0},{64,32},{96,64},{1,97},{33,1},{65,33},{97,65},{2,98}... | collective-permute-start | bytes 393224 | tf_op jit(solution)/shard_map/ppermute | solution.py:602

commit v7 on v6

--- a/solution.py
+++ b/solution.py
@@ -343,7 +343,11 @@
     for half in range(2):
         tile = 2 * target + half
         value = dot3_stacked(part_ref[tile], high_table[tile], low_table[tile])
-        out_ref[:, 256 * half : 256 * half + 256] = value[:72]
+        for block in (2 * half, 2 * half + 1):
+            part = value[:, 128 * (block % 2) : 128 * (block % 2) + 128]
+            out_ref[ROWS * block : ROWS * block + ROWS] = part[:ROWS]
+            out_ref[4 * ROWS + block : 4 * ROWS + block + 1] = part[ROWS : ROWS + 1]
+            out_ref[4 * ROWS + 4 + block : 4 * ROWS + 5 + block] = part[ROWS + 7 : ROWS + 8]
 
 
 def rest_kernel(part_ref, high_table, low_table, own_ref):
@@ -351,7 +355,7 @@
 
 
 def outer_sums(low, high, density, layers, rows, inner, tables):
-    piece = jax.ShapeDtypeStruct((72, 512), f32)
+    piece = jax.ShapeDtypeStruct((4 * ROWS + 8, 128), f32)
     two, one, three, parts = pl.pallas_call(
         outer_kernel,
         out_shape=(piece, piece, piece, jax.ShapeDtypeStruct((8, 160, 256), bf16)),
@@ -373,22 +377,29 @@
 
 def turn_kernel(a_ref, b_ref, c_ref, d_ref, out_ref):
     total = (a_ref[...] + b_ref[...]) + (c_ref[...] + d_ref[...])
-    turned = jnp.concatenate([total, jnp.zeros((56, 512), f32)], axis=0).T
+    none = jnp.zeros((56, 128), f32)
+    turned = [
+        jnp.concatenate([total[ROWS * block : ROWS * block + ROWS], total[4 * ROWS :], none], axis=0).T
+        for block in range(4)
+    ]
     lane = lax.broadcasted_iota(jnp.int32, (SKY, 128), 1)
     for half in range(2):
         at = slice(SKY * half, SKY * half + SKY)
         spill = jnp.zeros((SKY, 128), f32)
         for c in range(4):
-            first = 256 * half + 64 * c
-            real, imag = turned[first : first + SKY], turned[first + SKY : first + 2 * SKY]
+            block, first = 2 * half + c // 2, 64 * (c % 2)
+            real = turned[block][first : first + SKY]
+            imag = turned[block][first + SKY : first + 2 * SKY]
             out_ref[at, 0, 128 * c : 128 * c + 128] = jnp.where(
                 lane < 64, real, pltpu.roll(imag, 64, 1)
             )
             for sub, part in ((c, real), (4 + c, imag)):
                 up = (128 - 16 * sub) % 128
                 down = (up + 63) % 128
-                spill = jnp.where(lane == up, pltpu.roll(part, (up - 64) % 128, 1), spill)
-                spill = jnp.where(lane == down, pltpu.roll(part, (down - 71) % 128, 1), spill)
+                spill = jnp.where(lane == up, pltpu.roll(part, (up - 64 - block) % 128, 1), spill)
+                spill = jnp.where(
+                    lane == down, pltpu.roll(part, (down - 68 - block) % 128, 1), spill
+                )
         out_ref[at, 0, 512:640] = spill
 
 

time: 89.8 us -> 89.3 us (level)
  no operation moved by 1% of the time
where the time goes in v7:
time: 89.3 us; the launch traced here: 89.1 us
  blocking collectives  39.8 us (45%)
  starting transfers between devices  21.5 us (24%)
  Pallas kernels  14.9 us (17%)
  waiting for transfers between devices  9.47 us (11%)
  local copies, waits for them, and re-layouts  2.62 us (3%)
    all_to_all x1, blocking collectives, body(): pieces = lax.all_to_all(turn(summed), ('zhi', 'sky'), 0, 0, tiled=True)  22.7 us
    all_to_all x1, blocking collectives, body(): pieces = lax.all_to_all(pieces, ('zhi', 'sky'), 0, 0, tiled=True)  17.1 us
    ppermute x6, starting transfers between devices, deliver(): lax.ppermute(pieces[a], 'x', [(i, (i + a) % 4) for i in range(4)])  13.8 us
    ppermute x6, waiting for transfers between devices, deliver(): lax.ppermute(pieces[a], 'x', [(i, (i + a) % 4) for i in range(4)])  9.46 us
    pallas_call x1, Pallas kernels, inner_sums(): pl.pallas_call(inner_kernel, out_shape=(jax.ShapeDtypeStruct((ROWS + 8, N...  8.23 us
    ppermute x4, starting transfers between devices, swap(): return lax.ppermute(array, axes, pairs + [(b, a) for a, b in pairs])  7.67 us
    pallas_call x1, Pallas kernels, outer_sums(): pl.pallas_call(outer_kernel, out_shape=(piece, piece, piece, jax.ShapeDty...  2.18 us
  transfers between devices with their start and end apart: 10, of which 3 were waited for; matrix products, arithmetic and copies ran while one was open for 0% of the time, Pallas kernels for 11%

profile of v7, /device:TPU:1, one launch (start us, length us, event | category | flops | bytes accessed | tf_op | source)
XLA Modules:
  0.0 89.1 jit_solution(11649934973263335068)
XLA Ops:
  0.7 1.0 %constant_dynamic-slice_fusion = bf16[1,64,2048]{2,1,0:T(8,128)(2,1)S(1)} fusion(bf16[8,64,2048]{2,1,0:T(8,128)(2,1)} %d_ref.5, s32[]{:T(128)S(6)} %select_n.13), kind=kLoop, calls=%fused_computation | loop fusion | bytes 524292 | tf_op jit(solution)/shard_map/dynamic_slice | solution.py:622
  1.6 0.7 collective-permute-start
  2.3 0.0 copy-start
  2.3 1.6 %copy-done = bf16[8,64,2048]{2,1,0:T(8,128)(2,1)S(1)} copy-done((bf16[8,64,2048]{2,1,0:T(8,128)(2,1)S(1)}, bf16[8,64,2048]{2,1,0:T(8,128)(2,1)}, u32[]{:S(2)}) %copy-start) | copy-done | bytes 2097176
  3.9 0.2 edge_rows.1
  4.1 4.6 %collective-permute-start.1 = (bf16[1,64,2048]{2,1,0:T(8,128)(2,1)S(1)}, bf16[1,64,2048]{2,1,0:T(8,128)(2,1)S(1)}, u32[]{:S(2)}, u32[]{:S(2)}) collective-permute-start(bf16[1,64,2048]{2,1,0:T(8,128)(2,1)S(1)} %get-tuple-element.17), channel_id=1, source_target_pairs={{0,32},{64,96},{128,160},{192,224},{32,0},{96,64},{160,128},{224,1... | collective-permute-start | bytes 786440 | tf_op jit(solution)/shard_map/ppermute | solution.py:619
  8.7 1.2 %collective-permute-start.2 = (f32[8,2048]{1,0:T(8,128)S(1)}, f32[8,2048]{1,0:T(8,128)S(1)}, u32[]{:S(2)}, u32[]{:S(2)}) collective-permute-start(f32[8,2048]{1,0:T(8,128)S(1)} %get-tuple-element.18), channel_id=1, source_target_pairs={{0,1},{2,3},{4,5},{6,7},{8,9},{10,11},{12,13},{14,15},{16,17},{18,... | collective-permute-start | bytes 196616 | tf_op jit(solution)/shard_map/ppermute | solution.py:619
  9.9 1.2 %collective-permute-start.3 = (f32[8,2048]{1,0:T(8,128)S(1)}, f32[8,2048]{1,0:T(8,128)S(1)}, u32[]{:S(2)}, u32[]{:S(2)}) collective-permute-start(f32[8,2048]{1,0:T(8,128)S(1)} %get-tuple-element.19), channel_id=1, source_target_pairs={{1,2},{3,4},{5,6},{7,8},{9,10},{11,12},{13,14},{15,16},{17,18},{19... | collective-permute-start | bytes 196616 | tf_op jit(solution)/shard_map/ppermute | solution.py:619
  11.1 8.2 %inner_sums.1 = (f32[72,2048]{1,0:T(8,128)S(1)}, f32[8,2048]{1,0:T(8,128)S(1)}, f32[4,8,2048]{2,1,0:T(8,128)S(1)}) custom-call(f32[8]{0:T(128)S(1)} %copy-done.12, f32[8]{0:T(128)S(1)} %copy-done.13, bf16[8,64,2048]{2,1,0:T(8,128)(2,1)S(1)} %copy-done.1, s32[1,8,256]{2,1,0:T(8,128)S(1)} %copy-done.10), custom_call_target="tpu_custom_call" | custom-call | flops 40000000 | bytes 25165824 | tf_op jit(solution)/shard_map/inner_sums/pallas_call | solution.py:241
  19.4 0.0 collective-permute-done.2.row_ref
  19.4 0.0 collective-permute-done.1.other_layer_ref
  19.4 2.2 %outer_sums.1 = (f32[264,128]{1,0:T(8,128)S(1)}, f32[264,128]{1,0:T(8,128)S(1)}, f32[264,128]{1,0:T(8,128)S(1)}, bf16[8,160,256]{2,1,0:T(8,128)(2,1)S(1)}) custom-call(f32[8]{0:T(128)S(1)} %copy-done.12, f32[8]{0:T(128)S(1)} %copy-done.13, bf16[8,64,2048]{2,1,0:T(8,128)(2,1)S(1)} %copy-done.1, bf16[1,64,2048]{2,1,0:T(8,128)(2,1)S(1)} %collective-permute-done.layer_ref, ...), custom_call_target="tpu_custom_call" | custom-call | tf_op jit(solution)/shard_map/outer_sums/pallas_call | solution.py:359
  21.6 0.0 copy-start.6
  21.6 0.0 copy-start.7
  21.6 0.0 copy-start.8
  21.7 0.0 copy-start.9
  21.7 8.1 %collective-permute-start.4 = (f32[264,128]{1,0:T(8,128)S(1)}, f32[264,128]{1,0:T(8,128)S(1)}, u32[]{:S(2)}, u32[]{:S(2)}) collective-permute-start(f32[264,128]{1,0:T(8,128)S(1)} %get-tuple-element.24), channel_id=1, source_target_pairs={{0,64},{32,96},{64,0},{96,32},{1,65},{33,97},{65,1},{97,33},{2,66}... | collective-permute-start | bytes 405512 | tf_op jit(solution)/shard_map/ppermute | solution.py:613
  29.8 2.7 %collective-permute-start.6 = (f32[264,128]{1,0:T(8,128)S(1)}, f32[264,128]{1,0:T(8,128)S(1)}, u32[]{:S(2)}, u32[]{:S(2)}) collective-permute-start(f32[264,128]{1,0:T(8,128)S(1)} %get-tuple-element.26), channel_id=1, source_target_pairs={{0,96},{32,0},{64,32},{96,64},{1,97},{33,1},{65,33},{97,65},{2,98}... | collective-permute-start | bytes 405512 | tf_op jit(solution)/shard_map/ppermute | solution.py:613
  32.5 0.2 other_sums.1.a_ref
  32.7 3.6 %collective-permute-done.5.c_ref = f32[264,128]{1,0:T(8,128)S(1)} collective-permute-done((f32[264,128]{1,0:T(8,128)S(1)}, f32[264,128]{1,0:T(8,128)S(1)}, u32[]{:S(2)}, u32[]{:S(2)}) %collective-permute-start.5) | collective-permute-done | bytes 135200 | tf_op jit(solution)/shard_map/ppermute | solution.py:613
  36.3 0.3 turn.1
  36.7 22.7 %all_to_all.10.in_ref = f32[64,1,640]{2,1,0:T(1,128)S(1)} all-to-all(f32[64,1,640]{2,1,0:T(1,128)S(1)} %turn.1), channel_id=1, replica_groups=mesh['zhi'=2,'x'=4,'sky'=32] {'zhi','sky'}, dimensions={0} | all-to-all | bytes 327680 | tf_op jit(solution)/shard_map/all_to_all | solution.py:634
  59.4 1.0 %solve.1 = f32[64,8,128]{2,1,0:T(8,128)S(1)} custom-call(f32[64,1,640]{2,1,0:T(1,128)S(1)} %all_to_all.10.in_ref, f32[32,8,128]{2,1,0:T(8,128)S(1)} %copy-done.7, f32[32,8,128]{2,1,0:T(8,128)S(1)} %copy-done.6, bf16[128,256]{1,0:T(8,128)(2,1)S(1)} %copy-done.9, bf16[128,256]{1,0:T(8,128)(2,1)S(1)} %copy-done.8), custom_call_target="tpu_custom_call" | custom-call | tf_op jit(solution)/shard_map/solve/pallas_call | solution.py:528
  60.4 17.1 %all_to_all.11.in_ref = f32[64,8,128]{2,1,0:T(8,128)S(1)} all-to-all(f32[64,8,128]{2,1,0:T(8,128)S(1)} %solve.1), channel_id=1, replica_groups=mesh['zhi'=2,'x'=4,'sky'=32] {'zhi','sky'}, dimensions={0} | all-to-all | bytes 524288 | tf_op jit(solution)/shard_map/all_to_all | solution.py:636
  77.5 1.2 %back.1 = (f32[128,256]{1,0:T(8,128)S(1)}, f32[128,256]{1,0:T(8,128)S(1)}, f32[128,256]{1,0:T(8,128)S(1)}, f32[128,512]{1,0:T(8,128)S(1)}, f32[128,512]{1,0:T(8,128)S(1)}) custom-call(f32[16]{0:T(128)S(1)} %copy-done.11, f32[64,8,128]{2,1,0:T(8,128)S(1)} %all_to_all.11.in_ref, bf16[4,512,256]{2,1,0:T(8,128)(2,1)S(1)} %copy-done.3, ...), custom_call_target="tpu_custom_call" | custom-call | tf_op jit(solution)/shard_map/back/pallas_call | solution.py:574
  78.7 0.3 collective-permute-start.7
  79.0 0.9 %collective-permute-start.8 = (f32[128,256]{1,0:T(8,128)S(1)}, f32[128,256]{1,0:T(8,128)S(1)}, u32[]{:S(2)}, u32[]{:S(2)}) collective-permute-start(f32[128,256]{1,0:T(8,128)S(1)} %get-tuple-element.30), channel_id=1, source_target_pairs={{0,32},{32,64},{64,96},{96,0},{1,33},{33,65},{65,97},{97,1},{2,34}... | collective-permute-start | bytes 393224 | tf_op jit(solution)/shard_map/ppermute | solution.py:613
  79.9 1.8 %collective-permute-start.9 = (f32[128,256]{1,0:T(8,128)S(1)}, f32[128,256]{1,0:T(8,128)S(1)}, u32[]{:S(2)}, u32[]{:S(2)}) collective-permute-start(f32[128,256]{1,0:T(8,128)S(1)} %get-tuple-element.31), channel_id=1, source_target_pairs={{0,96},{32,0},{64,32},{96,64},{1,97},{33,1},{65,33},{97,65},{2,98}... | collective-permute-start | bytes 393224 | tf_op jit(solution)/shard_map/ppermute | solution.py:613
  81.7 0.8 back_rest.1.a_ref
  82.6 2.7 %collective-permute-done.7.b_ref = f32[128,256]{1,0:T(8,128)S(1)} collective-permute-done((f32[128,256]{1,0:T(8,128)S(1)}, f32[128,256]{1,0:T(8,128)S(1)}, u32[]{:S(2)}, u32[]{:S(2)}) %collective-permute-start.7) | collective-permute-done | bytes 131104 | tf_op jit(solution)/shard_map/ppermute | solution.py:613
  85.2 3.2 %collective-permute-done.8.c_ref = f32[128,256]{1,0:T(8,128)S(1)} collective-permute-done((f32[128,256]{1,0:T(8,128)S(1)}, f32[128,256]{1,0:T(8,128)S(1)}, u32[]{:S(2)}, u32[]{:S(2)}) %collective-permute-start.8) | collective-permute-done | bytes 131104 | tf_op jit(solution)/shard_map/ppermute | solution.py:613
  88.4 0.7 final.1
  (28 shorter events, 0.1 us)
Async XLA Ops:
  0.6 10.5 %copy-start.13 = (f32[8]{0:T(128)S(1)}, f32[8]{0:T(128)}, u32[]{:S(2)}) copy-start(f32[8]{0:T(128)} %high_ref.3) | copy-start | bytes 100
  0.6 10.5 %copy-start.12 = (f32[8]{0:T(128)S(1)}, f32[8]{0:T(128)}, u32[]{:S(2)}) copy-start(f32[8]{0:T(128)} %low_ref.3) | copy-start | bytes 100
  0.7 10.5 %copy-start.10 = (s32[1,8,256]{2,1,0:T(8,128)S(1)}, s32[1,8,256]{2,1,0:T(8,128)}, u32[]{:S(2)}) copy-start(s32[1,8,256]{2,1,0:T(8,128)} %refine_ref.1) | copy-start | bytes 24580
  1.6 17.8 %collective-permute-start = (bf16[1,64,2048]{2,1,0:T(8,128)(2,1)S(1)}, bf16[1,64,2048]{2,1,0:T(8,128)(2,1)S(1)}, u32[]{:S(2)}, u32[]{:S(2)}) collective-permute-start(bf16[1,64,2048]{2,1,0:T(8,128)(2,1)S(1)} %constant_dynamic-slice_fusion), channel_id=1, source_target_pairs={{32,64},{96,128},{160,192},{64,32},{128,96},{192,160},{33,65},{97,... | collective-permute-start | bytes 786440 | tf_op jit(solution)/shard_map/ppermute | solution.py:619
  2.3 1.6 %copy-start = (bf16[8,64,2048]{2,1,0:T(8,128)(2,1)S(1)}, bf16[8,64,2048]{2,1,0:T(8,128)(2,1)}, u32[]{:S(2)}) copy-start(bf16[8,64,2048]{2,1,0:T(8,128)(2,1)} %d_ref.5) | copy-start | bytes 6291460
  3.9 7.2 %copy-start.1 = (bf16[8,64,2048]{2,1,0:T(8,128)(2,1)S(1)}, bf16[8,64,2048]{2,1,0:T(8,128)(2,1)}, u32[]{:S(2)}) copy-start(bf16[8,64,2048]{2,1,0:T(8,128)(2,1)} %d_ref.5) | copy-start | bytes 6291460
  3.9 15.5 %copy-start.4 = (bf16[8,256,256]{2,1,0:T(8,128)(2,1)S(1)}, bf16[8,256,256]{2,1,0:T(8,128)(2,1)}, u32[]{:S(2)}) copy-start(bf16[8,256,256]{2,1,0:T(8,128)(2,1)} %constant.44.clone.low_table) | copy-start | bytes 3145732
  3.9 15.5 %copy-start.5 = (bf16[8,256,256]{2,1,0:T(8,128)(2,1)S(1)}, bf16[8,256,256]{2,1,0:T(8,128)(2,1)}, u32[]{:S(2)}) copy-start(bf16[8,256,256]{2,1,0:T(8,128)(2,1)} %constant.43.clone.high_table) | copy-start | bytes 3145732
  4.1 15.3 %collective-permute-start.1 = (bf16[1,64,2048]{2,1,0:T(8,128)(2,1)S(1)}, bf16[1,64,2048]{2,1,0:T(8,128)(2,1)S(1)}, u32[]{:S(2)}, u32[]{:S(2)}) collective-permute-start(bf16[1,64,2048]{2,1,0:T(8,128)(2,1)S(1)} %get-tuple-element.17), channel_id=1, source_target_pairs={{0,32},{64,96},{128,160},{192,224},{32,0},{96,64},{160,128},{224,1... | collective-permute-start | bytes 786440 | tf_op jit(solution)/shard_map/ppermute | solution.py:619
  8.7 10.7 %collective-permute-start.2 = (f32[8,2048]{1,0:T(8,128)S(1)}, f32[8,2048]{1,0:T(8,128)S(1)}, u32[]{:S(2)}, u32[]{:S(2)}) collective-permute-start(f32[8,2048]{1,0:T(8,128)S(1)} %get-tuple-element.18), channel_id=1, source_target_pairs={{0,1},{2,3},{4,5},{6,7},{8,9},{10,11},{12,13},{14,15},{16,17},{18,... | collective-permute-start | bytes 196616 | tf_op jit(solution)/shard_map/ppermute | solution.py:619
  9.9 9.5 %collective-permute-start.3 = (f32[8,2048]{1,0:T(8,128)S(1)}, f32[8,2048]{1,0:T(8,128)S(1)}, u32[]{:S(2)}, u32[]{:S(2)}) collective-permute-start(f32[8,2048]{1,0:T(8,128)S(1)} %get-tuple-element.19), channel_id=1, source_target_pairs={{1,2},{3,4},{5,6},{7,8},{9,10},{11,12},{13,14},{15,16},{17,18},{19... | collective-permute-start | bytes 196616 | tf_op jit(solution)/shard_map/ppermute | solution.py:619
  21.6 37.8 %copy-start.6 = (f32[32,8,128]{2,1,0:T(8,128)S(1)}, f32[32,8,128]{2,1,0:T(8,128)}, u32[]{:S(2)}) copy-start(f32[32,8,128]{2,1,0:T(8,128)} %constant.46.clone.sin_ref) | copy-start | bytes 393220
  21.6 37.8 %copy-start.7 = (f32[32,8,128]{2,1,0:T(8,128)S(1)}, f32[32,8,128]{2,1,0:T(8,128)}, u32[]{:S(2)}) copy-start(f32[32,8,128]{2,1,0:T(8,128)} %constant.45.clone.cos_ref) | copy-start | bytes 393220
  21.6 37.8 %copy-start.8 = (bf16[128,256]{1,0:T(8,128)(2,1)S(1)}, bf16[128,256]{1,0:T(8,128)(2,1)}, u32[]{:S(2)}) copy-start(bf16[128,256]{1,0:T(8,128)(2,1)} %constant.48.clone.low_table) | copy-start | bytes 196612
  21.7 37.8 %copy-start.9 = (bf16[128,256]{1,0:T(8,128)(2,1)S(1)}, bf16[128,256]{1,0:T(8,128)(2,1)}, u32[]{:S(2)}) copy-start(bf16[128,256]{1,0:T(8,128)(2,1)} %constant.47.clone.high_table) | copy-start | bytes 196612
  21.7 11.1 %collective-permute-start.4 = (f32[264,128]{1,0:T(8,128)S(1)}, f32[264,128]{1,0:T(8,128)S(1)}, u32[]{:S(2)}, u32[]{:S(2)}) collective-permute-start(f32[264,128]{1,0:T(8,128)S(1)} %get-tuple-element.24), channel_id=1, source_target_pairs={{0,64},{32,96},{64,0},{96,32},{1,65},{33,97},{65,1},{97,33},{2,66}... | collective-permute-start | bytes 405512 | tf_op jit(solution)/shard_map/ppermute | solution.py:613
  29.8 6.5 %collective-permute-start.5 = (f32[264,128]{1,0:T(8,128)S(1)}, f32[264,128]{1,0:T(8,128)S(1)}, u32[]{:S(2)}, u32[]{:S(2)}) collective-permute-start(f32[264,128]{1,0:T(8,128)S(1)} %get-tuple-element.25), channel_id=1, source_target_pairs={{0,32},{32,64},{64,96},{96,0},{1,33},{33,65},{65,97},{97,1},{2,34}... | collective-permute-start | bytes 405512 | tf_op jit(solution)/shard_map/ppermute | solution.py:613
  29.8 6.5 %collective-permute-start.6 = (f32[264,128]{1,0:T(8,128)S(1)}, f32[264,128]{1,0:T(8,128)S(1)}, u32[]{:S(2)}, u32[]{:S(2)}) collective-permute-start(f32[264,128]{1,0:T(8,128)S(1)} %get-tuple-element.26), channel_id=1, source_target_pairs={{0,96},{32,0},{64,32},{96,64},{1,97},{33,1},{65,33},{97,65},{2,98}... | collective-permute-start | bytes 405512 | tf_op jit(solution)/shard_map/ppermute | solution.py:613
  32.5 45.0 %copy-start.2 = (bf16[4,512,256]{2,1,0:T(8,128)(2,1)S(1)}, bf16[4,512,256]{2,1,0:T(8,128)(2,1)}, u32[]{:S(2)}) copy-start(bf16[4,512,256]{2,1,0:T(8,128)(2,1)} %constant.51.clone.low_table) | copy-start | bytes 3145732
  32.5 45.0 %copy-start.3 = (bf16[4,512,256]{2,1,0:T(8,128)(2,1)S(1)}, bf16[4,512,256]{2,1,0:T(8,128)(2,1)}, u32[]{:S(2)}) copy-start(bf16[4,512,256]{2,1,0:T(8,128)(2,1)} %constant.50.clone.high_table) | copy-start | bytes 3145732
  32.5 45.0 %copy-start.11 = (f32[16]{0:T(128)S(1)}, f32[16]{0:T(128)}, u32[]{:S(2)}) copy-start(f32[16]{0:T(128)} %constant.49.clone.eighth_ref) | copy-start | bytes 196
  78.7 6.5 %collective-permute-start.7 = (f32[128,256]{1,0:T(8,128)S(1)}, f32[128,256]{1,0:T(8,128)S(1)}, u32[]{:S(2)}, u32[]{:S(2)}) collective-permute-start(f32[128,256]{1,0:T(8,128)S(1)} %get-tuple-element.29), channel_id=1, source_target_pairs={{0,64},{32,96},{64,0},{96,32},{1,65},{33,97},{65,1},{97,33},{2,66}... | collective-permute-start | bytes 393224 | tf_op jit(solution)/shard_map/ppermute | solution.py:613
  79.0 9.4 %collective-permute-start.8 = (f32[128,256]{1,0:T(8,128)S(1)}, f32[128,256]{1,0:T(8,128)S(1)}, u32[]{:S(2)}, u32[]{:S(2)}) collective-permute-start(f32[128,256]{1,0:T(8,128)S(1)} %get-tuple-element.30), channel_id=1, source_target_pairs={{0,32},{32,64},{64,96},{96,0},{1,33},{33,65},{65,97},{97,1},{2,34}... | collective-permute-start | bytes 393224 | tf_op jit(solution)/shard_map/ppermute | solution.py:613
  79.9 8.5 %collective-permute-start.9 = (f32[128,256]{1,0:T(8,128)S(1)}, f32[128,256]{1,0:T(8,128)S(1)}, u32[]{:S(2)}, u32[]{:S(2)}) collective-permute-start(f32[128,256]{1,0:T(8,128)S(1)} %get-tuple-element.31), channel_id=1, source_target_pairs={{0,96},{32,0},{64,32},{96,64},{1,97},{33,1},{65,33},{97,65},{2,98}... | collective-permute-start | bytes 393224 | tf_op jit(solution)/shard_map/ppermute | solution.py:613

commit v8 on v7

--- a/solution.py
+++ b/solution.py
@@ -122,8 +122,10 @@
 SM = pl.BlockSpec(memory_space=pltpu.SMEM)
 
 
-def rows_kernel(d_ref, near_ref, far_ref, layer_ref):
-    layer_ref[0] = jnp.where(lax.axis_index("x") % 2 == 1, d_ref[0], d_ref[LAYERS - 1])
+def rows_kernel(d_ref, near_ref, far_ref, layer_ref, other_layer_ref):
+    odd = lax.axis_index("x") % 2
+    layer_ref[0] = d_ref[(LAYERS - 1) * odd]
+    other_layer_ref[0] = d_ref[(LAYERS - 1) * (1 - odd)]
     even = lax.axis_index("sky") % 2 == 0
     for z in range(LAYERS):
         first = d_ref[z, 0:16, :].astype(f32)[0:1]
@@ -136,9 +138,9 @@
     shape = jax.ShapeDtypeStruct((LAYERS, N), f32)
     return pl.pallas_call(
         rows_kernel,
-        out_shape=(shape, shape, jax.ShapeDtypeStruct((1, ROWS, N), bf16)),
+        out_shape=(shape, shape) + (jax.ShapeDtypeStruct((1, ROWS, N), bf16),) * 2,
         in_specs=[VM],
-        out_specs=(VM, VM, VM),
+        out_specs=(VM,) * 4,
         compiler_params=limit(8),
         name="edge_rows",
     )(density)
@@ -258,6 +260,7 @@
     low_ref,
     high_ref,
     d_ref,
+    cross_ref,
     layer_ref,
     other_layer_ref,
     row_ref,
@@ -276,7 +279,9 @@
     v0, v1 = d_ref[0].astype(f32), d_ref[1].astype(f32)
     v6, v7 = d_ref[6].astype(f32), d_ref[7].astype(f32)
     odd = los % 2 == 1
-    one, other = layer_ref[0].astype(f32), other_layer_ref[0].astype(f32)
+    crossing = jnp.logical_or(los == 3, los == 4)
+    one = jnp.where(crossing, cross_ref[0], layer_ref[0]).astype(f32)
+    other = other_layer_ref[0].astype(f32)
     below = jnp.where(los == 0, v0, jnp.where(odd, other, one))
     above = jnp.where(los == 7, v7, jnp.where(odd, one, other))
     slope0 = 0.125 * (high_ref[0] - low_ref[0])
@@ -359,7 +364,7 @@
     two, one, three, parts = pl.pallas_call(
         outer_kernel,
         out_shape=(piece, piece, piece, jax.ShapeDtypeStruct((8, 160, 256), bf16)),
-        in_specs=[SM, SM] + [VM] * 10,
+        in_specs=[SM, SM] + [VM] * 11,
         out_specs=(VM,) * 4,
         compiler_params=limit(32),
         name="outer_sums",
@@ -619,16 +624,17 @@
         return lax.ppermute(array, axes, pairs + [(b, a) for a, b in pairs])
 
     odd = lax.axis_index("x") % 2 == 1
-    layer = lax.dynamic_slice_in_dim(density, jnp.where(odd, LAYERS - 1, 0), 1, 0)
-    layer = swap(layer, LOS, [(1, 2), (3, 4), (5, 6)])
-    row, other_row, other_layer = edge_rows(density)
+    cross = lax.dynamic_slice_in_dim(density, jnp.where(odd, LAYERS - 1, 0), 1, 0)
+    cross = swap(cross, LOS, [(3, 4)])
+    row, other_row, layer, other_layer = edge_rows(density)
+    layer = swap(layer, LOS, [(1, 2), (5, 6)])
     other_layer = swap(other_layer, LOS, [(0, 1), (2, 3), (4, 5), (6, 7)])
     row = swap(row, "sky", [(i, i + 1) for i in range(0, SKY, 2)])
     other_row = swap(other_row, "sky", [(i, (i + 1) % SKY) for i in range(1, SKY, 2)])
     inner = inner_sums(weight_low, weight_high, density, refine)
     tables = halves(forward_table())
     summed = outer_sums(
-        weight_low, weight_high, density, (layer, other_layer), (row, other_row), inner, tables
+        weight_low, weight_high, density, (cross, layer, other_layer), (row, other_row), inner, tables
     )
     summed = deliver(summed)
     pieces = lax.all_to_all(turn(summed), ("zhi", "sky"), 0, 0, tiled=True)

time: 89.3 us -> 89.3 us (level)
    ppermute x4 -> x5, starting transfers between devices: 7.67 us -> 8.61 us  [swap(): return lax.ppermute(array, axes, pairs + [(b, a) for a, b in pairs])]
  transfers between devices with their start and end apart: 10 -> 11, of which waited for: 3 -> 3; matrix products, arithmetic and copies ran while one was open for 0% -> 0% of each run, Pallas kernels for 11% -> 11%
where the time goes in v8:
time: 89.3 us; the launch traced here: 89.1 us
  blocking collectives  39 us (44%)
  starting transfers between devices  22.3 us (25%)
  Pallas kernels  14.9 us (17%)
  waiting for transfers between devices  9.47 us (11%)
  local copies, waits for them, and re-layouts  2.62 us (3%)
    all_to_all x1, blocking collectives, body(): pieces = lax.all_to_all(turn(summed), ('zhi', 'sky'), 0, 0, tiled=True)  21.9 us
    all_to_all x1, blocking collectives, body(): pieces = lax.all_to_all(pieces, ('zhi', 'sky'), 0, 0, tiled=True)  17.1 us
    ppermute x6, starting transfers between devices, deliver(): lax.ppermute(pieces[a], 'x', [(i, (i + a) % 4) for i in range(4)])  13.7 us
    ppermute x6, waiting for transfers between devices, deliver(): lax.ppermute(pieces[a], 'x', [(i, (i + a) % 4) for i in range(4)])  9.46 us
    ppermute x5, starting transfers between devices, swap(): return lax.ppermute(array, axes, pairs + [(b, a) for a, b in pairs])  8.61 us
    pallas_call x1, Pallas kernels, inner_sums(): pl.pallas_call(inner_kernel, out_shape=(jax.ShapeDtypeStruct((ROWS + 8, N...  8.23 us
    pallas_call x1, Pallas kernels, outer_sums(): pl.pallas_call(outer_kernel, out_shape=(piece, piece, piece, jax.ShapeDty...  2.17 us
  transfers between devices with their start and end apart: 11, of which 3 were waited for; matrix products, arithmetic and copies ran while one was open for 0% of the time, Pallas kernels for 11%

profile of v8, /device:TPU:1, one launch (start us, length us, event | category | flops | bytes accessed | tf_op | source)
XLA Modules:
  0.0 89.1 jit_solution(535676844530216474)
XLA Ops:
  0.7 1.0 %constant_dynamic-slice_fusion = bf16[1,64,2048]{2,1,0:T(8,128)(2,1)S(1)} fusion(bf16[8,64,2048]{2,1,0:T(8,128)(2,1)} %d_ref.5, s32[]{:T(128)S(6)} %select_n.13), kind=kLoop, calls=%fused_computation | loop fusion | bytes 524292 | tf_op jit(solution)/shard_map/dynamic_slice | solution.py:627
  1.6 0.7 collective-permute-start
  2.3 0.0 copy-start
  2.3 1.6 %copy-done = bf16[8,64,2048]{2,1,0:T(8,128)(2,1)S(1)} copy-done((bf16[8,64,2048]{2,1,0:T(8,128)(2,1)S(1)}, bf16[8,64,2048]{2,1,0:T(8,128)(2,1)}, u32[]{:S(2)}) %copy-start) | copy-done | bytes 2097176
  3.9 0.2 edge_rows.1
  4.1 0.8 collective-permute-start.1
  4.9 4.7 %collective-permute-start.2 = (bf16[1,64,2048]{2,1,0:T(8,128)(2,1)S(1)}, bf16[1,64,2048]{2,1,0:T(8,128)(2,1)S(1)}, u32[]{:S(2)}, u32[]{:S(2)}) collective-permute-start(bf16[1,64,2048]{2,1,0:T(8,128)(2,1)S(1)} %get-tuple-element.19), channel_id=1, source_target_pairs={{0,32},{64,96},{128,160},{192,224},{32,0},{96,64},{160,128},{224,1... | collective-permute-start | bytes 786440 | tf_op jit(solution)/shard_map/ppermute | solution.py:624
  9.6 1.2 %collective-permute-start.3 = (f32[8,2048]{1,0:T(8,128)S(1)}, f32[8,2048]{1,0:T(8,128)S(1)}, u32[]{:S(2)}, u32[]{:S(2)}) collective-permute-start(f32[8,2048]{1,0:T(8,128)S(1)} %get-tuple-element.20), channel_id=1, source_target_pairs={{0,1},{2,3},{4,5},{6,7},{8,9},{10,11},{12,13},{14,15},{16,17},{18,... | collective-permute-start | bytes 196616 | tf_op jit(solution)/shard_map/ppermute | solution.py:624
  10.9 1.2 %collective-permute-start.4 = (f32[8,2048]{1,0:T(8,128)S(1)}, f32[8,2048]{1,0:T(8,128)S(1)}, u32[]{:S(2)}, u32[]{:S(2)}) collective-permute-start(f32[8,2048]{1,0:T(8,128)S(1)} %get-tuple-element.21), channel_id=1, source_target_pairs={{1,2},{3,4},{5,6},{7,8},{9,10},{11,12},{13,14},{15,16},{17,18},{19... | collective-permute-start | bytes 196616 | tf_op jit(solution)/shard_map/ppermute | solution.py:624
  12.1 8.2 %inner_sums.1 = (f32[72,2048]{1,0:T(8,128)S(1)}, f32[8,2048]{1,0:T(8,128)S(1)}, f32[4,8,2048]{2,1,0:T(8,128)S(1)}) custom-call(f32[8]{0:T(128)S(1)} %copy-done.12, f32[8]{0:T(128)S(1)} %copy-done.13, bf16[8,64,2048]{2,1,0:T(8,128)(2,1)S(1)} %copy-done.1, s32[1,8,256]{2,1,0:T(8,128)S(1)} %copy-done.10), custom_call_target="tpu_custom_call" | custom-call | flops 40000000 | bytes 25165824 | tf_op jit(solution)/shard_map/inner_sums/pallas_call | solution.py:243
  20.3 0.0 collective-permute-done.3.row_ref
  20.4 2.2 %outer_sums.1 = (f32[264,128]{1,0:T(8,128)S(1)}, f32[264,128]{1,0:T(8,128)S(1)}, f32[264,128]{1,0:T(8,128)S(1)}, bf16[8,160,256]{2,1,0:T(8,128)(2,1)S(1)}) custom-call(f32[8]{0:T(128)S(1)} %copy-done.12, f32[8]{0:T(128)S(1)} %copy-done.13, bf16[8,64,2048]{2,1,0:T(8,128)(2,1)S(1)} %copy-done.1, bf16[1,64,2048]{2,1,0:T(8,128)(2,1)S(1)} %collective-permute-done.cross_ref, ...), custom_call_target="tpu_custom_call" | custom-call | tf_op jit(solution)/shard_map/outer_sums/pallas_call | solution.py:364
  22.6 0.0 copy-start.6
  22.6 0.0 copy-start.7
  22.6 0.0 copy-start.8
  22.6 0.0 copy-start.9
  22.6 8.0 %collective-permute-start.5 = (f32[264,128]{1,0:T(8,128)S(1)}, f32[264,128]{1,0:T(8,128)S(1)}, u32[]{:S(2)}, u32[]{:S(2)}) collective-permute-start(f32[264,128]{1,0:T(8,128)S(1)} %get-tuple-element.26), channel_id=1, source_target_pairs={{0,64},{32,96},{64,0},{96,32},{1,65},{33,97},{65,1},{97,33},{2,66}... | collective-permute-start | bytes 405512 | tf_op jit(solution)/shard_map/ppermute | solution.py:618
  30.6 2.7 %collective-permute-start.7 = (f32[264,128]{1,0:T(8,128)S(1)}, f32[264,128]{1,0:T(8,128)S(1)}, u32[]{:S(2)}, u32[]{:S(2)}) collective-permute-start(f32[264,128]{1,0:T(8,128)S(1)} %get-tuple-element.28), channel_id=1, source_target_pairs={{0,96},{32,0},{64,32},{96,64},{1,97},{33,1},{65,33},{97,65},{2,98}... | collective-permute-start | bytes 405512 | tf_op jit(solution)/shard_map/ppermute | solution.py:618
  33.3 0.2 other_sums.1.a_ref
  33.6 3.6 %collective-permute-done.6.c_ref = f32[264,128]{1,0:T(8,128)S(1)} collective-permute-done((f32[264,128]{1,0:T(8,128)S(1)}, f32[264,128]{1,0:T(8,128)S(1)}, u32[]{:S(2)}, u32[]{:S(2)}) %collective-permute-start.6) | collective-permute-done | bytes 135200 | tf_op jit(solution)/shard_map/ppermute | solution.py:618
  37.2 0.3 turn.1
  37.5 21.9 %all_to_all.10.in_ref = f32[64,1,640]{2,1,0:T(1,128)S(1)} all-to-all(f32[64,1,640]{2,1,0:T(1,128)S(1)} %turn.1), channel_id=1, replica_groups=mesh['zhi'=2,'x'=4,'sky'=32] {'zhi','sky'}, dimensions={0} | all-to-all | bytes 327680 | tf_op jit(solution)/shard_map/all_to_all | solution.py:640
  59.4 1.0 %solve.1 = f32[64,8,128]{2,1,0:T(8,128)S(1)} custom-call(f32[64,1,640]{2,1,0:T(1,128)S(1)} %all_to_all.10.in_ref, f32[32,8,128]{2,1,0:T(8,128)S(1)} %copy-done.7, f32[32,8,128]{2,1,0:T(8,128)S(1)} %copy-done.6, bf16[128,256]{1,0:T(8,128)(2,1)S(1)} %copy-done.9, bf16[128,256]{1,0:T(8,128)(2,1)S(1)} %copy-done.8), custom_call_target="tpu_custom_call" | custom-call | tf_op jit(solution)/shard_map/solve/pallas_call | solution.py:533
  60.4 17.1 %all_to_all.11.in_ref = f32[64,8,128]{2,1,0:T(8,128)S(1)} all-to-all(f32[64,8,128]{2,1,0:T(8,128)S(1)} %solve.1), channel_id=1, replica_groups=mesh['zhi'=2,'x'=4,'sky'=32] {'zhi','sky'}, dimensions={0} | all-to-all | bytes 524288 | tf_op jit(solution)/shard_map/all_to_all | solution.py:642
  77.5 1.2 %back.1 = (f32[128,256]{1,0:T(8,128)S(1)}, f32[128,256]{1,0:T(8,128)S(1)}, f32[128,256]{1,0:T(8,128)S(1)}, f32[128,512]{1,0:T(8,128)S(1)}, f32[128,512]{1,0:T(8,128)S(1)}) custom-call(f32[16]{0:T(128)S(1)} %copy-done.11, f32[64,8,128]{2,1,0:T(8,128)S(1)} %all_to_all.11.in_ref, bf16[4,512,256]{2,1,0:T(8,128)(2,1)S(1)} %copy-done.5, ...), custom_call_target="tpu_custom_call" | custom-call | tf_op jit(solution)/shard_map/back/pallas_call | solution.py:579
  78.7 0.3 collective-permute-start.8
  79.0 0.9 collective-permute-start.9
  79.9 1.8 %collective-permute-start.10 = (f32[128,256]{1,0:T(8,128)S(1)}, f32[128,256]{1,0:T(8,128)S(1)}, u32[]{:S(2)}, u32[]{:S(2)}) collective-permute-start(f32[128,256]{1,0:T(8,128)S(1)} %get-tuple-element.33), channel_id=1, source_target_pairs={{0,96},{32,0},{64,32},{96,64},{1,97},{33,1},{65,33},{97,65},{2,98}... | collective-permute-start | bytes 393224 | tf_op jit(solution)/shard_map/ppermute | solution.py:618
  81.7 0.8 back_rest.1.a_ref
  82.6 2.7 %collective-permute-done.8.b_ref = f32[128,256]{1,0:T(8,128)S(1)} collective-permute-done((f32[128,256]{1,0:T(8,128)S(1)}, f32[128,256]{1,0:T(8,128)S(1)}, u32[]{:S(2)}, u32[]{:S(2)}) %collective-permute-start.8) | collective-permute-done | bytes 131104 | tf_op jit(solution)/shard_map/ppermute | solution.py:618
  85.2 3.2 %collective-permute-done.9.c_ref = f32[128,256]{1,0:T(8,128)S(1)} collective-permute-done((f32[128,256]{1,0:T(8,128)S(1)}, f32[128,256]{1,0:T(8,128)S(1)}, u32[]{:S(2)}, u32[]{:S(2)}) %collective-permute-start.9) | collective-permute-done | bytes 131104 | tf_op jit(solution)/shard_map/ppermute | solution.py:618
  88.4 0.7 final.1
  (30 shorter events, 0.1 us)
Async XLA Ops:
  0.6 11.4 %copy-start.13 = (f32[8]{0:T(128)S(1)}, f32[8]{0:T(128)}, u32[]{:S(2)}) copy-start(f32[8]{0:T(128)} %high_ref.3) | copy-start | bytes 100
  0.6 11.4 %copy-start.12 = (f32[8]{0:T(128)S(1)}, f32[8]{0:T(128)}, u32[]{:S(2)}) copy-start(f32[8]{0:T(128)} %low_ref.3) | copy-start | bytes 100
  0.7 11.4 %copy-start.10 = (s32[1,8,256]{2,1,0:T(8,128)S(1)}, s32[1,8,256]{2,1,0:T(8,128)}, u32[]{:S(2)}) copy-start(s32[1,8,256]{2,1,0:T(8,128)} %refine_ref.1) | copy-start | bytes 24580
  1.6 18.7 %collective-permute-start = (bf16[1,64,2048]{2,1,0:T(8,128)(2,1)S(1)}, bf16[1,64,2048]{2,1,0:T(8,128)(2,1)S(1)}, u32[]{:S(2)}, u32[]{:S(2)}) collective-permute-start(bf16[1,64,2048]{2,1,0:T(8,128)(2,1)S(1)} %constant_dynamic-slice_fusion), channel_id=1, source_target_pairs={{96,128},{128,96},{97,129},{129,97},{98,130},{130,98},{99,131},{13... | collective-permute-start | bytes 786440 | tf_op jit(solution)/shard_map/ppermute | solution.py:624
  2.3 1.6 %copy-start = (bf16[8,64,2048]{2,1,0:T(8,128)(2,1)S(1)}, bf16[8,64,2048]{2,1,0:T(8,128)(2,1)}, u32[]{:S(2)}) copy-start(bf16[8,64,2048]{2,1,0:T(8,128)(2,1)} %d_ref.5) | copy-start | bytes 6291460
  3.9 8.1 %copy-start.1 = (bf16[8,64,2048]{2,1,0:T(8,128)(2,1)S(1)}, bf16[8,64,2048]{2,1,0:T(8,128)(2,1)}, u32[]{:S(2)}) copy-start(bf16[8,64,2048]{2,1,0:T(8,128)(2,1)} %d_ref.5) | copy-start | bytes 6291460
  3.9 16.4 %copy-start.2 = (bf16[8,256,256]{2,1,0:T(8,128)(2,1)S(1)}, bf16[8,256,256]{2,1,0:T(8,128)(2,1)}, u32[]{:S(2)}) copy-start(bf16[8,256,256]{2,1,0:T(8,128)(2,1)} %constant.44.clone.low_table) | copy-start | bytes 3145732
  3.9 16.4 %copy-start.3 = (bf16[8,256,256]{2,1,0:T(8,128)(2,1)S(1)}, bf16[8,256,256]{2,1,0:T(8,128)(2,1)}, u32[]{:S(2)}) copy-start(bf16[8,256,256]{2,1,0:T(8,128)(2,1)} %constant.43.clone.high_table) | copy-start | bytes 3145732
  4.1 16.2 %collective-permute-start.1 = (bf16[1,64,2048]{2,1,0:T(8,128)(2,1)S(1)}, bf16[1,64,2048]{2,1,0:T(8,128)(2,1)S(1)}, u32[]{:S(2)}, u32[]{:S(2)}) collective-permute-start(bf16[1,64,2048]{2,1,0:T(8,128)(2,1)S(1)} %get-tuple-element.18), channel_id=1, source_target_pairs={{32,64},{160,192},{64,32},{192,160},{33,65},{161,193},{65,33},{193... | collective-permute-start | bytes 786440 | tf_op jit(solution)/shard_map/ppermute | solution.py:624
  4.9 15.4 %collective-permute-start.2 = (bf16[1,64,2048]{2,1,0:T(8,128)(2,1)S(1)}, bf16[1,64,2048]{2,1,0:T(8,128)(2,1)S(1)}, u32[]{:S(2)}, u32[]{:S(2)}) collective-permute-start(bf16[1,64,2048]{2,1,0:T(8,128)(2,1)S(1)} %get-tuple-element.19), channel_id=1, source_target_pairs={{0,32},{64,96},{128,160},{192,224},{32,0},{96,64},{160,128},{224,1... | collective-permute-start | bytes 786440 | tf_op jit(solution)/shard_map/ppermute | solution.py:624
  9.6 10.7 %collective-permute-start.3 = (f32[8,2048]{1,0:T(8,128)S(1)}, f32[8,2048]{1,0:T(8,128)S(1)}, u32[]{:S(2)}, u32[]{:S(2)}) collective-permute-start(f32[8,2048]{1,0:T(8,128)S(1)} %get-tuple-element.20), channel_id=1, source_target_pairs={{0,1},{2,3},{4,5},{6,7},{8,9},{10,11},{12,13},{14,15},{16,17},{18,... | collective-permute-start | bytes 196616 | tf_op jit(solution)/shard_map/ppermute | solution.py:624
  10.9 9.5 %collective-permute-start.4 = (f32[8,2048]{1,0:T(8,128)S(1)}, f32[8,2048]{1,0:T(8,128)S(1)}, u32[]{:S(2)}, u32[]{:S(2)}) collective-permute-start(f32[8,2048]{1,0:T(8,128)S(1)} %get-tuple-element.21), channel_id=1, source_target_pairs={{1,2},{3,4},{5,6},{7,8},{9,10},{11,12},{13,14},{15,16},{17,18},{19... | collective-permute-start | bytes 196616 | tf_op jit(solution)/shard_map/ppermute | solution.py:624
  22.6 36.8 %copy-start.6 = (f32[32,8,128]{2,1,0:T(8,128)S(1)}, f32[32,8,128]{2,1,0:T(8,128)}, u32[]{:S(2)}) copy-start(f32[32,8,128]{2,1,0:T(8,128)} %constant.46.clone.sin_ref) | copy-start | bytes 393220
  22.6 36.8 %copy-start.7 = (f32[32,8,128]{2,1,0:T(8,128)S(1)}, f32[32,8,128]{2,1,0:T(8,128)}, u32[]{:S(2)}) copy-start(f32[32,8,128]{2,1,0:T(8,128)} %constant.45.clone.cos_ref) | copy-start | bytes 393220
  22.6 36.8 %copy-start.8 = (bf16[128,256]{1,0:T(8,128)(2,1)S(1)}, bf16[128,256]{1,0:T(8,128)(2,1)}, u32[]{:S(2)}) copy-start(bf16[128,256]{1,0:T(8,128)(2,1)} %constant.48.clone.low_table) | copy-start | bytes 196612
  22.6 36.8 %copy-start.9 = (bf16[128,256]{1,0:T(8,128)(2,1)S(1)}, bf16[128,256]{1,0:T(8,128)(2,1)}, u32[]{:S(2)}) copy-start(bf16[128,256]{1,0:T(8,128)(2,1)} %constant.47.clone.high_table) | copy-start | bytes 196612
  22.6 10.9 %collective-permute-start.5 = (f32[264,128]{1,0:T(8,128)S(1)}, f32[264,128]{1,0:T(8,128)S(1)}, u32[]{:S(2)}, u32[]{:S(2)}) collective-permute-start(f32[264,128]{1,0:T(8,128)S(1)} %get-tuple-element.26), channel_id=1, source_target_pairs={{0,64},{32,96},{64,0},{96,32},{1,65},{33,97},{65,1},{97,33},{2,66}... | collective-permute-start | bytes 405512 | tf_op jit(solution)/shard_map/ppermute | solution.py:618
  30.6 6.5 %collective-permute-start.6 = (f32[264,128]{1,0:T(8,128)S(1)}, f32[264,128]{1,0:T(8,128)S(1)}, u32[]{:S(2)}, u32[]{:S(2)}) collective-permute-start(f32[264,128]{1,0:T(8,128)S(1)} %get-tuple-element.27), channel_id=1, source_target_pairs={{0,32},{32,64},{64,96},{96,0},{1,33},{33,65},{65,97},{97,1},{2,34}... | collective-permute-start | bytes 405512 | tf_op jit(solution)/shard_map/ppermute | solution.py:618
  30.6 6.5 %collective-permute-start.7 = (f32[264,128]{1,0:T(8,128)S(1)}, f32[264,128]{1,0:T(8,128)S(1)}, u32[]{:S(2)}, u32[]{:S(2)}) collective-permute-start(f32[264,128]{1,0:T(8,128)S(1)} %get-tuple-element.28), channel_id=1, source_target_pairs={{0,96},{32,0},{64,32},{96,64},{1,97},{33,1},{65,33},{97,65},{2,98}... | collective-permute-start | bytes 405512 | tf_op jit(solution)/shard_map/ppermute | solution.py:618
  33.3 44.2 %copy-start.4 = (bf16[4,512,256]{2,1,0:T(8,128)(2,1)S(1)}, bf16[4,512,256]{2,1,0:T(8,128)(2,1)}, u32[]{:S(2)}) copy-start(bf16[4,512,256]{2,1,0:T(8,128)(2,1)} %constant.51.clone.low_table) | copy-start | bytes 3145732
  33.3 44.2 %copy-start.5 = (bf16[4,512,256]{2,1,0:T(8,128)(2,1)S(1)}, bf16[4,512,256]{2,1,0:T(8,128)(2,1)}, u32[]{:S(2)}) copy-start(bf16[4,512,256]{2,1,0:T(8,128)(2,1)} %constant.50.clone.high_table) | copy-start | bytes 3145732
  33.3 44.2 %copy-start.11 = (f32[16]{0:T(128)S(1)}, f32[16]{0:T(128)}, u32[]{:S(2)}) copy-start(f32[16]{0:T(128)} %constant.49.clone.eighth_ref) | copy-start | bytes 196
  78.7 6.5 %collective-permute-start.8 = (f32[128,256]{1,0:T(8,128)S(1)}, f32[128,256]{1,0:T(8,128)S(1)}, u32[]{:S(2)}, u32[]{:S(2)}) collective-permute-start(f32[128,256]{1,0:T(8,128)S(1)} %get-tuple-element.31), channel_id=1, source_target_pairs={{0,64},{32,96},{64,0},{96,32},{1,65},{33,97},{65,1},{97,33},{2,66}... | collective-permute-start | bytes 393224 | tf_op jit(solution)/shard_map/ppermute | solution.py:618
  79.0 9.4 %collective-permute-start.9 = (f32[128,256]{1,0:T(8,128)S(1)}, f32[128,256]{1,0:T(8,128)S(1)}, u32[]{:S(2)}, u32[]{:S(2)}) collective-permute-start(f32[128,256]{1,0:T(8,128)S(1)} %get-tuple-element.32), channel_id=1, source_target_pairs={{0,32},{32,64},{64,96},{96,0},{1,33},{33,65},{65,97},{97,1},{2,34}... | collective-permute-start | bytes 393224 | tf_op jit(solution)/shard_map/ppermute | solution.py:618
  79.9 8.5 %collective-permute-start.10 = (f32[128,256]{1,0:T(8,128)S(1)}, f32[128,256]{1,0:T(8,128)S(1)}, u32[]{:S(2)}, u32[]{:S(2)}) collective-permute-start(f32[128,256]{1,0:T(8,128)S(1)} %get-tuple-element.33), channel_id=1, source_target_pairs={{0,96},{32,0},{64,32},{96,64},{1,97},{33,1},{65,33},{97,65},{2,98}... | collective-permute-start | bytes 393224 | tf_op jit(solution)/shard_map/ppermute | solution.py:618

commit v9 on v8

--- a/solution.py
+++ b/solution.py
@@ -623,12 +623,13 @@
     def swap(array, axes, pairs):
         return lax.ppermute(array, axes, pairs + [(b, a) for a, b in pairs])
 
-    odd = lax.axis_index("x") % 2 == 1
-    cross = lax.dynamic_slice_in_dim(density, jnp.where(odd, LAYERS - 1, 0), 1, 0)
-    cross = swap(cross, LOS, [(3, 4)])
+    def swap(array, axes, pairs):
+        return lax.ppermute(array, axes, pairs + [(b, a) for a, b in pairs])
+
     row, other_row, layer, other_layer = edge_rows(density)
+    other_layer = swap(other_layer, LOS, [(0, 1), (2, 3), (4, 5), (6, 7)])
+    cross = swap(layer, LOS, [(3, 4)])
     layer = swap(layer, LOS, [(1, 2), (5, 6)])
-    other_layer = swap(other_layer, LOS, [(0, 1), (2, 3), (4, 5), (6, 7)])
     row = swap(row, "sky", [(i, i + 1) for i in range(0, SKY, 2)])
     other_row = swap(other_row, "sky", [(i, (i + 1) % SKY) for i in range(1, SKY, 2)])
     inner = inner_sums(weight_low, weight_high, density, refine)

time: 89.3 us -> 92.1 us (1.031)
  blocking collectives: 39 us -> 42.4 us
  starting transfers between devices: 22.3 us -> 20.3 us
  local copies, waits for them, and re-layouts: 2.62 us -> 3.65 us
    all_to_all x1, blocking collectives: 21.9 us -> 25.3 us  [body(): pieces = lax.all_to_all(turn(summed), ('zhi', 'sky'), 0, 0, tiled=True)]
    ppermute x5, starting transfers between devices: 8.61 us -> 5.79 us  [swap(): return lax.ppermute(array, axes, pairs + [(b, a) for a, b in pairs])]
    unnamed x28 -> x32, local copies, waits for them, and re-layouts: 1.65 us -> 3.65 us
    dynamic_slice x1 -> x0, local copies, waits for them, and re-layouts: 0.97 us -> none  [body(): lax.dynamic_slice_in_dim(density, jnp.where(odd, LAYERS - 1, 0), 1, 0)]
  transfers between devices with their start and end apart: 11 -> 11, of which waited for: 3 -> 4; matrix products, arithmetic and copies ran while one was open for 0% -> 0% of each run, Pallas kernels for 11% -> 10%
where the time goes in v9:
time: 92.1 us; the launch traced here: 91.8 us
  blocking collectives  42.4 us (46%)
  starting transfers between devices  20.3 us (22%)
  Pallas kernels  14.9 us (16%)
  waiting for transfers between devices  9.75 us (11%)
  local copies, waits for them, and re-layouts  3.65 us (4%)
    all_to_all x1, blocking collectives, body(): pieces = lax.all_to_all(turn(summed), ('zhi', 'sky'), 0, 0, tiled=True)  25.3 us
    all_to_all x1, blocking collectives, body(): pieces = lax.all_to_all(pieces, ('zhi', 'sky'), 0, 0, tiled=True)  17.1 us
    ppermute x6, starting transfers between devices, deliver(): lax.ppermute(pieces[a], 'x', [(i, (i + a) % 4) for i in range(4)])  14.5 us
    ppermute x6, waiting for transfers between devices, deliver(): lax.ppermute(pieces[a], 'x', [(i, (i + a) % 4) for i in range(4)])  9.74 us
    pallas_call x1, Pallas kernels, inner_sums(): pl.pallas_call(inner_kernel, out_shape=(jax.ShapeDtypeStruct((ROWS + 8, N...  8.23 us
    ppermute x5, starting transfers between devices, swap(): return lax.ppermute(array, axes, pairs + [(b, a) for a, b in pairs])  5.79 us
    unnamed x32, local copies, waits for them, and re-layouts  3.65 us
    pallas_call x1, Pallas kernels, outer_sums(): pl.pallas_call(outer_kernel, out_shape=(piece, piece, piece, jax.ShapeDty...  2.18 us
  transfers between devices with their start and end apart: 11, of which 4 were waited for; matrix products, arithmetic and copies ran while one was open for 0% of the time, Pallas kernels for 10%

profile of v9, /device:TPU:1, one launch (start us, length us, event | category | flops | bytes accessed | tf_op | source)
XLA Modules:
  0.0 91.8 jit_solution(17685260588515263676)
XLA Ops:
  0.6 1.6 %copy-done = bf16[8,64,2048]{2,1,0:T(8,128)(2,1)S(1)} copy-done((bf16[8,64,2048]{2,1,0:T(8,128)(2,1)S(1)}, bf16[8,64,2048]{2,1,0:T(8,128)(2,1)}, u32[]{:S(2)}) %copy-start) | copy-done | bytes 2097176
  2.2 0.2 edge_rows.1
  2.4 2.1 %collective-permute-start.2 = (bf16[1,64,2048]{2,1,0:T(8,128)(2,1)S(1)}, bf16[1,64,2048]{2,1,0:T(8,128)(2,1)S(1)}, u32[]{:S(2)}, u32[]{:S(2)}) collective-permute-start(bf16[1,64,2048]{2,1,0:T(8,128)(2,1)S(1)} %get-tuple-element.19), channel_id=1, source_target_pairs={{0,32},{64,96},{128,160},{192,224},{32,0},{96,64},{160,128},{224,1... | collective-permute-start | bytes 786440 | tf_op jit(solution)/shard_map/ppermute | solution.py:627
  4.5 0.7 collective-permute-start.1
  5.2 0.7 collective-permute-start
  5.9 1.6 %collective-permute-start.3 = (f32[8,2048]{1,0:T(8,128)S(1)}, f32[8,2048]{1,0:T(8,128)S(1)}, u32[]{:S(2)}, u32[]{:S(2)}) collective-permute-start(f32[8,2048]{1,0:T(8,128)S(1)} %get-tuple-element.20), channel_id=1, source_target_pairs={{0,1},{2,3},{4,5},{6,7},{8,9},{10,11},{12,13},{14,15},{16,17},{18,... | collective-permute-start | bytes 196616 | tf_op jit(solution)/shard_map/ppermute | solution.py:627
  7.5 0.7 collective-permute-start.4
  8.2 0.7 copy-done.10
  8.9 0.7 copy-done.12
  9.6 0.7 copy-done.14
  10.2 8.2 %inner_sums.1 = (f32[72,2048]{1,0:T(8,128)S(1)}, f32[8,2048]{1,0:T(8,128)S(1)}, f32[4,8,2048]{2,1,0:T(8,128)S(1)}) custom-call(f32[8]{0:T(128)S(1)} %copy-done.12, f32[8]{0:T(128)S(1)} %copy-done.14, bf16[8,64,2048]{2,1,0:T(8,128)(2,1)S(1)} %copy-done.1, s32[1,8,256]{2,1,0:T(8,128)S(1)} %copy-done.10), custom_call_target="tpu_custom_call" | custom-call | flops 40000000 | bytes 25165824 | tf_op jit(solution)/shard_map/inner_sums/pallas_call | solution.py:243
  18.6 2.2 %outer_sums.1 = (f32[264,128]{1,0:T(8,128)S(1)}, f32[264,128]{1,0:T(8,128)S(1)}, f32[264,128]{1,0:T(8,128)S(1)}, bf16[8,160,256]{2,1,0:T(8,128)(2,1)S(1)}) custom-call(f32[8]{0:T(128)S(1)} %copy-done.13, f32[8]{0:T(128)S(1)} %copy-done.15, bf16[8,64,2048]{2,1,0:T(8,128)(2,1)S(1)} %copy-done.1, bf16[1,64,2048]{2,1,0:T(8,128)(2,1)S(1)} %collective-permute-done.cross_ref, ...), custom_call_target="tpu_custom_call" | custom-call | tf_op jit(solution)/shard_map/outer_sums/pallas_call | solution.py:364
  20.8 0.0 copy-start.6
  20.8 0.0 copy-start.7
  20.8 0.0 copy-start.8
  20.8 4.1 %collective-permute-start.5 = (f32[264,128]{1,0:T(8,128)S(1)}, f32[264,128]{1,0:T(8,128)S(1)}, u32[]{:S(2)}, u32[]{:S(2)}) collective-permute-start(f32[264,128]{1,0:T(8,128)S(1)} %get-tuple-element.26), channel_id=1, source_target_pairs={{0,64},{32,96},{64,0},{96,32},{1,65},{33,97},{65,1},{97,33},{2,66}... | collective-permute-start | bytes 405512 | tf_op jit(solution)/shard_map/ppermute | solution.py:618
  24.9 7.4 %collective-permute-start.6 = (f32[264,128]{1,0:T(8,128)S(1)}, f32[264,128]{1,0:T(8,128)S(1)}, u32[]{:S(2)}, u32[]{:S(2)}) collective-permute-start(f32[264,128]{1,0:T(8,128)S(1)} %get-tuple-element.27), channel_id=1, source_target_pairs={{0,32},{32,64},{64,96},{96,0},{1,33},{33,65},{65,97},{97,1},{2,34}... | collective-permute-start | bytes 405512 | tf_op jit(solution)/shard_map/ppermute | solution.py:618
  32.3 0.2 other_sums.1.a_ref
  32.6 2.0 %collective-permute-done.6.c_ref = f32[264,128]{1,0:T(8,128)S(1)} collective-permute-done((f32[264,128]{1,0:T(8,128)S(1)}, f32[264,128]{1,0:T(8,128)S(1)}, u32[]{:S(2)}, u32[]{:S(2)}) %collective-permute-start.6) | collective-permute-done | bytes 135200 | tf_op jit(solution)/shard_map/ppermute | solution.py:618
  34.5 1.9 %collective-permute-done.7.d_ref = f32[264,128]{1,0:T(8,128)S(1)} collective-permute-done((f32[264,128]{1,0:T(8,128)S(1)}, f32[264,128]{1,0:T(8,128)S(1)}, u32[]{:S(2)}, u32[]{:S(2)}) %collective-permute-start.7) | collective-permute-done | bytes 135200 | tf_op jit(solution)/shard_map/ppermute | solution.py:618
  36.4 0.3 turn.1
  36.8 25.3 %all_to_all.10.in_ref = f32[64,1,640]{2,1,0:T(1,128)S(1)} all-to-all(f32[64,1,640]{2,1,0:T(1,128)S(1)} %turn.1), channel_id=1, replica_groups=mesh['zhi'=2,'x'=4,'sky'=32] {'zhi','sky'}, dimensions={0} | all-to-all | bytes 327680 | tf_op jit(solution)/shard_map/all_to_all | solution.py:641
  62.2 1.0 %solve.1 = f32[64,8,128]{2,1,0:T(8,128)S(1)} custom-call(f32[64,1,640]{2,1,0:T(1,128)S(1)} %all_to_all.10.in_ref, f32[32,8,128]{2,1,0:T(8,128)S(1)} %copy-done.7, f32[32,8,128]{2,1,0:T(8,128)S(1)} %copy-done.6, bf16[128,256]{1,0:T(8,128)(2,1)S(1)} %copy-done.9, bf16[128,256]{1,0:T(8,128)(2,1)S(1)} %copy-done.8), custom_call_target="tpu_custom_call" | custom-call | tf_op jit(solution)/shard_map/solve/pallas_call | solution.py:533
  63.2 17.1 %all_to_all.11.in_ref = f32[64,8,128]{2,1,0:T(8,128)S(1)} all-to-all(f32[64,8,128]{2,1,0:T(8,128)S(1)} %solve.1), channel_id=1, replica_groups=mesh['zhi'=2,'x'=4,'sky'=32] {'zhi','sky'}, dimensions={0} | all-to-all | bytes 524288 | tf_op jit(solution)/shard_map/all_to_all | solution.py:643
  80.2 1.2 %back.1 = (f32[128,256]{1,0:T(8,128)S(1)}, f32[128,256]{1,0:T(8,128)S(1)}, f32[128,256]{1,0:T(8,128)S(1)}, f32[128,512]{1,0:T(8,128)S(1)}, f32[128,512]{1,0:T(8,128)S(1)}) custom-call(f32[16]{0:T(128)S(1)} %copy-done.11, f32[64,8,128]{2,1,0:T(8,128)S(1)} %all_to_all.11.in_ref, bf16[4,512,256]{2,1,0:T(8,128)(2,1)S(1)} %copy-done.5, ...), custom_call_target="tpu_custom_call" | custom-call | tf_op jit(solution)/shard_map/back/pallas_call | solution.py:579
  81.5 0.3 collective-permute-start.8
  81.8 0.9 collective-permute-start.9
  82.7 1.8 %collective-permute-start.10 = (f32[128,256]{1,0:T(8,128)S(1)}, f32[128,256]{1,0:T(8,128)S(1)}, u32[]{:S(2)}, u32[]{:S(2)}) collective-permute-start(f32[128,256]{1,0:T(8,128)S(1)} %get-tuple-element.33), channel_id=1, source_target_pairs={{0,96},{32,0},{64,32},{96,64},{1,97},{33,1},{65,33},{97,65},{2,98}... | collective-permute-start | bytes 393224 | tf_op jit(solution)/shard_map/ppermute | solution.py:618
  84.4 0.8 back_rest.1.a_ref
  85.3 2.7 %collective-permute-done.8.b_ref = f32[128,256]{1,0:T(8,128)S(1)} collective-permute-done((f32[128,256]{1,0:T(8,128)S(1)}, f32[128,256]{1,0:T(8,128)S(1)}, u32[]{:S(2)}, u32[]{:S(2)}) %collective-permute-start.8) | collective-permute-done | bytes 131104 | tf_op jit(solution)/shard_map/ppermute | solution.py:618
  87.9 3.2 %collective-permute-done.9.c_ref = f32[128,256]{1,0:T(8,128)S(1)} collective-permute-done((f32[128,256]{1,0:T(8,128)S(1)}, f32[128,256]{1,0:T(8,128)S(1)}, u32[]{:S(2)}, u32[]{:S(2)}) %collective-permute-start.9) | collective-permute-done | bytes 131104 | tf_op jit(solution)/shard_map/ppermute | solution.py:618
  91.1 0.7 final.1
  (33 shorter events, 0.1 us)
Async XLA Ops:
  0.6 1.6 %copy-start = (bf16[8,64,2048]{2,1,0:T(8,128)(2,1)S(1)}, bf16[8,64,2048]{2,1,0:T(8,128)(2,1)}, u32[]{:S(2)}) copy-start(bf16[8,64,2048]{2,1,0:T(8,128)(2,1)} %d_ref.5) | copy-start | bytes 6291460
  2.2 6.0 %copy-start.1 = (bf16[8,64,2048]{2,1,0:T(8,128)(2,1)S(1)}, bf16[8,64,2048]{2,1,0:T(8,128)(2,1)}, u32[]{:S(2)}) copy-start(bf16[8,64,2048]{2,1,0:T(8,128)(2,1)} %d_ref.5) | copy-start | bytes 6291460
  2.2 16.3 %copy-start.2 = (bf16[8,256,256]{2,1,0:T(8,128)(2,1)S(1)}, bf16[8,256,256]{2,1,0:T(8,128)(2,1)}, u32[]{:S(2)}) copy-start(bf16[8,256,256]{2,1,0:T(8,128)(2,1)} %constant.19.clone.low_table) | copy-start | bytes 3145732
  2.2 16.3 %copy-start.3 = (bf16[8,256,256]{2,1,0:T(8,128)(2,1)S(1)}, bf16[8,256,256]{2,1,0:T(8,128)(2,1)}, u32[]{:S(2)}) copy-start(bf16[8,256,256]{2,1,0:T(8,128)(2,1)} %constant.18.clone.high_table) | copy-start | bytes 3145732
  2.4 16.1 %collective-permute-start.2 = (bf16[1,64,2048]{2,1,0:T(8,128)(2,1)S(1)}, bf16[1,64,2048]{2,1,0:T(8,128)(2,1)S(1)}, u32[]{:S(2)}, u32[]{:S(2)}) collective-permute-start(bf16[1,64,2048]{2,1,0:T(8,128)(2,1)S(1)} %get-tuple-element.19), channel_id=1, source_target_pairs={{0,32},{64,96},{128,160},{192,224},{32,0},{96,64},{160,128},{224,1... | collective-permute-start | bytes 786440 | tf_op jit(solution)/shard_map/ppermute | solution.py:627
  4.5 14.0 %collective-permute-start.1 = (bf16[1,64,2048]{2,1,0:T(8,128)(2,1)S(1)}, bf16[1,64,2048]{2,1,0:T(8,128)(2,1)S(1)}, u32[]{:S(2)}, u32[]{:S(2)}) collective-permute-start(bf16[1,64,2048]{2,1,0:T(8,128)(2,1)S(1)} %get-tuple-element.18), channel_id=1, source_target_pairs={{32,64},{160,192},{64,32},{192,160},{33,65},{161,193},{65,33},{193... | collective-permute-start | bytes 786440 | tf_op jit(solution)/shard_map/ppermute | solution.py:627
  5.2 13.3 %collective-permute-start = (bf16[1,64,2048]{2,1,0:T(8,128)(2,1)S(1)}, bf16[1,64,2048]{2,1,0:T(8,128)(2,1)S(1)}, u32[]{:S(2)}, u32[]{:S(2)}) collective-permute-start(bf16[1,64,2048]{2,1,0:T(8,128)(2,1)S(1)} %get-tuple-element.18), channel_id=1, source_target_pairs={{96,128},{128,96},{97,129},{129,97},{98,130},{130,98},{99,131},{13... | collective-permute-start | bytes 786440 | tf_op jit(solution)/shard_map/ppermute | solution.py:627
  5.9 12.6 %collective-permute-start.3 = (f32[8,2048]{1,0:T(8,128)S(1)}, f32[8,2048]{1,0:T(8,128)S(1)}, u32[]{:S(2)}, u32[]{:S(2)}) collective-permute-start(f32[8,2048]{1,0:T(8,128)S(1)} %get-tuple-element.20), channel_id=1, source_target_pairs={{0,1},{2,3},{4,5},{6,7},{8,9},{10,11},{12,13},{14,15},{16,17},{18,... | collective-permute-start | bytes 196616 | tf_op jit(solution)/shard_map/ppermute | solution.py:627
  7.5 11.0 %collective-permute-start.4 = (f32[8,2048]{1,0:T(8,128)S(1)}, f32[8,2048]{1,0:T(8,128)S(1)}, u32[]{:S(2)}, u32[]{:S(2)}) collective-permute-start(f32[8,2048]{1,0:T(8,128)S(1)} %get-tuple-element.21), channel_id=1, source_target_pairs={{1,2},{3,4},{5,6},{7,8},{9,10},{11,12},{13,14},{15,16},{17,18},{19... | collective-permute-start | bytes 196616 | tf_op jit(solution)/shard_map/ppermute | solution.py:627
  8.2 0.7 copy-start.10
  8.9 0.7 copy-start.12
  9.6 0.7 copy-start.14
  10.2 8.3 %copy-start.13 = (f32[8]{0:T(128)S(1)}, f32[8]{0:T(128)}, u32[]{:S(2)}) copy-start(f32[8]{0:T(128)} %low_ref.3) | copy-start | bytes 100
  10.2 8.3 %copy-start.15 = (f32[8]{0:T(128)S(1)}, f32[8]{0:T(128)}, u32[]{:S(2)}) copy-start(f32[8]{0:T(128)} %high_ref.3) | copy-start | bytes 100
  20.8 41.4 %copy-start.6 = (f32[32,8,128]{2,1,0:T(8,128)S(1)}, f32[32,8,128]{2,1,0:T(8,128)}, u32[]{:S(2)}) copy-start(f32[32,8,128]{2,1,0:T(8,128)} %constant.21.clone.sin_ref) | copy-start | bytes 393220
  20.8 41.4 %copy-start.7 = (f32[32,8,128]{2,1,0:T(8,128)S(1)}, f32[32,8,128]{2,1,0:T(8,128)}, u32[]{:S(2)}) copy-start(f32[32,8,128]{2,1,0:T(8,128)} %constant.20.clone.cos_ref) | copy-start | bytes 393220
  20.8 41.4 %copy-start.8 = (bf16[128,256]{1,0:T(8,128)(2,1)S(1)}, bf16[128,256]{1,0:T(8,128)(2,1)}, u32[]{:S(2)}) copy-start(bf16[128,256]{1,0:T(8,128)(2,1)} %constant.23.clone.low_table) | copy-start | bytes 196612
  20.8 41.3 %copy-start.9 = (bf16[128,256]{1,0:T(8,128)(2,1)S(1)}, bf16[128,256]{1,0:T(8,128)(2,1)}, u32[]{:S(2)}) copy-start(bf16[128,256]{1,0:T(8,128)(2,1)} %constant.22.clone.high_table) | copy-start | bytes 196612
  20.8 11.7 %collective-permute-start.5 = (f32[264,128]{1,0:T(8,128)S(1)}, f32[264,128]{1,0:T(8,128)S(1)}, u32[]{:S(2)}, u32[]{:S(2)}) collective-permute-start(f32[264,128]{1,0:T(8,128)S(1)} %get-tuple-element.26), channel_id=1, source_target_pairs={{0,64},{32,96},{64,0},{96,32},{1,65},{33,97},{65,1},{97,33},{2,66}... | collective-permute-start | bytes 405512 | tf_op jit(solution)/shard_map/ppermute | solution.py:618
  24.9 9.6 %collective-permute-start.6 = (f32[264,128]{1,0:T(8,128)S(1)}, f32[264,128]{1,0:T(8,128)S(1)}, u32[]{:S(2)}, u32[]{:S(2)}) collective-permute-start(f32[264,128]{1,0:T(8,128)S(1)} %get-tuple-element.27), channel_id=1, source_target_pairs={{0,32},{32,64},{64,96},{96,0},{1,33},{33,65},{65,97},{97,1},{2,34}... | collective-permute-start | bytes 405512 | tf_op jit(solution)/shard_map/ppermute | solution.py:618
  32.3 4.2 %collective-permute-start.7 = (f32[264,128]{1,0:T(8,128)S(1)}, f32[264,128]{1,0:T(8,128)S(1)}, u32[]{:S(2)}, u32[]{:S(2)}) collective-permute-start(f32[264,128]{1,0:T(8,128)S(1)} %get-tuple-element.28), channel_id=1, source_target_pairs={{0,96},{32,0},{64,32},{96,64},{1,97},{33,1},{65,33},{97,65},{2,98}... | collective-permute-start | bytes 405512 | tf_op jit(solution)/shard_map/ppermute | solution.py:618
  32.3 47.9 %copy-start.4 = (bf16[4,512,256]{2,1,0:T(8,128)(2,1)S(1)}, bf16[4,512,256]{2,1,0:T(8,128)(2,1)}, u32[]{:S(2)}) copy-start(bf16[4,512,256]{2,1,0:T(8,128)(2,1)} %constant.26.clone.low_table) | copy-start | bytes 3145732
  32.3 47.9 %copy-start.5 = (bf16[4,512,256]{2,1,0:T(8,128)(2,1)S(1)}, bf16[4,512,256]{2,1,0:T(8,128)(2,1)}, u32[]{:S(2)}) copy-start(bf16[4,512,256]{2,1,0:T(8,128)(2,1)} %constant.25.clone.high_table) | copy-start | bytes 3145732
  32.3 47.9 %copy-start.11 = (f32[16]{0:T(128)S(1)}, f32[16]{0:T(128)}, u32[]{:S(2)}) copy-start(f32[16]{0:T(128)} %constant.24.clone.eighth_ref) | copy-start | bytes 196
  81.5 6.5 %collective-permute-start.8 = (f32[128,256]{1,0:T(8,128)S(1)}, f32[128,256]{1,0:T(8,128)S(1)}, u32[]{:S(2)}, u32[]{:S(2)}) collective-permute-start(f32[128,256]{1,0:T(8,128)S(1)} %get-tuple-element.31), channel_id=1, source_target_pairs={{0,64},{32,96},{64,0},{96,32},{1,65},{33,97},{65,1},{97,33},{2,66}... | collective-permute-start | bytes 393224 | tf_op jit(solution)/shard_map/ppermute | solution.py:618
  81.8 9.4 %collective-permute-start.9 = (f32[128,256]{1,0:T(8,128)S(1)}, f32[128,256]{1,0:T(8,128)S(1)}, u32[]{:S(2)}, u32[]{:S(2)}) collective-permute-start(f32[128,256]{1,0:T(8,128)S(1)} %get-tuple-element.32), channel_id=1, source_target_pairs={{0,32},{32,64},{64,96},{96,0},{1,33},{33,65},{65,97},{97,1},{2,34}... | collective-permute-start | bytes 393224 | tf_op jit(solution)/shard_map/ppermute | solution.py:618
  82.7 8.5 %collective-permute-start.10 = (f32[128,256]{1,0:T(8,128)S(1)}, f32[128,256]{1,0:T(8,128)S(1)}, u32[]{:S(2)}, u32[]{:S(2)}) collective-permute-start(f32[128,256]{1,0:T(8,128)S(1)} %get-tuple-element.33), channel_id=1, source_target_pairs={{0,96},{32,0},{64,32},{96,64},{1,97},{33,1},{65,33},{97,65},{2,98}... | collective-permute-start | bytes 393224 | tf_op jit(solution)/shard_map/ppermute | solution.py:618

commit v10 on v8

--- a/solution.py
+++ b/solution.py
@@ -326,16 +326,25 @@
             total = term if total is None else total + term
         return total
 
-    def cosines(k):
-        first = part[0] + part[8] if k % 2 == 0 else part[0] - part[8]
-        return first + weigh((float(np.cos(np.pi * k * a / 8)), even[a - 1]) for a in range(1, 8))
-
-    def sines(k):
-        return weigh((float(-np.sin(np.pi * k * a / 8)), odd[a - 1]) for a in range(1, 8))
-
+    ends = (part[0] + part[8], part[0] - part[8])
+    cosine, sine = [None] * 9, [None] * 9
+    for k in range(5):
+        factors = [float(np.cos(np.pi * k * a / 8)) for a in range(1, 8)]
+        plain = ends[k % 2] + weigh([(factors[a - 1], even[a - 1]) for a in (2, 4, 6)])
+        turned = weigh([(factors[a - 1], even[a - 1]) for a in (1, 3, 5, 7)])
+        cosine[k] = plain if turned is None else plain + turned
+        if k < 4:
+            cosine[8 - k] = plain - turned
+    for k in range(1, 5):
+        factors = [float(-np.sin(np.pi * k * a / 8)) for a in range(1, 8)]
+        plain = weigh([(factors[a - 1], odd[a - 1]) for a in (2, 4, 6)])
+        turned = weigh([(factors[a - 1], odd[a - 1]) for a in (1, 3, 5, 7)])
+        sine[k] = turned if plain is None else turned + plain
+        if k < 4:
+            sine[8 - k] = turned - plain
     for tile in range(8):
-        second = sines(tile) if tile else cosines(8)
-        value = jnp.concatenate([cosines(tile), second], axis=1)
+        second = sine[tile] if tile else cosine[8]
+        value = jnp.concatenate([cosine[tile], second], axis=1)
         value = jnp.concatenate([value, jnp.zeros((8, 256), f32)], axis=0)
         part_ref[tile] = stacked(value)
     transform_for(2, part_ref, high_table, low_table, far_ref)
@@ -615,7 +624,7 @@
 
 def deliver(pieces):
     return [pieces[0]] + [
-        lax.ppermute(pieces[a], "x", [(i, (i + a) % 4) for i in range(4)]) for a in (2, 1, 3)
+        lax.ppermute(pieces[a], "x", [(i, (i + a) % 4) for i in range(4)]) for a in (1, 2, 3)
     ]
 
 

time: 89.3 us -> 89.6 us (level)
  blocking collectives: 39 us -> 40.6 us
  waiting for transfers between devices: 9.47 us -> 8.52 us
    all_to_all x1, blocking collectives: 21.9 us -> 23.5 us  [body(): pieces = lax.all_to_all(turn(summed), ('zhi', 'sky'), 0, 0, tiled=True)]
    ppermute x6, waiting for transfers between devices: 9.46 us -> 8.51 us  [deliver(): lax.ppermute(pieces[a], 'x', [(i, (i + a) % 4) for i in range(4)])]
  transfers between devices with their start and end apart: 11 -> 11, of which waited for: 3 -> 4; matrix products, arithmetic and copies ran while one was open for 0% -> 0% of each run, Pallas kernels for 11% -> 11%
where the time goes in v10:
time: 89.6 us; the launch traced here: 89.4 us
  blocking collectives  40.6 us (45%)
  starting transfers between devices  22 us (25%)
  Pallas kernels  14.8 us (17%)
  waiting for transfers between devices  8.52 us (10%)
  local copies, waits for them, and re-layouts  2.62 us (3%)
  between operations  0.9 us (1%)
    all_to_all x1, blocking collectives, body(): pieces = lax.all_to_all(turn(summed), ('zhi', 'sky'), 0, 0, tiled=True)  23.5 us
    all_to_all x1, blocking collectives, body(): pieces = lax.all_to_all(pieces, ('zhi', 'sky'), 0, 0, tiled=True)  17.1 us
    ppermute x6, starting transfers between devices, deliver(): lax.ppermute(pieces[a], 'x', [(i, (i + a) % 4) for i in range(4)])  13.4 us
    ppermute x5, starting transfers between devices, swap(): return lax.ppermute(array, axes, pairs + [(b, a) for a, b in pairs])  8.61 us
    ppermute x6, waiting for transfers between devices, deliver(): lax.ppermute(pieces[a], 'x', [(i, (i + a) % 4) for i in range(4)])  8.51 us
    pallas_call x1, Pallas kernels, inner_sums(): pl.pallas_call(inner_kernel, out_shape=(jax.ShapeDtypeStruct((ROWS + 8, N...  8.23 us
    pallas_call x1, Pallas kernels, outer_sums(): pl.pallas_call(outer_kernel, out_shape=(piece, piece, piece, jax.ShapeDty...  2.08 us
  transfers between devices with their start and end apart: 11, of which 4 were waited for; matrix products, arithmetic and copies ran while one was open for 0% of the time, Pallas kernels for 11%

profile of v10, /device:TPU:1, one launch (start us, length us, event | category | flops | bytes accessed | tf_op | source)
XLA Modules:
  0.0 89.4 jit_solution(9230757528993839473)
XLA Ops:
  0.7 1.0 %constant_dynamic-slice_fusion = bf16[1,64,2048]{2,1,0:T(8,128)(2,1)S(1)} fusion(bf16[8,64,2048]{2,1,0:T(8,128)(2,1)} %d_ref.5, s32[]{:T(128)S(6)} %select_n.13), kind=kLoop, calls=%fused_computation | loop fusion | bytes 524292 | tf_op jit(solution)/shard_map/dynamic_slice | solution.py:636
  1.6 0.7 collective-permute-start
  2.3 0.0 copy-start
  2.3 1.6 %copy-done = bf16[8,64,2048]{2,1,0:T(8,128)(2,1)S(1)} copy-done((bf16[8,64,2048]{2,1,0:T(8,128)(2,1)S(1)}, bf16[8,64,2048]{2,1,0:T(8,128)(2,1)}, u32[]{:S(2)}) %copy-start) | copy-done | bytes 2097176
  3.9 0.2 edge_rows.1
  4.1 0.8 collective-permute-start.1
  4.9 4.7 %collective-permute-start.2 = (bf16[1,64,2048]{2,1,0:T(8,128)(2,1)S(1)}, bf16[1,64,2048]{2,1,0:T(8,128)(2,1)S(1)}, u32[]{:S(2)}, u32[]{:S(2)}) collective-permute-start(bf16[1,64,2048]{2,1,0:T(8,128)(2,1)S(1)} %get-tuple-element.19), channel_id=1, source_target_pairs={{0,32},{64,96},{128,160},{192,224},{32,0},{96,64},{160,128},{224,1... | collective-permute-start | bytes 786440 | tf_op jit(solution)/shard_map/ppermute | solution.py:633
  9.6 1.2 %collective-permute-start.3 = (f32[8,2048]{1,0:T(8,128)S(1)}, f32[8,2048]{1,0:T(8,128)S(1)}, u32[]{:S(2)}, u32[]{:S(2)}) collective-permute-start(f32[8,2048]{1,0:T(8,128)S(1)} %get-tuple-element.20), channel_id=1, source_target_pairs={{0,1},{2,3},{4,5},{6,7},{8,9},{10,11},{12,13},{14,15},{16,17},{18,... | collective-permute-start | bytes 196616 | tf_op jit(solution)/shard_map/ppermute | solution.py:633
  10.9 1.2 %collective-permute-start.4 = (f32[8,2048]{1,0:T(8,128)S(1)}, f32[8,2048]{1,0:T(8,128)S(1)}, u32[]{:S(2)}, u32[]{:S(2)}) collective-permute-start(f32[8,2048]{1,0:T(8,128)S(1)} %get-tuple-element.21), channel_id=1, source_target_pairs={{1,2},{3,4},{5,6},{7,8},{9,10},{11,12},{13,14},{15,16},{17,18},{19... | collective-permute-start | bytes 196616 | tf_op jit(solution)/shard_map/ppermute | solution.py:633
  12.1 8.2 %inner_sums.1 = (f32[72,2048]{1,0:T(8,128)S(1)}, f32[8,2048]{1,0:T(8,128)S(1)}, f32[4,8,2048]{2,1,0:T(8,128)S(1)}) custom-call(f32[8]{0:T(128)S(1)} %copy-done.12, f32[8]{0:T(128)S(1)} %copy-done.13, bf16[8,64,2048]{2,1,0:T(8,128)(2,1)S(1)} %copy-done.1, s32[1,8,256]{2,1,0:T(8,128)S(1)} %copy-done.10), custom_call_target="tpu_custom_call" | custom-call | flops 40000000 | bytes 25165824 | tf_op jit(solution)/shard_map/inner_sums/pallas_call | solution.py:243
  20.4 2.1 %outer_sums.1 = (f32[264,128]{1,0:T(8,128)S(1)}, f32[264,128]{1,0:T(8,128)S(1)}, f32[264,128]{1,0:T(8,128)S(1)}, bf16[8,160,256]{2,1,0:T(8,128)(2,1)S(1)}) custom-call(f32[8]{0:T(128)S(1)} %copy-done.12, f32[8]{0:T(128)S(1)} %copy-done.13, bf16[8,64,2048]{2,1,0:T(8,128)(2,1)S(1)} %copy-done.1, bf16[1,64,2048]{2,1,0:T(8,128)(2,1)S(1)} %collective-permute-done.cross_ref, ...), custom_call_target="tpu_custom_call" | custom-call | tf_op jit(solution)/shard_map/outer_sums/pallas_call | solution.py:373
  22.5 0.0 copy-start.6
  22.5 0.0 copy-start.7
  22.5 0.0 copy-start.8
  22.5 0.0 copy-start.9
  22.5 0.1 collective-permute-start.5
  22.6 8.0 %collective-permute-start.6 = (f32[264,128]{1,0:T(8,128)S(1)}, f32[264,128]{1,0:T(8,128)S(1)}, u32[]{:S(2)}, u32[]{:S(2)}) collective-permute-start(f32[264,128]{1,0:T(8,128)S(1)} %get-tuple-element.27), channel_id=1, source_target_pairs={{0,64},{32,96},{64,0},{96,32},{1,65},{33,97},{65,1},{97,33},{2,66}... | collective-permute-start | bytes 405512 | tf_op jit(solution)/shard_map/ppermute | solution.py:627
  30.6 2.0 %collective-permute-start.7 = (f32[264,128]{1,0:T(8,128)S(1)}, f32[264,128]{1,0:T(8,128)S(1)}, u32[]{:S(2)}, u32[]{:S(2)}) collective-permute-start(f32[264,128]{1,0:T(8,128)S(1)} %get-tuple-element.28), channel_id=1, source_target_pairs={{0,96},{32,0},{64,32},{96,64},{1,97},{33,1},{65,33},{97,65},{2,98}... | collective-permute-start | bytes 405512 | tf_op jit(solution)/shard_map/ppermute | solution.py:627
  32.6 0.2 other_sums.1.a_ref
  32.9 1.6 %collective-permute-done.6.c_ref = f32[264,128]{1,0:T(8,128)S(1)} collective-permute-done((f32[264,128]{1,0:T(8,128)S(1)}, f32[264,128]{1,0:T(8,128)S(1)}, u32[]{:S(2)}, u32[]{:S(2)}) %collective-permute-start.6) | collective-permute-done | bytes 135200 | tf_op jit(solution)/shard_map/ppermute | solution.py:627
  34.5 1.5 %collective-permute-done.7.d_ref = f32[264,128]{1,0:T(8,128)S(1)} collective-permute-done((f32[264,128]{1,0:T(8,128)S(1)}, f32[264,128]{1,0:T(8,128)S(1)}, u32[]{:S(2)}, u32[]{:S(2)}) %collective-permute-start.7) | collective-permute-done | bytes 135200 | tf_op jit(solution)/shard_map/ppermute | solution.py:627
  36.0 0.3 turn.1
  36.4 23.5 %all_to_all.10.in_ref = f32[64,1,640]{2,1,0:T(1,128)S(1)} all-to-all(f32[64,1,640]{2,1,0:T(1,128)S(1)} %turn.1), channel_id=1, replica_groups=mesh['zhi'=2,'x'=4,'sky'=32] {'zhi','sky'}, dimensions={0} | all-to-all | bytes 327680 | tf_op jit(solution)/shard_map/all_to_all | solution.py:649
  59.9 1.0 %solve.1 = f32[64,8,128]{2,1,0:T(8,128)S(1)} custom-call(f32[64,1,640]{2,1,0:T(1,128)S(1)} %all_to_all.10.in_ref, f32[32,8,128]{2,1,0:T(8,128)S(1)} %copy-done.7, f32[32,8,128]{2,1,0:T(8,128)S(1)} %copy-done.6, bf16[128,256]{1,0:T(8,128)(2,1)S(1)} %copy-done.9, bf16[128,256]{1,0:T(8,128)(2,1)S(1)} %copy-done.8), custom_call_target="tpu_custom_call" | custom-call | tf_op jit(solution)/shard_map/solve/pallas_call | solution.py:542
  60.9 17.1 %all_to_all.11.in_ref = f32[64,8,128]{2,1,0:T(8,128)S(1)} all-to-all(f32[64,8,128]{2,1,0:T(8,128)S(1)} %solve.1), channel_id=1, replica_groups=mesh['zhi'=2,'x'=4,'sky'=32] {'zhi','sky'}, dimensions={0} | all-to-all | bytes 524288 | tf_op jit(solution)/shard_map/all_to_all | solution.py:651
  78.0 1.2 %back.1 = (f32[128,256]{1,0:T(8,128)S(1)}, f32[128,256]{1,0:T(8,128)S(1)}, f32[128,256]{1,0:T(8,128)S(1)}, f32[128,512]{1,0:T(8,128)S(1)}, f32[128,512]{1,0:T(8,128)S(1)}) custom-call(f32[16]{0:T(128)S(1)} %copy-done.11, f32[64,8,128]{2,1,0:T(8,128)S(1)} %all_to_all.11.in_ref, bf16[4,512,256]{2,1,0:T(8,128)(2,1)S(1)} %copy-done.5, ...), custom_call_target="tpu_custom_call" | custom-call | tf_op jit(solution)/shard_map/back/pallas_call | solution.py:588
  79.2 0.1 collective-permute-start.8
  79.3 3.2 %collective-permute-start.9 = (f32[128,256]{1,0:T(8,128)S(1)}, f32[128,256]{1,0:T(8,128)S(1)}, u32[]{:S(2)}, u32[]{:S(2)}) collective-permute-start(f32[128,256]{1,0:T(8,128)S(1)} %get-tuple-element.32), channel_id=1, source_target_pairs={{0,64},{32,96},{64,0},{96,32},{1,65},{33,97},{65,1},{97,33},{2,66}... | collective-permute-start | bytes 393224 | tf_op jit(solution)/shard_map/ppermute | solution.py:627
  82.5 0.8 back_rest.1.a_ref
  83.3 2.0 %collective-permute-done.8.b_ref = f32[128,256]{1,0:T(8,128)S(1)} collective-permute-done((f32[128,256]{1,0:T(8,128)S(1)}, f32[128,256]{1,0:T(8,128)S(1)}, u32[]{:S(2)}, u32[]{:S(2)}) %collective-permute-start.8) | collective-permute-done | bytes 131104 | tf_op jit(solution)/shard_map/ppermute | solution.py:627
  85.3 3.4 %collective-permute-done.9.c_ref = f32[128,256]{1,0:T(8,128)S(1)} collective-permute-done((f32[128,256]{1,0:T(8,128)S(1)}, f32[128,256]{1,0:T(8,128)S(1)}, u32[]{:S(2)}, u32[]{:S(2)}) %collective-permute-start.9) | collective-permute-done | bytes 131104 | tf_op jit(solution)/shard_map/ppermute | solution.py:627
  88.7 0.7 final.1
  (30 shorter events, 0.1 us)
Async XLA Ops:
  0.6 11.4 %copy-start.13 = (f32[8]{0:T(128)S(1)}, f32[8]{0:T(128)}, u32[]{:S(2)}) copy-start(f32[8]{0:T(128)} %high_ref.3) | copy-start | bytes 100
  0.6 11.4 %copy-start.12 = (f32[8]{0:T(128)S(1)}, f32[8]{0:T(128)}, u32[]{:S(2)}) copy-start(f32[8]{0:T(128)} %low_ref.3) | copy-start | bytes 100
  0.7 11.4 %copy-start.10 = (s32[1,8,256]{2,1,0:T(8,128)S(1)}, s32[1,8,256]{2,1,0:T(8,128)}, u32[]{:S(2)}) copy-start(s32[1,8,256]{2,1,0:T(8,128)} %refine_ref.1) | copy-start | bytes 24580
  1.6 18.7 %collective-permute-start = (bf16[1,64,2048]{2,1,0:T(8,128)(2,1)S(1)}, bf16[1,64,2048]{2,1,0:T(8,128)(2,1)S(1)}, u32[]{:S(2)}, u32[]{:S(2)}) collective-permute-start(bf16[1,64,2048]{2,1,0:T(8,128)(2,1)S(1)} %constant_dynamic-slice_fusion), channel_id=1, source_target_pairs={{96,128},{128,96},{97,129},{129,97},{98,130},{130,98},{99,131},{13... | collective-permute-start | bytes 786440 | tf_op jit(solution)/shard_map/ppermute | solution.py:633
  2.3 1.6 %copy-start = (bf16[8,64,2048]{2,1,0:T(8,128)(2,1)S(1)}, bf16[8,64,2048]{2,1,0:T(8,128)(2,1)}, u32[]{:S(2)}) copy-start(bf16[8,64,2048]{2,1,0:T(8,128)(2,1)} %d_ref.5) | copy-start | bytes 6291460
  3.9 8.1 %copy-start.1 = (bf16[8,64,2048]{2,1,0:T(8,128)(2,1)S(1)}, bf16[8,64,2048]{2,1,0:T(8,128)(2,1)}, u32[]{:S(2)}) copy-start(bf16[8,64,2048]{2,1,0:T(8,128)(2,1)} %d_ref.5) | copy-start | bytes 6291460
  3.9 16.4 %copy-start.2 = (bf16[8,256,256]{2,1,0:T(8,128)(2,1)S(1)}, bf16[8,256,256]{2,1,0:T(8,128)(2,1)}, u32[]{:S(2)}) copy-start(bf16[8,256,256]{2,1,0:T(8,128)(2,1)} %constant.44.clone.low_table) | copy-start | bytes 3145732
  3.9 16.4 %copy-start.3 = (bf16[8,256,256]{2,1,0:T(8,128)(2,1)S(1)}, bf16[8,256,256]{2,1,0:T(8,128)(2,1)}, u32[]{:S(2)}) copy-start(bf16[8,256,256]{2,1,0:T(8,128)(2,1)} %constant.43.clone.high_table) | copy-start | bytes 3145732
  4.1 16.2 %collective-permute-start.1 = (bf16[1,64,2048]{2,1,0:T(8,128)(2,1)S(1)}, bf16[1,64,2048]{2,1,0:T(8,128)(2,1)S(1)}, u32[]{:S(2)}, u32[]{:S(2)}) collective-permute-start(bf16[1,64,2048]{2,1,0:T(8,128)(2,1)S(1)} %get-tuple-element.18), channel_id=1, source_target_pairs={{32,64},{160,192},{64,32},{192,160},{33,65},{161,193},{65,33},{193... | collective-permute-start | bytes 786440 | tf_op jit(solution)/shard_map/ppermute | solution.py:633
  4.9 15.4 %collective-permute-start.2 = (bf16[1,64,2048]{2,1,0:T(8,128)(2,1)S(1)}, bf16[1,64,2048]{2,1,0:T(8,128)(2,1)S(1)}, u32[]{:S(2)}, u32[]{:S(2)}) collective-permute-start(bf16[1,64,2048]{2,1,0:T(8,128)(2,1)S(1)} %get-tuple-element.19), channel_id=1, source_target_pairs={{0,32},{64,96},{128,160},{192,224},{32,0},{96,64},{160,128},{224,1... | collective-permute-start | bytes 786440 | tf_op jit(solution)/shard_map/ppermute | solution.py:633
  9.6 10.7 %collective-permute-start.3 = (f32[8,2048]{1,0:T(8,128)S(1)}, f32[8,2048]{1,0:T(8,128)S(1)}, u32[]{:S(2)}, u32[]{:S(2)}) collective-permute-start(f32[8,2048]{1,0:T(8,128)S(1)} %get-tuple-element.20), channel_id=1, source_target_pairs={{0,1},{2,3},{4,5},{6,7},{8,9},{10,11},{12,13},{14,15},{16,17},{18,... | collective-permute-start | bytes 196616 | tf_op jit(solution)/shard_map/ppermute | solution.py:633
  10.9 9.5 %collective-permute-start.4 = (f32[8,2048]{1,0:T(8,128)S(1)}, f32[8,2048]{1,0:T(8,128)S(1)}, u32[]{:S(2)}, u32[]{:S(2)}) collective-permute-start(f32[8,2048]{1,0:T(8,128)S(1)} %get-tuple-element.21), channel_id=1, source_target_pairs={{1,2},{3,4},{5,6},{7,8},{9,10},{11,12},{13,14},{15,16},{17,18},{19... | collective-permute-start | bytes 196616 | tf_op jit(solution)/shard_map/ppermute | solution.py:633
  22.5 37.4 %copy-start.6 = (f32[32,8,128]{2,1,0:T(8,128)S(1)}, f32[32,8,128]{2,1,0:T(8,128)}, u32[]{:S(2)}) copy-start(f32[32,8,128]{2,1,0:T(8,128)} %constant.46.clone.sin_ref) | copy-start | bytes 393220
  22.5 37.4 %copy-start.7 = (f32[32,8,128]{2,1,0:T(8,128)S(1)}, f32[32,8,128]{2,1,0:T(8,128)}, u32[]{:S(2)}) copy-start(f32[32,8,128]{2,1,0:T(8,128)} %constant.45.clone.cos_ref) | copy-start | bytes 393220
  22.5 37.4 %copy-start.8 = (bf16[128,256]{1,0:T(8,128)(2,1)S(1)}, bf16[128,256]{1,0:T(8,128)(2,1)}, u32[]{:S(2)}) copy-start(bf16[128,256]{1,0:T(8,128)(2,1)} %constant.48.clone.low_table) | copy-start | bytes 196612
  22.5 37.3 %copy-start.9 = (bf16[128,256]{1,0:T(8,128)(2,1)S(1)}, bf16[128,256]{1,0:T(8,128)(2,1)}, u32[]{:S(2)}) copy-start(bf16[128,256]{1,0:T(8,128)(2,1)} %constant.47.clone.high_table) | copy-start | bytes 196612
  22.5 10.3 %collective-permute-start.5 = (f32[264,128]{1,0:T(8,128)S(1)}, f32[264,128]{1,0:T(8,128)S(1)}, u32[]{:S(2)}, u32[]{:S(2)}) collective-permute-start(f32[264,128]{1,0:T(8,128)S(1)} %get-tuple-element.26), channel_id=1, source_target_pairs={{0,32},{32,64},{64,96},{96,0},{1,33},{33,65},{65,97},{97,1},{2,34}... | collective-permute-start | bytes 405512 | tf_op jit(solution)/shard_map/ppermute | solution.py:627
  22.6 11.9 %collective-permute-start.6 = (f32[264,128]{1,0:T(8,128)S(1)}, f32[264,128]{1,0:T(8,128)S(1)}, u32[]{:S(2)}, u32[]{:S(2)}) collective-permute-start(f32[264,128]{1,0:T(8,128)S(1)} %get-tuple-element.27), channel_id=1, source_target_pairs={{0,64},{32,96},{64,0},{96,32},{1,65},{33,97},{65,1},{97,33},{2,66}... | collective-permute-start | bytes 405512 | tf_op jit(solution)/shard_map/ppermute | solution.py:627
  30.6 5.4 %collective-permute-start.7 = (f32[264,128]{1,0:T(8,128)S(1)}, f32[264,128]{1,0:T(8,128)S(1)}, u32[]{:S(2)}, u32[]{:S(2)}) collective-permute-start(f32[264,128]{1,0:T(8,128)S(1)} %get-tuple-element.28), channel_id=1, source_target_pairs={{0,96},{32,0},{64,32},{96,64},{1,97},{33,1},{65,33},{97,65},{2,98}... | collective-permute-start | bytes 405512 | tf_op jit(solution)/shard_map/ppermute | solution.py:627
  32.6 45.3 %copy-start.4 = (bf16[4,512,256]{2,1,0:T(8,128)(2,1)S(1)}, bf16[4,512,256]{2,1,0:T(8,128)(2,1)}, u32[]{:S(2)}) copy-start(bf16[4,512,256]{2,1,0:T(8,128)(2,1)} %constant.51.clone.low_table) | copy-start | bytes 3145732
  32.6 45.3 %copy-start.5 = (bf16[4,512,256]{2,1,0:T(8,128)(2,1)S(1)}, bf16[4,512,256]{2,1,0:T(8,128)(2,1)}, u32[]{:S(2)}) copy-start(bf16[4,512,256]{2,1,0:T(8,128)(2,1)} %constant.50.clone.high_table) | copy-start | bytes 3145732
  32.6 45.3 %copy-start.11 = (f32[16]{0:T(128)S(1)}, f32[16]{0:T(128)}, u32[]{:S(2)}) copy-start(f32[16]{0:T(128)} %constant.49.clone.eighth_ref) | copy-start | bytes 196
  79.2 6.1 %collective-permute-start.8 = (f32[128,256]{1,0:T(8,128)S(1)}, f32[128,256]{1,0:T(8,128)S(1)}, u32[]{:S(2)}, u32[]{:S(2)}) collective-permute-start(f32[128,256]{1,0:T(8,128)S(1)} %get-tuple-element.31), channel_id=1, source_target_pairs={{0,32},{32,64},{64,96},{96,0},{1,33},{33,65},{65,97},{97,1},{2,34}... | collective-permute-start | bytes 393224 | tf_op jit(solution)/shard_map/ppermute | solution.py:627
  79.3 9.4 %collective-permute-start.9 = (f32[128,256]{1,0:T(8,128)S(1)}, f32[128,256]{1,0:T(8,128)S(1)}, u32[]{:S(2)}, u32[]{:S(2)}) collective-permute-start(f32[128,256]{1,0:T(8,128)S(1)} %get-tuple-element.32), channel_id=1, source_target_pairs={{0,64},{32,96},{64,0},{96,32},{1,65},{33,97},{65,1},{97,33},{2,66}... | collective-permute-start | bytes 393224 | tf_op jit(solution)/shard_map/ppermute | solution.py:627
  82.5 6.2 %collective-permute-start.10 = (f32[128,256]{1,0:T(8,128)S(1)}, f32[128,256]{1,0:T(8,128)S(1)}, u32[]{:S(2)}, u32[]{:S(2)}) collective-permute-start(f32[128,256]{1,0:T(8,128)S(1)} %get-tuple-element.33), channel_id=1, source_target_pairs={{0,96},{32,0},{64,32},{96,64},{1,97},{33,1},{65,33},{97,65},{2,98}... | collective-permute-start | bytes 393224 | tf_op jit(solution)/shard_map/ppermute | solution.py:627

commit v11 on v10

--- a/solution.py
+++ b/solution.py
@@ -624,7 +624,7 @@
 
 def deliver(pieces):
     return [pieces[0]] + [
-        lax.ppermute(pieces[a], "x", [(i, (i + a) % 4) for i in range(4)]) for a in (1, 2, 3)
+        lax.ppermute(pieces[a], "x", [(i, (i + a) % 4) for i in range(4)]) for a in (2, 1, 3)
     ]
 
 

time: 89.6 us -> 89.2 us (level)
  blocking collectives: 40.6 us -> 39 us
  waiting for transfers between devices: 8.52 us -> 9.47 us
    all_to_all x1, blocking collectives: 23.5 us -> 21.9 us  [body(): pieces = lax.all_to_all(turn(summed), ('zhi', 'sky'), 0, 0, tiled=True)]
    ppermute x6, waiting for transfers between devices: 8.51 us -> 9.46 us  [deliver(): lax.ppermute(pieces[a], 'x', [(i, (i + a) % 4) for i in range(4)])]
  transfers between devices with their start and end apart: 11 -> 11, of which waited for: 4 -> 3; matrix products, arithmetic and copies ran while one was open for 0% -> 0% of each run, Pallas kernels for 11% -> 11%
where the time goes in v11:
time: 89.2 us; the launch traced here: 89 us
  blocking collectives  39 us (44%)
  starting transfers between devices  22.3 us (25%)
  Pallas kernels  14.8 us (17%)
  waiting for transfers between devices  9.47 us (11%)
  local copies, waits for them, and re-layouts  2.62 us (3%)
    all_to_all x1, blocking collectives, body(): pieces = lax.all_to_all(turn(summed), ('zhi', 'sky'), 0, 0, tiled=True)  21.9 us
    all_to_all x1, blocking collectives, body(): pieces = lax.all_to_all(pieces, ('zhi', 'sky'), 0, 0, tiled=True)  17.1 us
    ppermute x6, starting transfers between devices, deliver(): lax.ppermute(pieces[a], 'x', [(i, (i + a) % 4) for i in range(4)])  13.7 us
    ppermute x6, waiting for transfers between devices, deliver(): lax.ppermute(pieces[a], 'x', [(i, (i + a) % 4) for i in range(4)])  9.46 us
    ppermute x5, starting transfers between devices, swap(): return lax.ppermute(array, axes, pairs + [(b, a) for a, b in pairs])  8.61 us
    pallas_call x1, Pallas kernels, inner_sums(): pl.pallas_call(inner_kernel, out_shape=(jax.ShapeDtypeStruct((ROWS + 8, N...  8.23 us
    pallas_call x1, Pallas kernels, outer_sums(): pl.pallas_call(outer_kernel, out_shape=(piece, piece, piece, jax.ShapeDty...  2.08 us
  transfers between devices with their start and end apart: 11, of which 3 were waited for; matrix products, arithmetic and copies ran while one was open for 0% of the time, Pallas kernels for 11%

profile of v11, /device:TPU:1, one launch (start us, length us, event | category | flops | bytes accessed | tf_op | source)
XLA Modules:
  0.0 89.0 jit_solution(7303287533325161340)
XLA Ops:
  0.7 1.0 %constant_dynamic-slice_fusion = bf16[1,64,2048]{2,1,0:T(8,128)(2,1)S(1)} fusion(bf16[8,64,2048]{2,1,0:T(8,128)(2,1)} %d_ref.5, s32[]{:T(128)S(6)} %select_n.13), kind=kLoop, calls=%fused_computation | loop fusion | bytes 524292 | tf_op jit(solution)/shard_map/dynamic_slice | solution.py:636
  1.6 0.7 collective-permute-start
  2.3 0.0 copy-start
  2.3 1.6 %copy-done = bf16[8,64,2048]{2,1,0:T(8,128)(2,1)S(1)} copy-done((bf16[8,64,2048]{2,1,0:T(8,128)(2,1)S(1)}, bf16[8,64,2048]{2,1,0:T(8,128)(2,1)}, u32[]{:S(2)}) %copy-start) | copy-done | bytes 2097176
  3.9 0.2 edge_rows.1
  4.1 0.8 collective-permute-start.1
  4.9 4.7 %collective-permute-start.2 = (bf16[1,64,2048]{2,1,0:T(8,128)(2,1)S(1)}, bf16[1,64,2048]{2,1,0:T(8,128)(2,1)S(1)}, u32[]{:S(2)}, u32[]{:S(2)}) collective-permute-start(bf16[1,64,2048]{2,1,0:T(8,128)(2,1)S(1)} %get-tuple-element.19), channel_id=1, source_target_pairs={{0,32},{64,96},{128,160},{192,224},{32,0},{96,64},{160,128},{224,1... | collective-permute-start | bytes 786440 | tf_op jit(solution)/shard_map/ppermute | solution.py:633
  9.6 1.2 %collective-permute-start.3 = (f32[8,2048]{1,0:T(8,128)S(1)}, f32[8,2048]{1,0:T(8,128)S(1)}, u32[]{:S(2)}, u32[]{:S(2)}) collective-permute-start(f32[8,2048]{1,0:T(8,128)S(1)} %get-tuple-element.20), channel_id=1, source_target_pairs={{0,1},{2,3},{4,5},{6,7},{8,9},{10,11},{12,13},{14,15},{16,17},{18,... | collective-permute-start | bytes 196616 | tf_op jit(solution)/shard_map/ppermute | solution.py:633
  10.9 1.2 %collective-permute-start.4 = (f32[8,2048]{1,0:T(8,128)S(1)}, f32[8,2048]{1,0:T(8,128)S(1)}, u32[]{:S(2)}, u32[]{:S(2)}) collective-permute-start(f32[8,2048]{1,0:T(8,128)S(1)} %get-tuple-element.21), channel_id=1, source_target_pairs={{1,2},{3,4},{5,6},{7,8},{9,10},{11,12},{13,14},{15,16},{17,18},{19... | collective-permute-start | bytes 196616 | tf_op jit(solution)/shard_map/ppermute | solution.py:633
  12.1 8.2 %inner_sums.1 = (f32[72,2048]{1,0:T(8,128)S(1)}, f32[8,2048]{1,0:T(8,128)S(1)}, f32[4,8,2048]{2,1,0:T(8,128)S(1)}) custom-call(f32[8]{0:T(128)S(1)} %copy-done.12, f32[8]{0:T(128)S(1)} %copy-done.13, bf16[8,64,2048]{2,1,0:T(8,128)(2,1)S(1)} %copy-done.1, s32[1,8,256]{2,1,0:T(8,128)S(1)} %copy-done.10), custom_call_target="tpu_custom_call" | custom-call | flops 40000000 | bytes 25165824 | tf_op jit(solution)/shard_map/inner_sums/pallas_call | solution.py:243
  20.3 0.0 collective-permute-done.4.other_row_ref
  20.4 2.1 %outer_sums.1 = (f32[264,128]{1,0:T(8,128)S(1)}, f32[264,128]{1,0:T(8,128)S(1)}, f32[264,128]{1,0:T(8,128)S(1)}, bf16[8,160,256]{2,1,0:T(8,128)(2,1)S(1)}) custom-call(f32[8]{0:T(128)S(1)} %copy-done.12, f32[8]{0:T(128)S(1)} %copy-done.13, bf16[8,64,2048]{2,1,0:T(8,128)(2,1)S(1)} %copy-done.1, bf16[1,64,2048]{2,1,0:T(8,128)(2,1)S(1)} %collective-permute-done.cross_ref, ...), custom_call_target="tpu_custom_call" | custom-call | tf_op jit(solution)/shard_map/outer_sums/pallas_call | solution.py:373
  22.5 0.0 copy-start.6
  22.5 0.0 copy-start.7
  22.5 0.0 copy-start.8
  22.5 0.0 copy-start.9
  22.5 8.0 %collective-permute-start.5 = (f32[264,128]{1,0:T(8,128)S(1)}, f32[264,128]{1,0:T(8,128)S(1)}, u32[]{:S(2)}, u32[]{:S(2)}) collective-permute-start(f32[264,128]{1,0:T(8,128)S(1)} %get-tuple-element.26), channel_id=1, source_target_pairs={{0,64},{32,96},{64,0},{96,32},{1,65},{33,97},{65,1},{97,33},{2,66}... | collective-permute-start | bytes 405512 | tf_op jit(solution)/shard_map/ppermute | solution.py:627
  30.6 2.7 %collective-permute-start.7 = (f32[264,128]{1,0:T(8,128)S(1)}, f32[264,128]{1,0:T(8,128)S(1)}, u32[]{:S(2)}, u32[]{:S(2)}) collective-permute-start(f32[264,128]{1,0:T(8,128)S(1)} %get-tuple-element.28), channel_id=1, source_target_pairs={{0,96},{32,0},{64,32},{96,64},{1,97},{33,1},{65,33},{97,65},{2,98}... | collective-permute-start | bytes 405512 | tf_op jit(solution)/shard_map/ppermute | solution.py:627
  33.2 0.2 other_sums.1.a_ref
  33.5 3.6 %collective-permute-done.6.c_ref = f32[264,128]{1,0:T(8,128)S(1)} collective-permute-done((f32[264,128]{1,0:T(8,128)S(1)}, f32[264,128]{1,0:T(8,128)S(1)}, u32[]{:S(2)}, u32[]{:S(2)}) %collective-permute-start.6) | collective-permute-done | bytes 135200 | tf_op jit(solution)/shard_map/ppermute | solution.py:627
  37.1 0.3 turn.1
  37.4 21.9 %all_to_all.10.in_ref = f32[64,1,640]{2,1,0:T(1,128)S(1)} all-to-all(f32[64,1,640]{2,1,0:T(1,128)S(1)} %turn.1), channel_id=1, replica_groups=mesh['zhi'=2,'x'=4,'sky'=32] {'zhi','sky'}, dimensions={0} | all-to-all | bytes 327680 | tf_op jit(solution)/shard_map/all_to_all | solution.py:649
  59.4 1.0 %solve.1 = f32[64,8,128]{2,1,0:T(8,128)S(1)} custom-call(f32[64,1,640]{2,1,0:T(1,128)S(1)} %all_to_all.10.in_ref, f32[32,8,128]{2,1,0:T(8,128)S(1)} %copy-done.7, f32[32,8,128]{2,1,0:T(8,128)S(1)} %copy-done.6, bf16[128,256]{1,0:T(8,128)(2,1)S(1)} %copy-done.9, bf16[128,256]{1,0:T(8,128)(2,1)S(1)} %copy-done.8), custom_call_target="tpu_custom_call" | custom-call | tf_op jit(solution)/shard_map/solve/pallas_call | solution.py:542
  60.4 17.1 %all_to_all.11.in_ref = f32[64,8,128]{2,1,0:T(8,128)S(1)} all-to-all(f32[64,8,128]{2,1,0:T(8,128)S(1)} %solve.1), channel_id=1, replica_groups=mesh['zhi'=2,'x'=4,'sky'=32] {'zhi','sky'}, dimensions={0} | all-to-all | bytes 524288 | tf_op jit(solution)/shard_map/all_to_all | solution.py:651
  77.4 1.2 %back.1 = (f32[128,256]{1,0:T(8,128)S(1)}, f32[128,256]{1,0:T(8,128)S(1)}, f32[128,256]{1,0:T(8,128)S(1)}, f32[128,512]{1,0:T(8,128)S(1)}, f32[128,512]{1,0:T(8,128)S(1)}) custom-call(f32[16]{0:T(128)S(1)} %copy-done.11, f32[64,8,128]{2,1,0:T(8,128)S(1)} %all_to_all.11.in_ref, bf16[4,512,256]{2,1,0:T(8,128)(2,1)S(1)} %copy-done.5, ...), custom_call_target="tpu_custom_call" | custom-call | tf_op jit(solution)/shard_map/back/pallas_call | solution.py:588
  78.7 0.3 collective-permute-start.8
  79.0 0.9 %collective-permute-start.9 = (f32[128,256]{1,0:T(8,128)S(1)}, f32[128,256]{1,0:T(8,128)S(1)}, u32[]{:S(2)}, u32[]{:S(2)}) collective-permute-start(f32[128,256]{1,0:T(8,128)S(1)} %get-tuple-element.32), channel_id=1, source_target_pairs={{0,32},{32,64},{64,96},{96,0},{1,33},{33,65},{65,97},{97,1},{2,34}... | collective-permute-start | bytes 393224 | tf_op jit(solution)/shard_map/ppermute | solution.py:627
  79.9 1.8 %collective-permute-start.10 = (f32[128,256]{1,0:T(8,128)S(1)}, f32[128,256]{1,0:T(8,128)S(1)}, u32[]{:S(2)}, u32[]{:S(2)}) collective-permute-start(f32[128,256]{1,0:T(8,128)S(1)} %get-tuple-element.33), channel_id=1, source_target_pairs={{0,96},{32,0},{64,32},{96,64},{1,97},{33,1},{65,33},{97,65},{2,98}... | collective-permute-start | bytes 393224 | tf_op jit(solution)/shard_map/ppermute | solution.py:627
  81.6 0.8 back_rest.1.a_ref
  82.5 2.7 %collective-permute-done.8.b_ref = f32[128,256]{1,0:T(8,128)S(1)} collective-permute-done((f32[128,256]{1,0:T(8,128)S(1)}, f32[128,256]{1,0:T(8,128)S(1)}, u32[]{:S(2)}, u32[]{:S(2)}) %collective-permute-start.8) | collective-permute-done | bytes 131104 | tf_op jit(solution)/shard_map/ppermute | solution.py:627
  85.1 3.2 %collective-permute-done.9.c_ref = f32[128,256]{1,0:T(8,128)S(1)} collective-permute-done((f32[128,256]{1,0:T(8,128)S(1)}, f32[128,256]{1,0:T(8,128)S(1)}, u32[]{:S(2)}, u32[]{:S(2)}) %collective-permute-start.9) | collective-permute-done | bytes 131104 | tf_op jit(solution)/shard_map/ppermute | solution.py:627
  88.3 0.7 final.1
  (30 shorter events, 0.1 us)
Async XLA Ops:
  0.6 11.4 %copy-start.13 = (f32[8]{0:T(128)S(1)}, f32[8]{0:T(128)}, u32[]{:S(2)}) copy-start(f32[8]{0:T(128)} %high_ref.3) | copy-start | bytes 100
  0.6 11.4 %copy-start.12 = (f32[8]{0:T(128)S(1)}, f32[8]{0:T(128)}, u32[]{:S(2)}) copy-start(f32[8]{0:T(128)} %low_ref.3) | copy-start | bytes 100
  0.7 11.4 %copy-start.10 = (s32[1,8,256]{2,1,0:T(8,128)S(1)}, s32[1,8,256]{2,1,0:T(8,128)}, u32[]{:S(2)}) copy-start(s32[1,8,256]{2,1,0:T(8,128)} %refine_ref.1) | copy-start | bytes 24580
  1.6 18.7 %collective-permute-start = (bf16[1,64,2048]{2,1,0:T(8,128)(2,1)S(1)}, bf16[1,64,2048]{2,1,0:T(8,128)(2,1)S(1)}, u32[]{:S(2)}, u32[]{:S(2)}) collective-permute-start(bf16[1,64,2048]{2,1,0:T(8,128)(2,1)S(1)} %constant_dynamic-slice_fusion), channel_id=1, source_target_pairs={{96,128},{128,96},{97,129},{129,97},{98,130},{130,98},{99,131},{13... | collective-permute-start | bytes 786440 | tf_op jit(solution)/shard_map/ppermute | solution.py:633
  2.3 1.6 %copy-start = (bf16[8,64,2048]{2,1,0:T(8,128)(2,1)S(1)}, bf16[8,64,2048]{2,1,0:T(8,128)(2,1)}, u32[]{:S(2)}) copy-start(bf16[8,64,2048]{2,1,0:T(8,128)(2,1)} %d_ref.5) | copy-start | bytes 6291460
  3.9 8.1 %copy-start.1 = (bf16[8,64,2048]{2,1,0:T(8,128)(2,1)S(1)}, bf16[8,64,2048]{2,1,0:T(8,128)(2,1)}, u32[]{:S(2)}) copy-start(bf16[8,64,2048]{2,1,0:T(8,128)(2,1)} %d_ref.5) | copy-start | bytes 6291460
  3.9 16.4 %copy-start.2 = (bf16[8,256,256]{2,1,0:T(8,128)(2,1)S(1)}, bf16[8,256,256]{2,1,0:T(8,128)(2,1)}, u32[]{:S(2)}) copy-start(bf16[8,256,256]{2,1,0:T(8,128)(2,1)} %constant.44.clone.low_table) | copy-start | bytes 3145732
  3.9 16.4 %copy-start.3 = (bf16[8,256,256]{2,1,0:T(8,128)(2,1)S(1)}, bf16[8,256,256]{2,1,0:T(8,128)(2,1)}, u32[]{:S(2)}) copy-start(bf16[8,256,256]{2,1,0:T(8,128)(2,1)} %constant.43.clone.high_table) | copy-start | bytes 3145732
  4.1 16.2 %collective-permute-start.1 = (bf16[1,64,2048]{2,1,0:T(8,128)(2,1)S(1)}, bf16[1,64,2048]{2,1,0:T(8,128)(2,1)S(1)}, u32[]{:S(2)}, u32[]{:S(2)}) collective-permute-start(bf16[1,64,2048]{2,1,0:T(8,128)(2,1)S(1)} %get-tuple-element.18), channel_id=1, source_target_pairs={{32,64},{160,192},{64,32},{192,160},{33,65},{161,193},{65,33},{193... | collective-permute-start | bytes 786440 | tf_op jit(solution)/shard_map/ppermute | solution.py:633
  4.9 15.4 %collective-permute-start.2 = (bf16[1,64,2048]{2,1,0:T(8,128)(2,1)S(1)}, bf16[1,64,2048]{2,1,0:T(8,128)(2,1)S(1)}, u32[]{:S(2)}, u32[]{:S(2)}) collective-permute-start(bf16[1,64,2048]{2,1,0:T(8,128)(2,1)S(1)} %get-tuple-element.19), channel_id=1, source_target_pairs={{0,32},{64,96},{128,160},{192,224},{32,0},{96,64},{160,128},{224,1... | collective-permute-start | bytes 786440 | tf_op jit(solution)/shard_map/ppermute | solution.py:633
  9.6 10.7 %collective-permute-start.3 = (f32[8,2048]{1,0:T(8,128)S(1)}, f32[8,2048]{1,0:T(8,128)S(1)}, u32[]{:S(2)}, u32[]{:S(2)}) collective-permute-start(f32[8,2048]{1,0:T(8,128)S(1)} %get-tuple-element.20), channel_id=1, source_target_pairs={{0,1},{2,3},{4,5},{6,7},{8,9},{10,11},{12,13},{14,15},{16,17},{18,... | collective-permute-start | bytes 196616 | tf_op jit(solution)/shard_map/ppermute | solution.py:633
  10.9 9.5 %collective-permute-start.4 = (f32[8,2048]{1,0:T(8,128)S(1)}, f32[8,2048]{1,0:T(8,128)S(1)}, u32[]{:S(2)}, u32[]{:S(2)}) collective-permute-start(f32[8,2048]{1,0:T(8,128)S(1)} %get-tuple-element.21), channel_id=1, source_target_pairs={{1,2},{3,4},{5,6},{7,8},{9,10},{11,12},{13,14},{15,16},{17,18},{19... | collective-permute-start | bytes 196616 | tf_op jit(solution)/shard_map/ppermute | solution.py:633
  22.5 36.9 %copy-start.6 = (f32[32,8,128]{2,1,0:T(8,128)S(1)}, f32[32,8,128]{2,1,0:T(8,128)}, u32[]{:S(2)}) copy-start(f32[32,8,128]{2,1,0:T(8,128)} %constant.46.clone.sin_ref) | copy-start | bytes 393220
  22.5 36.8 %copy-start.7 = (f32[32,8,128]{2,1,0:T(8,128)S(1)}, f32[32,8,128]{2,1,0:T(8,128)}, u32[]{:S(2)}) copy-start(f32[32,8,128]{2,1,0:T(8,128)} %constant.45.clone.cos_ref) | copy-start | bytes 393220
  22.5 36.8 %copy-start.8 = (bf16[128,256]{1,0:T(8,128)(2,1)S(1)}, bf16[128,256]{1,0:T(8,128)(2,1)}, u32[]{:S(2)}) copy-start(bf16[128,256]{1,0:T(8,128)(2,1)} %constant.48.clone.low_table) | copy-start | bytes 196612
  22.5 36.8 %copy-start.9 = (bf16[128,256]{1,0:T(8,128)(2,1)S(1)}, bf16[128,256]{1,0:T(8,128)(2,1)}, u32[]{:S(2)}) copy-start(bf16[128,256]{1,0:T(8,128)(2,1)} %constant.47.clone.high_table) | copy-start | bytes 196612
  22.5 10.9 %collective-permute-start.5 = (f32[264,128]{1,0:T(8,128)S(1)}, f32[264,128]{1,0:T(8,128)S(1)}, u32[]{:S(2)}, u32[]{:S(2)}) collective-permute-start(f32[264,128]{1,0:T(8,128)S(1)} %get-tuple-element.26), channel_id=1, source_target_pairs={{0,64},{32,96},{64,0},{96,32},{1,65},{33,97},{65,1},{97,33},{2,66}... | collective-permute-start | bytes 405512 | tf_op jit(solution)/shard_map/ppermute | solution.py:627
  30.6 6.5 %collective-permute-start.6 = (f32[264,128]{1,0:T(8,128)S(1)}, f32[264,128]{1,0:T(8,128)S(1)}, u32[]{:S(2)}, u32[]{:S(2)}) collective-permute-start(f32[264,128]{1,0:T(8,128)S(1)} %get-tuple-element.27), channel_id=1, source_target_pairs={{0,32},{32,64},{64,96},{96,0},{1,33},{33,65},{65,97},{97,1},{2,34}... | collective-permute-start | bytes 405512 | tf_op jit(solution)/shard_map/ppermute | solution.py:627
  30.6 6.5 %collective-permute-start.7 = (f32[264,128]{1,0:T(8,128)S(1)}, f32[264,128]{1,0:T(8,128)S(1)}, u32[]{:S(2)}, u32[]{:S(2)}) collective-permute-start(f32[264,128]{1,0:T(8,128)S(1)} %get-tuple-element.28), channel_id=1, source_target_pairs={{0,96},{32,0},{64,32},{96,64},{1,97},{33,1},{65,33},{97,65},{2,98}... | collective-permute-start | bytes 405512 | tf_op jit(solution)/shard_map/ppermute | solution.py:627
  33.2 44.2 %copy-start.4 = (bf16[4,512,256]{2,1,0:T(8,128)(2,1)S(1)}, bf16[4,512,256]{2,1,0:T(8,128)(2,1)}, u32[]{:S(2)}) copy-start(bf16[4,512,256]{2,1,0:T(8,128)(2,1)} %constant.51.clone.low_table) | copy-start | bytes 3145732
  33.2 44.2 %copy-start.5 = (bf16[4,512,256]{2,1,0:T(8,128)(2,1)S(1)}, bf16[4,512,256]{2,1,0:T(8,128)(2,1)}, u32[]{:S(2)}) copy-start(bf16[4,512,256]{2,1,0:T(8,128)(2,1)} %constant.50.clone.high_table) | copy-start | bytes 3145732
  33.2 44.2 %copy-start.11 = (f32[16]{0:T(128)S(1)}, f32[16]{0:T(128)}, u32[]{:S(2)}) copy-start(f32[16]{0:T(128)} %constant.49.clone.eighth_ref) | copy-start | bytes 196
  78.7 6.5 %collective-permute-start.8 = (f32[128,256]{1,0:T(8,128)S(1)}, f32[128,256]{1,0:T(8,128)S(1)}, u32[]{:S(2)}, u32[]{:S(2)}) collective-permute-start(f32[128,256]{1,0:T(8,128)S(1)} %get-tuple-element.31), channel_id=1, source_target_pairs={{0,64},{32,96},{64,0},{96,32},{1,65},{33,97},{65,1},{97,33},{2,66}... | collective-permute-start | bytes 393224 | tf_op jit(solution)/shard_map/ppermute | solution.py:627
  79.0 9.4 %collective-permute-start.9 = (f32[128,256]{1,0:T(8,128)S(1)}, f32[128,256]{1,0:T(8,128)S(1)}, u32[]{:S(2)}, u32[]{:S(2)}) collective-permute-start(f32[128,256]{1,0:T(8,128)S(1)} %get-tuple-element.32), channel_id=1, source_target_pairs={{0,32},{32,64},{64,96},{96,0},{1,33},{33,65},{65,97},{97,1},{2,34}... | collective-permute-start | bytes 393224 | tf_op jit(solution)/shard_map/ppermute | solution.py:627
  79.9 8.5 %collective-permute-start.10 = (f32[128,256]{1,0:T(8,128)S(1)}, f32[128,256]{1,0:T(8,128)S(1)}, u32[]{:S(2)}, u32[]{:S(2)}) collective-permute-start(f32[128,256]{1,0:T(8,128)S(1)} %get-tuple-element.33), channel_id=1, source_target_pairs={{0,96},{32,0},{64,32},{96,64},{1,97},{33,1},{65,33},{97,65},{2,98}... | collective-permute-start | bytes 393224 | tf_op jit(solution)/shard_map/ppermute | solution.py:627

commit v12 on v11

--- a/solution.py
+++ b/solution.py
@@ -604,22 +604,34 @@
     return own, one, two, three
 
 
-def final_kernel(a_ref, b_ref, c_ref, d_ref, x_ref, y_ref):
-    total = (a_ref[...] + b_ref[...]) + (c_ref[...] + d_ref[...])
+def early_kernel(a_ref, b_ref, c_ref, sum_ref):
+    sum_ref[...] = (a_ref[...] + b_ref[...]) + c_ref[...]
+
+
+def final_kernel(sum_ref, last_ref, x_ref, y_ref):
+    total = sum_ref[...] + last_ref[...]
     x_ref[...] = total[:ROWS]
     y_ref[...] = total[ROWS:]
 
 
 def final(pieces):
+    early = pl.pallas_call(
+        early_kernel,
+        out_shape=jax.ShapeDtypeStruct((128, 256), f32),
+        in_specs=[VM] * 3,
+        out_specs=VM,
+        compiler_params=limit(24),
+        name="early",
+    )(*pieces[:3])
     shape = jax.ShapeDtypeStruct((ROWS, 256), f32)
     return pl.pallas_call(
         final_kernel,
         out_shape=(shape, shape),
-        in_specs=[VM] * 4,
+        in_specs=[VM] * 2,
         out_specs=(VM, VM),
         compiler_params=limit(24),
         name="final",
-    )(*pieces)
+    )(early, pieces[3])
 
 
 def deliver(pieces):

time: 89.2 us -> 89.3 us (level)
  no operation moved by 1% of the time
where the time goes in v12:
time: 89.3 us; the launch traced here: 89 us
  blocking collectives  39 us (44%)
  starting transfers between devices  22.3 us (25%)
  Pallas kernels  14.8 us (17%)
  waiting for transfers between devices  9.47 us (11%)
  local copies, waits for them, and re-layouts  2.62 us (3%)
    all_to_all x1, blocking collectives, body(): pieces = lax.all_to_all(turn(summed), ('zhi', 'sky'), 0, 0, tiled=True)  21.9 us
    all_to_all x1, blocking collectives, body(): pieces = lax.all_to_all(pieces, ('zhi', 'sky'), 0, 0, tiled=True)  17.1 us
    ppermute x6, starting transfers between devices, deliver(): lax.ppermute(pieces[a], 'x', [(i, (i + a) % 4) for i in range(4)])  13.7 us
    ppermute x6, waiting for transfers between devices, deliver(): lax.ppermute(pieces[a], 'x', [(i, (i + a) % 4) for i in range(4)])  9.46 us
    ppermute x5, starting transfers between devices, swap(): return lax.ppermute(array, axes, pairs + [(b, a) for a, b in pairs])  8.61 us
    pallas_call x1, Pallas kernels, inner_sums(): pl.pallas_call(inner_kernel, out_shape=(jax.ShapeDtypeStruct((ROWS + 8, N...  8.23 us
    pallas_call x1, Pallas kernels, outer_sums(): pl.pallas_call(outer_kernel, out_shape=(piece, piece, piece, jax.ShapeDty...  2.08 us
  transfers between devices with their start and end apart: 11, of which 3 were waited for; matrix products, arithmetic and copies ran while one was open for 0% of the time, Pallas kernels for 11%

profile of v12, /device:TPU:1, one launch (start us, length us, event | category | flops | bytes accessed | tf_op | source)
XLA Modules:
  0.0 89.0 jit_solution(12474688085874861446)
XLA Ops:
  0.7 1.0 %constant_dynamic-slice_fusion = bf16[1,64,2048]{2,1,0:T(8,128)(2,1)S(1)} fusion(bf16[8,64,2048]{2,1,0:T(8,128)(2,1)} %d_ref.5, s32[]{:T(128)S(6)} %select_n.13), kind=kLoop, calls=%fused_computation | loop fusion | bytes 524292 | tf_op jit(solution)/shard_map/dynamic_slice | solution.py:648
  1.6 0.7 collective-permute-start
  2.3 0.0 copy-start
  2.3 1.6 %copy-done = bf16[8,64,2048]{2,1,0:T(8,128)(2,1)S(1)} copy-done((bf16[8,64,2048]{2,1,0:T(8,128)(2,1)S(1)}, bf16[8,64,2048]{2,1,0:T(8,128)(2,1)}, u32[]{:S(2)}) %copy-start) | copy-done | bytes 2097176
  3.9 0.2 edge_rows.1
  4.1 0.8 collective-permute-start.1
  4.9 4.7 %collective-permute-start.2 = (bf16[1,64,2048]{2,1,0:T(8,128)(2,1)S(1)}, bf16[1,64,2048]{2,1,0:T(8,128)(2,1)S(1)}, u32[]{:S(2)}, u32[]{:S(2)}) collective-permute-start(bf16[1,64,2048]{2,1,0:T(8,128)(2,1)S(1)} %get-tuple-element.19), channel_id=1, source_target_pairs={{0,32},{64,96},{128,160},{192,224},{32,0},{96,64},{160,128},{224,1... | collective-permute-start | bytes 786440 | tf_op jit(solution)/shard_map/ppermute | solution.py:645
  9.6 1.2 %collective-permute-start.3 = (f32[8,2048]{1,0:T(8,128)S(1)}, f32[8,2048]{1,0:T(8,128)S(1)}, u32[]{:S(2)}, u32[]{:S(2)}) collective-permute-start(f32[8,2048]{1,0:T(8,128)S(1)} %get-tuple-element.20), channel_id=1, source_target_pairs={{0,1},{2,3},{4,5},{6,7},{8,9},{10,11},{12,13},{14,15},{16,17},{18,... | collective-permute-start | bytes 196616 | tf_op jit(solution)/shard_map/ppermute | solution.py:645
  10.9 1.2 %collective-permute-start.4 = (f32[8,2048]{1,0:T(8,128)S(1)}, f32[8,2048]{1,0:T(8,128)S(1)}, u32[]{:S(2)}, u32[]{:S(2)}) collective-permute-start(f32[8,2048]{1,0:T(8,128)S(1)} %get-tuple-element.21), channel_id=1, source_target_pairs={{1,2},{3,4},{5,6},{7,8},{9,10},{11,12},{13,14},{15,16},{17,18},{19... | collective-permute-start | bytes 196616 | tf_op jit(solution)/shard_map/ppermute | solution.py:645
  12.1 8.2 %inner_sums.1 = (f32[72,2048]{1,0:T(8,128)S(1)}, f32[8,2048]{1,0:T(8,128)S(1)}, f32[4,8,2048]{2,1,0:T(8,128)S(1)}) custom-call(f32[8]{0:T(128)S(1)} %copy-done.12, f32[8]{0:T(128)S(1)} %copy-done.13, bf16[8,64,2048]{2,1,0:T(8,128)(2,1)S(1)} %copy-done.1, s32[1,8,256]{2,1,0:T(8,128)S(1)} %copy-done.10), custom_call_target="tpu_custom_call" | custom-call | flops 40000000 | bytes 25165824 | tf_op jit(solution)/shard_map/inner_sums/pallas_call | solution.py:243
  20.3 0.0 collective-permute-done.4.other_row_ref
  20.4 2.1 %outer_sums.1 = (f32[264,128]{1,0:T(8,128)S(1)}, f32[264,128]{1,0:T(8,128)S(1)}, f32[264,128]{1,0:T(8,128)S(1)}, bf16[8,160,256]{2,1,0:T(8,128)(2,1)S(1)}) custom-call(f32[8]{0:T(128)S(1)} %copy-done.12, f32[8]{0:T(128)S(1)} %copy-done.13, bf16[8,64,2048]{2,1,0:T(8,128)(2,1)S(1)} %copy-done.1, bf16[1,64,2048]{2,1,0:T(8,128)(2,1)S(1)} %collective-permute-done.cross_ref, ...), custom_call_target="tpu_custom_call" | custom-call | tf_op jit(solution)/shard_map/outer_sums/pallas_call | solution.py:373
  22.5 0.0 copy-start.6
  22.5 0.0 copy-start.7
  22.5 0.0 copy-start.8
  22.5 0.0 copy-start.9
  22.5 8.0 %collective-permute-start.5 = (f32[264,128]{1,0:T(8,128)S(1)}, f32[264,128]{1,0:T(8,128)S(1)}, u32[]{:S(2)}, u32[]{:S(2)}) collective-permute-start(f32[264,128]{1,0:T(8,128)S(1)} %get-tuple-element.26), channel_id=1, source_target_pairs={{0,64},{32,96},{64,0},{96,32},{1,65},{33,97},{65,1},{97,33},{2,66}... | collective-permute-start | bytes 405512 | tf_op jit(solution)/shard_map/ppermute | solution.py:639
  30.6 2.7 %collective-permute-start.7 = (f32[264,128]{1,0:T(8,128)S(1)}, f32[264,128]{1,0:T(8,128)S(1)}, u32[]{:S(2)}, u32[]{:S(2)}) collective-permute-start(f32[264,128]{1,0:T(8,128)S(1)} %get-tuple-element.28), channel_id=1, source_target_pairs={{0,96},{32,0},{64,32},{96,64},{1,97},{33,1},{65,33},{97,65},{2,98}... | collective-permute-start | bytes 405512 | tf_op jit(solution)/shard_map/ppermute | solution.py:639
  33.2 0.2 other_sums.1.a_ref
  33.5 3.6 %collective-permute-done.6.c_ref = f32[264,128]{1,0:T(8,128)S(1)} collective-permute-done((f32[264,128]{1,0:T(8,128)S(1)}, f32[264,128]{1,0:T(8,128)S(1)}, u32[]{:S(2)}, u32[]{:S(2)}) %collective-permute-start.6) | collective-permute-done | bytes 135200 | tf_op jit(solution)/shard_map/ppermute | solution.py:639
  37.1 0.3 turn.1
  37.4 21.9 %all_to_all.10.in_ref = f32[64,1,640]{2,1,0:T(1,128)S(1)} all-to-all(f32[64,1,640]{2,1,0:T(1,128)S(1)} %turn.1), channel_id=1, replica_groups=mesh['zhi'=2,'x'=4,'sky'=32] {'zhi','sky'}, dimensions={0} | all-to-all | bytes 327680 | tf_op jit(solution)/shard_map/all_to_all | solution.py:661
  59.4 1.0 %solve.1 = f32[64,8,128]{2,1,0:T(8,128)S(1)} custom-call(f32[64,1,640]{2,1,0:T(1,128)S(1)} %all_to_all.10.in_ref, f32[32,8,128]{2,1,0:T(8,128)S(1)} %copy-done.7, f32[32,8,128]{2,1,0:T(8,128)S(1)} %copy-done.6, bf16[128,256]{1,0:T(8,128)(2,1)S(1)} %copy-done.9, bf16[128,256]{1,0:T(8,128)(2,1)S(1)} %copy-done.8), custom_call_target="tpu_custom_call" | custom-call | tf_op jit(solution)/shard_map/solve/pallas_call | solution.py:542
  60.4 17.1 %all_to_all.11.in_ref = f32[64,8,128]{2,1,0:T(8,128)S(1)} all-to-all(f32[64,8,128]{2,1,0:T(8,128)S(1)} %solve.1), channel_id=1, replica_groups=mesh['zhi'=2,'x'=4,'sky'=32] {'zhi','sky'}, dimensions={0} | all-to-all | bytes 524288 | tf_op jit(solution)/shard_map/all_to_all | solution.py:663
  77.4 1.2 %back.1 = (f32[128,256]{1,0:T(8,128)S(1)}, f32[128,256]{1,0:T(8,128)S(1)}, f32[128,256]{1,0:T(8,128)S(1)}, f32[128,512]{1,0:T(8,128)S(1)}, f32[128,512]{1,0:T(8,128)S(1)}) custom-call(f32[16]{0:T(128)S(1)} %copy-done.11, f32[64,8,128]{2,1,0:T(8,128)S(1)} %all_to_all.11.in_ref, bf16[4,512,256]{2,1,0:T(8,128)(2,1)S(1)} %copy-done.5, ...), custom_call_target="tpu_custom_call" | custom-call | tf_op jit(solution)/shard_map/back/pallas_call | solution.py:588
  78.7 0.3 collective-permute-start.8
  79.0 0.9 %collective-permute-start.9 = (f32[128,256]{1,0:T(8,128)S(1)}, f32[128,256]{1,0:T(8,128)S(1)}, u32[]{:S(2)}, u32[]{:S(2)}) collective-permute-start(f32[128,256]{1,0:T(8,128)S(1)} %get-tuple-element.32), channel_id=1, source_target_pairs={{0,32},{32,64},{64,96},{96,0},{1,33},{33,65},{65,97},{97,1},{2,34}... | collective-permute-start | bytes 393224 | tf_op jit(solution)/shard_map/ppermute | solution.py:639
  79.9 1.8 %collective-permute-start.10 = (f32[128,256]{1,0:T(8,128)S(1)}, f32[128,256]{1,0:T(8,128)S(1)}, u32[]{:S(2)}, u32[]{:S(2)}) collective-permute-start(f32[128,256]{1,0:T(8,128)S(1)} %get-tuple-element.33), channel_id=1, source_target_pairs={{0,96},{32,0},{64,32},{96,64},{1,97},{33,1},{65,33},{97,65},{2,98}... | collective-permute-start | bytes 393224 | tf_op jit(solution)/shard_map/ppermute | solution.py:639
  81.6 0.8 back_rest.1.a_ref
  82.5 2.7 %collective-permute-done.8.b_ref = f32[128,256]{1,0:T(8,128)S(1)} collective-permute-done((f32[128,256]{1,0:T(8,128)S(1)}, f32[128,256]{1,0:T(8,128)S(1)}, u32[]{:S(2)}, u32[]{:S(2)}) %collective-permute-start.8) | collective-permute-done | bytes 131104 | tf_op jit(solution)/shard_map/ppermute | solution.py:639
  85.1 3.2 %collective-permute-done.9.c_ref = f32[128,256]{1,0:T(8,128)S(1)} collective-permute-done((f32[128,256]{1,0:T(8,128)S(1)}, f32[128,256]{1,0:T(8,128)S(1)}, u32[]{:S(2)}, u32[]{:S(2)}) %collective-permute-start.9) | collective-permute-done | bytes 131104 | tf_op jit(solution)/shard_map/ppermute | solution.py:639
  88.4 0.7 final.1
  (31 shorter events, 0.1 us)
Async XLA Ops:
  0.6 11.4 %copy-start.13 = (f32[8]{0:T(128)S(1)}, f32[8]{0:T(128)}, u32[]{:S(2)}) copy-start(f32[8]{0:T(128)} %high_ref.3) | copy-start | bytes 100
  0.6 11.4 %copy-start.12 = (f32[8]{0:T(128)S(1)}, f32[8]{0:T(128)}, u32[]{:S(2)}) copy-start(f32[8]{0:T(128)} %low_ref.3) | copy-start | bytes 100
  0.7 11.4 %copy-start.10 = (s32[1,8,256]{2,1,0:T(8,128)S(1)}, s32[1,8,256]{2,1,0:T(8,128)}, u32[]{:S(2)}) copy-start(s32[1,8,256]{2,1,0:T(8,128)} %refine_ref.1) | copy-start | bytes 24580
  1.6 18.7 %collective-permute-start = (bf16[1,64,2048]{2,1,0:T(8,128)(2,1)S(1)}, bf16[1,64,2048]{2,1,0:T(8,128)(2,1)S(1)}, u32[]{:S(2)}, u32[]{:S(2)}) collective-permute-start(bf16[1,64,2048]{2,1,0:T(8,128)(2,1)S(1)} %constant_dynamic-slice_fusion), channel_id=1, source_target_pairs={{96,128},{128,96},{97,129},{129,97},{98,130},{130,98},{99,131},{13... | collective-permute-start | bytes 786440 | tf_op jit(solution)/shard_map/ppermute | solution.py:645
  2.3 1.6 %copy-start = (bf16[8,64,2048]{2,1,0:T(8,128)(2,1)S(1)}, bf16[8,64,2048]{2,1,0:T(8,128)(2,1)}, u32[]{:S(2)}) copy-start(bf16[8,64,2048]{2,1,0:T(8,128)(2,1)} %d_ref.5) | copy-start | bytes 6291460
  3.9 8.1 %copy-start.1 = (bf16[8,64,2048]{2,1,0:T(8,128)(2,1)S(1)}, bf16[8,64,2048]{2,1,0:T(8,128)(2,1)}, u32[]{:S(2)}) copy-start(bf16[8,64,2048]{2,1,0:T(8,128)(2,1)} %d_ref.5) | copy-start | bytes 6291460
  3.9 16.4 %copy-start.2 = (bf16[8,256,256]{2,1,0:T(8,128)(2,1)S(1)}, bf16[8,256,256]{2,1,0:T(8,128)(2,1)}, u32[]{:S(2)}) copy-start(bf16[8,256,256]{2,1,0:T(8,128)(2,1)} %constant.44.clone.low_table) | copy-start | bytes 3145732
  3.9 16.4 %copy-start.3 = (bf16[8,256,256]{2,1,0:T(8,128)(2,1)S(1)}, bf16[8,256,256]{2,1,0:T(8,128)(2,1)}, u32[]{:S(2)}) copy-start(bf16[8,256,256]{2,1,0:T(8,128)(2,1)} %constant.43.clone.high_table) | copy-start | bytes 3145732
  4.1 16.2 %collective-permute-start.1 = (bf16[1,64,2048]{2,1,0:T(8,128)(2,1)S(1)}, bf16[1,64,2048]{2,1,0:T(8,128)(2,1)S(1)}, u32[]{:S(2)}, u32[]{:S(2)}) collective-permute-start(bf16[1,64,2048]{2,1,0:T(8,128)(2,1)S(1)} %get-tuple-element.18), channel_id=1, source_target_pairs={{32,64},{160,192},{64,32},{192,160},{33,65},{161,193},{65,33},{193... | collective-permute-start | bytes 786440 | tf_op jit(solution)/shard_map/ppermute | solution.py:645
  4.9 15.4 %collective-permute-start.2 = (bf16[1,64,2048]{2,1,0:T(8,128)(2,1)S(1)}, bf16[1,64,2048]{2,1,0:T(8,128)(2,1)S(1)}, u32[]{:S(2)}, u32[]{:S(2)}) collective-permute-start(bf16[1,64,2048]{2,1,0:T(8,128)(2,1)S(1)} %get-tuple-element.19), channel_id=1, source_target_pairs={{0,32},{64,96},{128,160},{192,224},{32,0},{96,64},{160,128},{224,1... | collective-permute-start | bytes 786440 | tf_op jit(solution)/shard_map/ppermute | solution.py:645
  9.6 10.7 %collective-permute-start.3 = (f32[8,2048]{1,0:T(8,128)S(1)}, f32[8,2048]{1,0:T(8,128)S(1)}, u32[]{:S(2)}, u32[]{:S(2)}) collective-permute-start(f32[8,2048]{1,0:T(8,128)S(1)} %get-tuple-element.20), channel_id=1, source_target_pairs={{0,1},{2,3},{4,5},{6,7},{8,9},{10,11},{12,13},{14,15},{16,17},{18,... | collective-permute-start | bytes 196616 | tf_op jit(solution)/shard_map/ppermute | solution.py:645
  10.9 9.5 %collective-permute-start.4 = (f32[8,2048]{1,0:T(8,128)S(1)}, f32[8,2048]{1,0:T(8,128)S(1)}, u32[]{:S(2)}, u32[]{:S(2)}) collective-permute-start(f32[8,2048]{1,0:T(8,128)S(1)} %get-tuple-element.21), channel_id=1, source_target_pairs={{1,2},{3,4},{5,6},{7,8},{9,10},{11,12},{13,14},{15,16},{17,18},{19... | collective-permute-start | bytes 196616 | tf_op jit(solution)/shard_map/ppermute | solution.py:645
  22.5 36.9 %copy-start.6 = (f32[32,8,128]{2,1,0:T(8,128)S(1)}, f32[32,8,128]{2,1,0:T(8,128)}, u32[]{:S(2)}) copy-start(f32[32,8,128]{2,1,0:T(8,128)} %constant.46.clone.sin_ref) | copy-start | bytes 393220
  22.5 36.8 %copy-start.7 = (f32[32,8,128]{2,1,0:T(8,128)S(1)}, f32[32,8,128]{2,1,0:T(8,128)}, u32[]{:S(2)}) copy-start(f32[32,8,128]{2,1,0:T(8,128)} %constant.45.clone.cos_ref) | copy-start | bytes 393220
  22.5 36.8 %copy-start.8 = (bf16[128,256]{1,0:T(8,128)(2,1)S(1)}, bf16[128,256]{1,0:T(8,128)(2,1)}, u32[]{:S(2)}) copy-start(bf16[128,256]{1,0:T(8,128)(2,1)} %constant.48.clone.low_table) | copy-start | bytes 196612
  22.5 36.8 %copy-start.9 = (bf16[128,256]{1,0:T(8,128)(2,1)S(1)}, bf16[128,256]{1,0:T(8,128)(2,1)}, u32[]{:S(2)}) copy-start(bf16[128,256]{1,0:T(8,128)(2,1)} %constant.47.clone.high_table) | copy-start | bytes 196612
  22.5 10.9 %collective-permute-start.5 = (f32[264,128]{1,0:T(8,128)S(1)}, f32[264,128]{1,0:T(8,128)S(1)}, u32[]{:S(2)}, u32[]{:S(2)}) collective-permute-start(f32[264,128]{1,0:T(8,128)S(1)} %get-tuple-element.26), channel_id=1, source_target_pairs={{0,64},{32,96},{64,0},{96,32},{1,65},{33,97},{65,1},{97,33},{2,66}... | collective-permute-start | bytes 405512 | tf_op jit(solution)/shard_map/ppermute | solution.py:639
  30.6 6.5 %collective-permute-start.6 = (f32[264,128]{1,0:T(8,128)S(1)}, f32[264,128]{1,0:T(8,128)S(1)}, u32[]{:S(2)}, u32[]{:S(2)}) collective-permute-start(f32[264,128]{1,0:T(8,128)S(1)} %get-tuple-element.27), channel_id=1, source_target_pairs={{0,32},{32,64},{64,96},{96,0},{1,33},{33,65},{65,97},{97,1},{2,34}... | collective-permute-start | bytes 405512 | tf_op jit(solution)/shard_map/ppermute | solution.py:639
  30.6 6.5 %collective-permute-start.7 = (f32[264,128]{1,0:T(8,128)S(1)}, f32[264,128]{1,0:T(8,128)S(1)}, u32[]{:S(2)}, u32[]{:S(2)}) collective-permute-start(f32[264,128]{1,0:T(8,128)S(1)} %get-tuple-element.28), channel_id=1, source_target_pairs={{0,96},{32,0},{64,32},{96,64},{1,97},{33,1},{65,33},{97,65},{2,98}... | collective-permute-start | bytes 405512 | tf_op jit(solution)/shard_map/ppermute | solution.py:639
  33.2 44.2 %copy-start.4 = (bf16[4,512,256]{2,1,0:T(8,128)(2,1)S(1)}, bf16[4,512,256]{2,1,0:T(8,128)(2,1)}, u32[]{:S(2)}) copy-start(bf16[4,512,256]{2,1,0:T(8,128)(2,1)} %constant.51.clone.low_table) | copy-start | bytes 3145732
  33.2 44.2 %copy-start.5 = (bf16[4,512,256]{2,1,0:T(8,128)(2,1)S(1)}, bf16[4,512,256]{2,1,0:T(8,128)(2,1)}, u32[]{:S(2)}) copy-start(bf16[4,512,256]{2,1,0:T(8,128)(2,1)} %constant.50.clone.high_table) | copy-start | bytes 3145732
  33.2 44.2 %copy-start.11 = (f32[16]{0:T(128)S(1)}, f32[16]{0:T(128)}, u32[]{:S(2)}) copy-start(f32[16]{0:T(128)} %constant.49.clone.eighth_ref) | copy-start | bytes 196
  78.7 6.5 %collective-permute-start.8 = (f32[128,256]{1,0:T(8,128)S(1)}, f32[128,256]{1,0:T(8,128)S(1)}, u32[]{:S(2)}, u32[]{:S(2)}) collective-permute-start(f32[128,256]{1,0:T(8,128)S(1)} %get-tuple-element.31), channel_id=1, source_target_pairs={{0,64},{32,96},{64,0},{96,32},{1,65},{33,97},{65,1},{97,33},{2,66}... | collective-permute-start | bytes 393224 | tf_op jit(solution)/shard_map/ppermute | solution.py:639
  79.0 9.4 %collective-permute-start.9 = (f32[128,256]{1,0:T(8,128)S(1)}, f32[128,256]{1,0:T(8,128)S(1)}, u32[]{:S(2)}, u32[]{:S(2)}) collective-permute-start(f32[128,256]{1,0:T(8,128)S(1)} %get-tuple-element.32), channel_id=1, source_target_pairs={{0,32},{32,64},{64,96},{96,0},{1,33},{33,65},{65,97},{97,1},{2,34}... | collective-permute-start | bytes 393224 | tf_op jit(solution)/shard_map/ppermute | solution.py:639
  79.9 8.5 %collective-permute-start.10 = (f32[128,256]{1,0:T(8,128)S(1)}, f32[128,256]{1,0:T(8,128)S(1)}, u32[]{:S(2)}, u32[]{:S(2)}) collective-permute-start(f32[128,256]{1,0:T(8,128)S(1)} %get-tuple-element.33), channel_id=1, source_target_pairs={{0,96},{32,0},{64,32},{96,64},{1,97},{33,1},{65,33},{97,65},{2,98}... | collective-permute-start | bytes 393224 | tf_op jit(solution)/shard_map/ppermute | solution.py:639

commit v13 on v11

--- a/solution.py
+++ b/solution.py
@@ -154,7 +154,7 @@
     return 0.75 * field + 0.125 * (pltpu.roll(field, 1, 1) + pltpu.roll(field, N - 1, 1))
 
 
-CHUNK = 512
+CHUNK = 1024
 
 
 def inner_kernel(

time: 89.2 us -> 89.4 us (level)
  blocking collectives: 39 us -> 40.3 us
  Pallas kernels: 14.8 us -> 13.6 us
    pallas_call x1, Pallas kernels: 8.23 us -> 7.05 us  [inner_sums(): pl.pallas_call(inner_kernel, out_shape=(jax.ShapeDtypeStruct((ROWS + 8, N...]
    all_to_all x1, blocking collectives: 21.9 us -> 23.1 us  [body(): pieces = lax.all_to_all(turn(summed), ('zhi', 'sky'), 0, 0, tiled=True)]
  transfers between devices with their start and end apart: 11 -> 11, of which waited for: 3 -> 3; matrix products, arithmetic and copies ran while one was open for 0% -> 0% of each run, Pallas kernels for 11% -> 9%
where the time goes in v13:
time: 89.4 us; the launch traced here: 89.2 us
  blocking collectives  40.3 us (45%)
  starting transfers between devices  22.3 us (25%)
  Pallas kernels  13.6 us (15%)
  waiting for transfers between devices  9.47 us (11%)
  local copies, waits for them, and re-layouts  2.62 us (3%)
    all_to_all x1, blocking collectives, body(): pieces = lax.all_to_all(turn(summed), ('zhi', 'sky'), 0, 0, tiled=True)  23.1 us
    all_to_all x1, blocking collectives, body(): pieces = lax.all_to_all(pieces, ('zhi', 'sky'), 0, 0, tiled=True)  17.3 us
    ppermute x6, starting transfers between devices, deliver(): lax.ppermute(pieces[a], 'x', [(i, (i + a) % 4) for i in range(4)])  13.7 us
    ppermute x6, waiting for transfers between devices, deliver(): lax.ppermute(pieces[a], 'x', [(i, (i + a) % 4) for i in range(4)])  9.46 us
    ppermute x5, starting transfers between devices, swap(): return lax.ppermute(array, axes, pairs + [(b, a) for a, b in pairs])  8.61 us
    pallas_call x1, Pallas kernels, inner_sums(): pl.pallas_call(inner_kernel, out_shape=(jax.ShapeDtypeStruct((ROWS + 8, N...  7.05 us
    pallas_call x1, Pallas kernels, outer_sums(): pl.pallas_call(outer_kernel, out_shape=(piece, piece, piece, jax.ShapeDty...  2.1 us
  transfers between devices with their start and end apart: 11, of which 3 were waited for; matrix products, arithmetic and copies ran while one was open for 0% of the time, Pallas kernels for 9%

profile of v13, /device:TPU:1, one launch (start us, length us, event | category | flops | bytes accessed | tf_op | source)
XLA Modules:
  0.0 89.2 jit_solution(8550689820579745577)
XLA Ops:
  0.7 1.0 %constant_dynamic-slice_fusion = bf16[1,64,2048]{2,1,0:T(8,128)(2,1)S(1)} fusion(bf16[8,64,2048]{2,1,0:T(8,128)(2,1)} %d_ref.5, s32[]{:T(128)S(6)} %select_n.13), kind=kLoop, calls=%fused_computation | loop fusion | bytes 524292 | tf_op jit(solution)/shard_map/dynamic_slice | solution.py:636
  1.6 0.7 collective-permute-start
  2.3 0.0 copy-start
  2.3 1.6 %copy-done = bf16[8,64,2048]{2,1,0:T(8,128)(2,1)S(1)} copy-done((bf16[8,64,2048]{2,1,0:T(8,128)(2,1)S(1)}, bf16[8,64,2048]{2,1,0:T(8,128)(2,1)}, u32[]{:S(2)}) %copy-start) | copy-done | bytes 2097176
  3.9 0.2 edge_rows.1
  4.1 0.8 collective-permute-start.1
  4.9 4.7 %collective-permute-start.2 = (bf16[1,64,2048]{2,1,0:T(8,128)(2,1)S(1)}, bf16[1,64,2048]{2,1,0:T(8,128)(2,1)S(1)}, u32[]{:S(2)}, u32[]{:S(2)}) collective-permute-start(bf16[1,64,2048]{2,1,0:T(8,128)(2,1)S(1)} %get-tuple-element.19), channel_id=1, source_target_pairs={{0,32},{64,96},{128,160},{192,224},{32,0},{96,64},{160,128},{224,1... | collective-permute-start | bytes 786440 | tf_op jit(solution)/shard_map/ppermute | solution.py:633
  9.6 1.2 %collective-permute-start.3 = (f32[8,2048]{1,0:T(8,128)S(1)}, f32[8,2048]{1,0:T(8,128)S(1)}, u32[]{:S(2)}, u32[]{:S(2)}) collective-permute-start(f32[8,2048]{1,0:T(8,128)S(1)} %get-tuple-element.20), channel_id=1, source_target_pairs={{0,1},{2,3},{4,5},{6,7},{8,9},{10,11},{12,13},{14,15},{16,17},{18,... | collective-permute-start | bytes 196616 | tf_op jit(solution)/shard_map/ppermute | solution.py:633
  10.9 1.2 %collective-permute-start.4 = (f32[8,2048]{1,0:T(8,128)S(1)}, f32[8,2048]{1,0:T(8,128)S(1)}, u32[]{:S(2)}, u32[]{:S(2)}) collective-permute-start(f32[8,2048]{1,0:T(8,128)S(1)} %get-tuple-element.21), channel_id=1, source_target_pairs={{1,2},{3,4},{5,6},{7,8},{9,10},{11,12},{13,14},{15,16},{17,18},{19... | collective-permute-start | bytes 196616 | tf_op jit(solution)/shard_map/ppermute | solution.py:633
  12.1 7.0 %inner_sums.1 = (f32[72,2048]{1,0:T(8,128)S(1)}, f32[8,2048]{1,0:T(8,128)S(1)}, f32[4,8,2048]{2,1,0:T(8,128)S(1)}) custom-call(f32[8]{0:T(128)S(1)} %copy-done.12, f32[8]{0:T(128)S(1)} %copy-done.13, bf16[8,64,2048]{2,1,0:T(8,128)(2,1)S(1)} %copy-done.1, s32[1,8,256]{2,1,0:T(8,128)S(1)} %copy-done.10), custom_call_target="tpu_custom_call" | custom-call | flops 40000000 | bytes 25165824 | tf_op jit(solution)/shard_map/inner_sums/pallas_call | solution.py:243
  19.1 0.0 collective-permute-done.3.row_ref
  19.2 2.1 %outer_sums.1 = (f32[264,128]{1,0:T(8,128)S(1)}, f32[264,128]{1,0:T(8,128)S(1)}, f32[264,128]{1,0:T(8,128)S(1)}, bf16[8,160,256]{2,1,0:T(8,128)(2,1)S(1)}) custom-call(f32[8]{0:T(128)S(1)} %copy-done.12, f32[8]{0:T(128)S(1)} %copy-done.13, bf16[8,64,2048]{2,1,0:T(8,128)(2,1)S(1)} %copy-done.1, bf16[1,64,2048]{2,1,0:T(8,128)(2,1)S(1)} %collective-permute-done.cross_ref, ...), custom_call_target="tpu_custom_call" | custom-call | tf_op jit(solution)/shard_map/outer_sums/pallas_call | solution.py:373
  21.3 0.0 copy-start.6
  21.3 0.0 copy-start.7
  21.3 0.0 copy-start.8
  21.4 0.0 copy-start.9
  21.4 8.0 %collective-permute-start.5 = (f32[264,128]{1,0:T(8,128)S(1)}, f32[264,128]{1,0:T(8,128)S(1)}, u32[]{:S(2)}, u32[]{:S(2)}) collective-permute-start(f32[264,128]{1,0:T(8,128)S(1)} %get-tuple-element.26), channel_id=1, source_target_pairs={{0,64},{32,96},{64,0},{96,32},{1,65},{33,97},{65,1},{97,33},{2,66}... | collective-permute-start | bytes 405512 | tf_op jit(solution)/shard_map/ppermute | solution.py:627
  29.4 2.7 %collective-permute-start.7 = (f32[264,128]{1,0:T(8,128)S(1)}, f32[264,128]{1,0:T(8,128)S(1)}, u32[]{:S(2)}, u32[]{:S(2)}) collective-permute-start(f32[264,128]{1,0:T(8,128)S(1)} %get-tuple-element.28), channel_id=1, source_target_pairs={{0,96},{32,0},{64,32},{96,64},{1,97},{33,1},{65,33},{97,65},{2,98}... | collective-permute-start | bytes 405512 | tf_op jit(solution)/shard_map/ppermute | solution.py:627
  32.1 0.2 other_sums.1.a_ref
  32.3 3.6 %collective-permute-done.6.c_ref = f32[264,128]{1,0:T(8,128)S(1)} collective-permute-done((f32[264,128]{1,0:T(8,128)S(1)}, f32[264,128]{1,0:T(8,128)S(1)}, u32[]{:S(2)}, u32[]{:S(2)}) %collective-permute-start.6) | collective-permute-done | bytes 135200 | tf_op jit(solution)/shard_map/ppermute | solution.py:627
  35.9 0.3 turn.1
  36.2 23.1 %all_to_all.10.in_ref = f32[64,1,640]{2,1,0:T(1,128)S(1)} all-to-all(f32[64,1,640]{2,1,0:T(1,128)S(1)} %turn.1), channel_id=1, replica_groups=mesh['zhi'=2,'x'=4,'sky'=32] {'zhi','sky'}, dimensions={0} | all-to-all | bytes 327680 | tf_op jit(solution)/shard_map/all_to_all | solution.py:649
  59.4 1.0 %solve.1 = f32[64,8,128]{2,1,0:T(8,128)S(1)} custom-call(f32[64,1,640]{2,1,0:T(1,128)S(1)} %all_to_all.10.in_ref, f32[32,8,128]{2,1,0:T(8,128)S(1)} %copy-done.7, f32[32,8,128]{2,1,0:T(8,128)S(1)} %copy-done.6, bf16[128,256]{1,0:T(8,128)(2,1)S(1)} %copy-done.9, bf16[128,256]{1,0:T(8,128)(2,1)S(1)} %copy-done.8), custom_call_target="tpu_custom_call" | custom-call | tf_op jit(solution)/shard_map/solve/pallas_call | solution.py:542
  60.4 17.3 %all_to_all.11.in_ref = f32[64,8,128]{2,1,0:T(8,128)S(1)} all-to-all(f32[64,8,128]{2,1,0:T(8,128)S(1)} %solve.1), channel_id=1, replica_groups=mesh['zhi'=2,'x'=4,'sky'=32] {'zhi','sky'}, dimensions={0} | all-to-all | bytes 524288 | tf_op jit(solution)/shard_map/all_to_all | solution.py:651
  77.6 1.2 %back.1 = (f32[128,256]{1,0:T(8,128)S(1)}, f32[128,256]{1,0:T(8,128)S(1)}, f32[128,256]{1,0:T(8,128)S(1)}, f32[128,512]{1,0:T(8,128)S(1)}, f32[128,512]{1,0:T(8,128)S(1)}) custom-call(f32[16]{0:T(128)S(1)} %copy-done.11, f32[64,8,128]{2,1,0:T(8,128)S(1)} %all_to_all.11.in_ref, bf16[4,512,256]{2,1,0:T(8,128)(2,1)S(1)} %copy-done.5, ...), custom_call_target="tpu_custom_call" | custom-call | tf_op jit(solution)/shard_map/back/pallas_call | solution.py:588
  78.8 0.3 collective-permute-start.8
  79.1 0.9 collective-permute-start.9
  80.0 1.8 %collective-permute-start.10 = (f32[128,256]{1,0:T(8,128)S(1)}, f32[128,256]{1,0:T(8,128)S(1)}, u32[]{:S(2)}, u32[]{:S(2)}) collective-permute-start(f32[128,256]{1,0:T(8,128)S(1)} %get-tuple-element.33), channel_id=1, source_target_pairs={{0,96},{32,0},{64,32},{96,64},{1,97},{33,1},{65,33},{97,65},{2,98}... | collective-permute-start | bytes 393224 | tf_op jit(solution)/shard_map/ppermute | solution.py:627
  81.8 0.8 back_rest.1.a_ref
  82.7 2.7 %collective-permute-done.8.b_ref = f32[128,256]{1,0:T(8,128)S(1)} collective-permute-done((f32[128,256]{1,0:T(8,128)S(1)}, f32[128,256]{1,0:T(8,128)S(1)}, u32[]{:S(2)}, u32[]{:S(2)}) %collective-permute-start.8) | collective-permute-done | bytes 131104 | tf_op jit(solution)/shard_map/ppermute | solution.py:627
  85.3 3.2 %collective-permute-done.9.c_ref = f32[128,256]{1,0:T(8,128)S(1)} collective-permute-done((f32[128,256]{1,0:T(8,128)S(1)}, f32[128,256]{1,0:T(8,128)S(1)}, u32[]{:S(2)}, u32[]{:S(2)}) %collective-permute-start.9) | collective-permute-done | bytes 131104 | tf_op jit(solution)/shard_map/ppermute | solution.py:627
  88.5 0.7 final.1
  (30 shorter events, 0.1 us)
Async XLA Ops:
  0.6 11.4 %copy-start.13 = (f32[8]{0:T(128)S(1)}, f32[8]{0:T(128)}, u32[]{:S(2)}) copy-start(f32[8]{0:T(128)} %high_ref.3) | copy-start | bytes 100
  0.6 11.4 %copy-start.12 = (f32[8]{0:T(128)S(1)}, f32[8]{0:T(128)}, u32[]{:S(2)}) copy-start(f32[8]{0:T(128)} %low_ref.3) | copy-start | bytes 100
  0.7 11.4 %copy-start.10 = (s32[1,8,256]{2,1,0:T(8,128)S(1)}, s32[1,8,256]{2,1,0:T(8,128)}, u32[]{:S(2)}) copy-start(s32[1,8,256]{2,1,0:T(8,128)} %refine_ref.1) | copy-start | bytes 24580
  1.6 17.5 %collective-permute-start = (bf16[1,64,2048]{2,1,0:T(8,128)(2,1)S(1)}, bf16[1,64,2048]{2,1,0:T(8,128)(2,1)S(1)}, u32[]{:S(2)}, u32[]{:S(2)}) collective-permute-start(bf16[1,64,2048]{2,1,0:T(8,128)(2,1)S(1)} %constant_dynamic-slice_fusion), channel_id=1, source_target_pairs={{96,128},{128,96},{97,129},{129,97},{98,130},{130,98},{99,131},{13... | collective-permute-start | bytes 786440 | tf_op jit(solution)/shard_map/ppermute | solution.py:633
  2.3 1.6 %copy-start = (bf16[8,64,2048]{2,1,0:T(8,128)(2,1)S(1)}, bf16[8,64,2048]{2,1,0:T(8,128)(2,1)}, u32[]{:S(2)}) copy-start(bf16[8,64,2048]{2,1,0:T(8,128)(2,1)} %d_ref.5) | copy-start | bytes 6291460
  3.9 8.1 %copy-start.1 = (bf16[8,64,2048]{2,1,0:T(8,128)(2,1)S(1)}, bf16[8,64,2048]{2,1,0:T(8,128)(2,1)}, u32[]{:S(2)}) copy-start(bf16[8,64,2048]{2,1,0:T(8,128)(2,1)} %d_ref.5) | copy-start | bytes 6291460
  3.9 15.3 %copy-start.2 = (bf16[8,256,256]{2,1,0:T(8,128)(2,1)S(1)}, bf16[8,256,256]{2,1,0:T(8,128)(2,1)}, u32[]{:S(2)}) copy-start(bf16[8,256,256]{2,1,0:T(8,128)(2,1)} %constant.44.clone.low_table) | copy-start | bytes 3145732
  3.9 15.3 %copy-start.3 = (bf16[8,256,256]{2,1,0:T(8,128)(2,1)S(1)}, bf16[8,256,256]{2,1,0:T(8,128)(2,1)}, u32[]{:S(2)}) copy-start(bf16[8,256,256]{2,1,0:T(8,128)(2,1)} %constant.43.clone.high_table) | copy-start | bytes 3145732
  4.1 15.0 %collective-permute-start.1 = (bf16[1,64,2048]{2,1,0:T(8,128)(2,1)S(1)}, bf16[1,64,2048]{2,1,0:T(8,128)(2,1)S(1)}, u32[]{:S(2)}, u32[]{:S(2)}) collective-permute-start(bf16[1,64,2048]{2,1,0:T(8,128)(2,1)S(1)} %get-tuple-element.18), channel_id=1, source_target_pairs={{32,64},{160,192},{64,32},{192,160},{33,65},{161,193},{65,33},{193... | collective-permute-start | bytes 786440 | tf_op jit(solution)/shard_map/ppermute | solution.py:633
  4.9 14.2 %collective-permute-start.2 = (bf16[1,64,2048]{2,1,0:T(8,128)(2,1)S(1)}, bf16[1,64,2048]{2,1,0:T(8,128)(2,1)S(1)}, u32[]{:S(2)}, u32[]{:S(2)}) collective-permute-start(bf16[1,64,2048]{2,1,0:T(8,128)(2,1)S(1)} %get-tuple-element.19), channel_id=1, source_target_pairs={{0,32},{64,96},{128,160},{192,224},{32,0},{96,64},{160,128},{224,1... | collective-permute-start | bytes 786440 | tf_op jit(solution)/shard_map/ppermute | solution.py:633
  9.6 9.5 %collective-permute-start.3 = (f32[8,2048]{1,0:T(8,128)S(1)}, f32[8,2048]{1,0:T(8,128)S(1)}, u32[]{:S(2)}, u32[]{:S(2)}) collective-permute-start(f32[8,2048]{1,0:T(8,128)S(1)} %get-tuple-element.20), channel_id=1, source_target_pairs={{0,1},{2,3},{4,5},{6,7},{8,9},{10,11},{12,13},{14,15},{16,17},{18,... | collective-permute-start | bytes 196616 | tf_op jit(solution)/shard_map/ppermute | solution.py:633
  10.9 8.3 %collective-permute-start.4 = (f32[8,2048]{1,0:T(8,128)S(1)}, f32[8,2048]{1,0:T(8,128)S(1)}, u32[]{:S(2)}, u32[]{:S(2)}) collective-permute-start(f32[8,2048]{1,0:T(8,128)S(1)} %get-tuple-element.21), channel_id=1, source_target_pairs={{1,2},{3,4},{5,6},{7,8},{9,10},{11,12},{13,14},{15,16},{17,18},{19... | collective-permute-start | bytes 196616 | tf_op jit(solution)/shard_map/ppermute | solution.py:633
  21.3 38.0 %copy-start.6 = (f32[32,8,128]{2,1,0:T(8,128)S(1)}, f32[32,8,128]{2,1,0:T(8,128)}, u32[]{:S(2)}) copy-start(f32[32,8,128]{2,1,0:T(8,128)} %constant.46.clone.sin_ref) | copy-start | bytes 393220
  21.3 38.0 %copy-start.7 = (f32[32,8,128]{2,1,0:T(8,128)S(1)}, f32[32,8,128]{2,1,0:T(8,128)}, u32[]{:S(2)}) copy-start(f32[32,8,128]{2,1,0:T(8,128)} %constant.45.clone.cos_ref) | copy-start | bytes 393220
  21.3 38.0 %copy-start.8 = (bf16[128,256]{1,0:T(8,128)(2,1)S(1)}, bf16[128,256]{1,0:T(8,128)(2,1)}, u32[]{:S(2)}) copy-start(bf16[128,256]{1,0:T(8,128)(2,1)} %constant.48.clone.low_table) | copy-start | bytes 196612
  21.4 38.0 %copy-start.9 = (bf16[128,256]{1,0:T(8,128)(2,1)S(1)}, bf16[128,256]{1,0:T(8,128)(2,1)}, u32[]{:S(2)}) copy-start(bf16[128,256]{1,0:T(8,128)(2,1)} %constant.47.clone.high_table) | copy-start | bytes 196612
  21.4 10.9 %collective-permute-start.5 = (f32[264,128]{1,0:T(8,128)S(1)}, f32[264,128]{1,0:T(8,128)S(1)}, u32[]{:S(2)}, u32[]{:S(2)}) collective-permute-start(f32[264,128]{1,0:T(8,128)S(1)} %get-tuple-element.26), channel_id=1, source_target_pairs={{0,64},{32,96},{64,0},{96,32},{1,65},{33,97},{65,1},{97,33},{2,66}... | collective-permute-start | bytes 405512 | tf_op jit(solution)/shard_map/ppermute | solution.py:627
  29.4 6.5 %collective-permute-start.6 = (f32[264,128]{1,0:T(8,128)S(1)}, f32[264,128]{1,0:T(8,128)S(1)}, u32[]{:S(2)}, u32[]{:S(2)}) collective-permute-start(f32[264,128]{1,0:T(8,128)S(1)} %get-tuple-element.27), channel_id=1, source_target_pairs={{0,32},{32,64},{64,96},{96,0},{1,33},{33,65},{65,97},{97,1},{2,34}... | collective-permute-start | bytes 405512 | tf_op jit(solution)/shard_map/ppermute | solution.py:627
  29.4 6.5 %collective-permute-start.7 = (f32[264,128]{1,0:T(8,128)S(1)}, f32[264,128]{1,0:T(8,128)S(1)}, u32[]{:S(2)}, u32[]{:S(2)}) collective-permute-start(f32[264,128]{1,0:T(8,128)S(1)} %get-tuple-element.28), channel_id=1, source_target_pairs={{0,96},{32,0},{64,32},{96,64},{1,97},{33,1},{65,33},{97,65},{2,98}... | collective-permute-start | bytes 405512 | tf_op jit(solution)/shard_map/ppermute | solution.py:627
  32.0 45.6 %copy-start.4 = (bf16[4,512,256]{2,1,0:T(8,128)(2,1)S(1)}, bf16[4,512,256]{2,1,0:T(8,128)(2,1)}, u32[]{:S(2)}) copy-start(bf16[4,512,256]{2,1,0:T(8,128)(2,1)} %constant.51.clone.low_table) | copy-start | bytes 3145732
  32.0 45.6 %copy-start.5 = (bf16[4,512,256]{2,1,0:T(8,128)(2,1)S(1)}, bf16[4,512,256]{2,1,0:T(8,128)(2,1)}, u32[]{:S(2)}) copy-start(bf16[4,512,256]{2,1,0:T(8,128)(2,1)} %constant.50.clone.high_table) | copy-start | bytes 3145732
  32.1 45.6 %copy-start.11 = (f32[16]{0:T(128)S(1)}, f32[16]{0:T(128)}, u32[]{:S(2)}) copy-start(f32[16]{0:T(128)} %constant.49.clone.eighth_ref) | copy-start | bytes 196
  78.8 6.5 %collective-permute-start.8 = (f32[128,256]{1,0:T(8,128)S(1)}, f32[128,256]{1,0:T(8,128)S(1)}, u32[]{:S(2)}, u32[]{:S(2)}) collective-permute-start(f32[128,256]{1,0:T(8,128)S(1)} %get-tuple-element.31), channel_id=1, source_target_pairs={{0,64},{32,96},{64,0},{96,32},{1,65},{33,97},{65,1},{97,33},{2,66}... | collective-permute-start | bytes 393224 | tf_op jit(solution)/shard_map/ppermute | solution.py:627
  79.1 9.4 %collective-permute-start.9 = (f32[128,256]{1,0:T(8,128)S(1)}, f32[128,256]{1,0:T(8,128)S(1)}, u32[]{:S(2)}, u32[]{:S(2)}) collective-permute-start(f32[128,256]{1,0:T(8,128)S(1)} %get-tuple-element.32), channel_id=1, source_target_pairs={{0,32},{32,64},{64,96},{96,0},{1,33},{33,65},{65,97},{97,1},{2,34}... | collective-permute-start | bytes 393224 | tf_op jit(solution)/shard_map/ppermute | solution.py:627
  80.0 8.5 %collective-permute-start.10 = (f32[128,256]{1,0:T(8,128)S(1)}, f32[128,256]{1,0:T(8,128)S(1)}, u32[]{:S(2)}, u32[]{:S(2)}) collective-permute-start(f32[128,256]{1,0:T(8,128)S(1)} %get-tuple-element.33), channel_id=1, source_target_pairs={{0,96},{32,0},{64,32},{96,64},{1,97},{33,1},{65,33},{97,65},{2,98}... | collective-permute-start | bytes 393224 | tf_op jit(solution)/shard_map/ppermute | solution.py:627
